TPU v7x, 32 devices: a whole 2x2x4 slice. The times are simulated.
32 devices in a mesh: mod: 2 (over x), loop: 4 (over z), line: 4 (over y, core).
Axes of the slice: x: 2, y: 2, z: 4, core: 2. Of those that a mesh axis runs over, the one named last changes fastest.
Arguments:
- act: bfloat16 [2, 12288, 512], P('mod', ('loop', 'line'))
- dy: bfloat16 [2, 12288, 1280], P('mod', ('loop', 'line')), may hold values from -6 to 6
- w_out: bfloat16 [2, 512, 1280], P('mod'), may hold values from -0.15625 to 0.15625
- counts: int32 [2, 4, 4], P('mod', 'loop', 'line'), may hold values from 192 to 768, as said below
Outputs:
- grad_clipped: float32 [2, 512, 1280], P('mod', 'loop')
- hidden_grad: bfloat16 [2, 12288, 512], P('mod', ('loop', 'line'))
Inputs may be any that keep to these rules, and one draw needn't show every extreme that they name: `counts`: in each tower some device has all 768 slots live.
All inputs are finite; a program needn't handle non-finite values.
Results may differ from a plain program's by a relative error of at most 0.001.
Values sent between devices are 32-bit elements; how exact they have to be, the bound alone decides.
No kernel may reach another device: no remote copies, remote signals or barrier semaphores. Data moves between devices by JAX's collectives and lax.ppermute only.
A program may use at most 64 MiB of HBM per device.

v0:
```python
import jax
import jax.numpy as jnp
from jax import lax
from jax.sharding import PartitionSpec as P


def on_device(act, dy, w_out, counts):
    tokens = act[0]
    upstream = dy[0]
    weight = w_out[0]
    rows = tokens.shape[0]
    hidden = tokens.shape[1]
    block = weight.shape[1]
    live = lax.broadcasted_iota(jnp.int32, (rows, 1), 0) < counts[0, 0]
    masked = jnp.where(live, tokens, jnp.zeros_like(tokens))
    entries = lax.axis_size("mod") * hidden * block
    share = lax.psum_scatter(
        lax.dot_general(
            masked, upstream, (((0,), (0,)), ((), ())), preferred_element_type=jnp.float32
        ),
        "loop",
        scatter_dimension=0,
        tiled=True,
    )
    share = lax.psum(share, "line")
    total = lax.psum(jnp.sum(share * share), ("mod", "loop"))
    factor = 1.0 / jnp.sqrt(total / entries + 1e-06)
    clipped = share * factor
    back = lax.dot_general(
        upstream, weight, (((1,), (1,)), ((), ())), preferred_element_type=jnp.float32
    )
    hidden_grad = jnp.where(live, back, jnp.zeros_like(back)).astype(jnp.bfloat16)
    return (clipped[None], hidden_grad[None])


def solution(mesh):
    in_specs = (
        P("mod", ("loop", "line"), None),
        P("mod", ("loop", "line"), None),
        P("mod", None, None),
        P("mod", "loop", "line"),
    )
    out_specs = (P("mod", "loop", None), P("mod", ("loop", "line"), None))
    return jax.shard_map(
        on_device, mesh=mesh, in_specs=in_specs, out_specs=out_specs, check_vma=False
    )
```

profile of v0, /device:TPU:0, one launch (start us, length us, event | category | flops | bytes accessed | tf_op | source)
XLA Modules:
  0.0 139.3 jit_solution(6424267391732542886)
XLA Ops:
  7.2 0.0 copy-start
  7.2 0.0 reduce-scatter.2.cloned.1.call-start
  8.0 0.7 copy-done
  8.7 3.9 %fusion.2 = f32[512,1280]{1,0:T(8,128)} fusion(bf16[1,768,1280]{2,1,0:T(8,128)(2,1)S(1)} %copy-done, bf16[1,768,512]{2,1,0:T(8,128)(2,1)} %param.4, pred[768]{0:T(1024)(128)(4,1)S(1)} %iota_compare_fusion), kind=kOutput, calls=%fused_computation.2 | convolution fusion | flops 1007026176 | bytes 5374720 | tf_op jit(solution)/shard_map/dot_general | solution.py:18
  12.7 0.0 reduce-scatter.2.cloned.1.call-update
  12.7 0.0 all-reduce.2.cloned.1.call-start
  12.8 54.9 %reduce-scatter.2.cloned.1.call-done = f32[128,1280]{1,0:T(8,128)} async-done(((f32[512,1280]{1,0:T(8,128)}), f32[128,1280]{1,0:T(8,128)}) %reduce-scatter.2.cloned.1.call-update) | async-done | bytes 655376 | tf_op jit(solution)/shard_map/reduce_scatter | solution.py:17
  67.7 0.0 all-reduce.2.cloned.1.call-update
  67.7 35.8 %all-reduce.2.cloned.1.call-done = f32[128,1280]{1,0:T(8,128)} async-done(((f32[128,1280]{1,0:T(8,128)}), f32[128,1280]{1,0:T(8,128)}) %all-reduce.2.cloned.1.call-update) | async-done | bytes 655376 | tf_op jit(solution)/shard_map/psum | solution.py:25
  103.5 1.9 %multiply_reduce_fusion = f32[]{:T(128)} fusion(f32[128,1280]{1,0:T(8,128)} %all-reduce.2.cloned.1.call-done), kind=kLoop, calls=%fused_computation.11 | loop fusion | flops 327679 | bytes 655364 | tf_op jit(solution)/shard_map/reduce_sum | solution.py:26
  105.4 0.0 copy-start.1
  105.4 3.5 %fusion.7 = bf16[1,768,512]{2,1,0:T(8,128)(2,1)} fusion(bf16[1,512,1280]{2,1,0:T(8,128)(2,1)} %param.6, bf16[1,768,1280]{2,1,0:T(8,128)(2,1)S(1)} %copy-done, pred[768]{0:T(1024)(128)(4,1)S(1)} %iota_compare_fusion), kind=kOutput, calls=%fused_computation.6 | convolution fusion | flops 1007419392 | bytes 4064000 | tf_op jit(solution)/shard_map/dot_general | solution.py:29
  108.9 22.1 %psum.15 = f32[]{:T(128)} all-reduce(f32[]{:T(128)} %multiply_reduce_fusion), channel_id=1, replica_groups=mesh['mod'=2,'loop'=4,'line'=4] {'mod','loop'}, use_global_device_ids=true, to_apply=%region_3.4 | all-reduce | flops 1 | bytes 8 | tf_op jit(solution)/shard_map/psum | solution.py:26
  131.6 0.0 copy-done.1
  131.6 0.9 multiply_bitcast_fusion
  (1 shorter events, 0.0 us)
Async XLA Ops:
  7.2 1.6 %copy-start = (bf16[1,768,1280]{2,1,0:T(8,128)(2,1)S(1)}, bf16[1,768,1280]{2,1,0:T(8,128)(2,1)}, u32[]{:S(2)}) copy-start(bf16[1,768,1280]{2,1,0:T(8,128)(2,1)} %param.5) | copy-start | bytes 5898244
  7.2 60.5 %reduce-scatter.2.cloned.1.call-start = ((), (), s32[]{:S(2)}) async-start(), calls=%async_computation.1 | async-start | bytes 3276800 | tf_op jit(solution)/shard_map/reduce_scatter | solution.py:17
  12.7 90.8 %all-reduce.2.cloned.1.call-start = ((), (), s32[]{:S(2)}) async-start(), calls=%async_computation.2 | async-start | bytes 1310720 | tf_op jit(solution)/shard_map/psum | solution.py:25
  105.4 26.2 %copy-start.1 = (f32[128,1280]{1,0:T(8,128)S(1)}, f32[128,1280]{1,0:T(8,128)}, u32[]{:S(2)}) copy-start(f32[128,1280]{1,0:T(8,128)} %all-reduce.2.cloned.1.call-done) | copy-start | bytes 1966084
Sparse Core Ops, SparseCore 0:
  12.8 54.8 reduce-scatter.1
  70.0 33.4 all-reduce.1
where the time goes:
time: 140 us; the launch traced here: 139 us
  waiting for transfers between devices  90.8 us (65%)
  blocking collectives  22.1 us (16%)
  between operations  15.5 us (11%)
  matrix products  7.42 us (5%)
  other arithmetic  2.75 us (2%)
    reduce_scatter x1, waiting for transfers between devices, on_device(): lax.psum_scatter(lax.dot_general(masked, upstream, (((0,), (0,)), ((), ()...  54.9 us
    psum x1, waiting for transfers between devices, on_device(): share = lax.psum(share, 'line')  35.8 us
    psum x1, blocking collectives, on_device(): total = lax.psum(jnp.sum(share * share), ('mod', 'loop'))  22.1 us
    dot_general x1, matrix products, on_device(): lax.dot_general(masked, upstream, (((0,), (0,)), ((), ())), preferred_ele...  3.95 us
    dot_general x1, matrix products, on_device(): lax.dot_general(upstream, weight, (((1,), (1,)), ((), ())), preferred_ele...  3.47 us
  transfers between devices with their start and end apart: 2, of which 2 were waited for; matrix products, arithmetic and copies ran while one was open for 0% of the time, Pallas kernels for 0%

commit v1 on v0

v1 whole, which is shorter than its diff:
```python
import jax
import jax.numpy as jnp
from jax import lax
from jax.sharding import PartitionSpec as P

CORES = 2


def swap(x, axis, distance):
    size = lax.axis_size(axis)
    return lax.ppermute(x, axis, [(i, i ^ distance) for i in range(size)])


def doubled(size):
    distance = 1
    while distance < size:
        yield distance
        distance *= 2


def piece(x, index):
    return lax.dynamic_index_in_dim(x, index, 0, keepdims=False)


def scatter_sum(x, axis, index, stride=1):
    size = x.shape[0]
    got = [swap(piece(x, index ^ d), axis, d * stride) for d in range(1, size)]
    total = piece(x, index)
    for part in got:
        total = total + part
    return total


def on_device(act, dy, w_out, counts):
    tokens = act[0]
    upstream = dy[0]
    weight = w_out[0]
    rows, hidden = tokens.shape
    block = weight.shape[1]
    n_loop = lax.axis_size("loop")
    n_y = lax.axis_size("line") // CORES
    z = lax.axis_index("loop")
    line = lax.axis_index("line")
    core = line % CORES
    y = line // CORES
    own_rows = hidden // n_loop
    half = block // CORES
    first = half * 3 // 5 // 128 * 128

    live = lax.broadcasted_iota(jnp.int32, (rows, 1), 0) < counts[0, 0]
    masked = jnp.where(live, tokens, jnp.zeros_like(tokens))
    entries = lax.axis_size("mod") * hidden * block

    def term(start, width):
        columns = lax.dynamic_slice_in_dim(upstream, start, width, 1)
        return lax.dot_general(
            masked, columns, (((0,), (0,)), ((), ())), preferred_element_type=jnp.float32
        )

    def chip_sum(start, width):
        other = swap(term((1 - core) * half + start, width), "line", 1)
        return term(core * half + start, width) + other

    late = chip_sum(first, half - first).reshape(n_loop, own_rows, half - first)
    early = chip_sum(0, first).reshape(n_loop, n_y, own_rows // n_y, first)
    early = scatter_sum(early.transpose(1, 0, 2, 3), "line", y, CORES)
    late = scatter_sum(late, "loop", z)
    early = scatter_sum(early, "loop", z)
    for d in doubled(n_y):
        late = late + swap(late, "line", d * CORES)

    squares = jnp.sum(early * early, axis=0).reshape(-1, 128).sum(0)
    squares_late = jnp.sum(late * late, axis=0).reshape(-1, 128).sum(0)
    total = (squares + jnp.where(y == 0, squares_late, 0.0)).reshape(1, 128)
    for d in doubled(n_y * CORES):
        total = total + swap(total, "line", d)
    for d in doubled(n_loop):
        total = total + swap(total, "loop", d)
    for d in doubled(lax.axis_size("mod")):
        total = total + swap(total, "mod", d)
    factor = 1.0 / jnp.sqrt(jnp.sum(total) / entries + 1e-06)

    early = early[None]
    for d in doubled(n_y):
        other = swap(early, "line", d * CORES)
        upper = (y // d) % 2 == 1
        early = jnp.where(
            upper, jnp.concatenate([other, early]), jnp.concatenate([early, other])
        )
    mine = jnp.concatenate([early.reshape(own_rows, first), late], axis=1)
    other = swap(mine, "line", 1)
    share = jnp.where(
        core == 1,
        jnp.concatenate([other, mine], axis=1),
        jnp.concatenate([mine, other], axis=1),
    )
    clipped = share * factor

    back = lax.dot_general(
        upstream, weight, (((1,), (1,)), ((), ())), preferred_element_type=jnp.float32
    )
    hidden_grad = jnp.where(live, back, jnp.zeros_like(back)).astype(jnp.bfloat16)
    return (clipped[None], hidden_grad[None])


def solution(mesh):
    in_specs = (
        P("mod", ("loop", "line"), None),
        P("mod", ("loop", "line"), None),
        P("mod", None, None),
        P("mod", "loop", "line"),
    )
    out_specs = (P("mod", "loop", None), P("mod", ("loop", "line"), None))
    return jax.shard_map(
        on_device, mesh=mesh, in_specs=in_specs, out_specs=out_specs, check_vma=False
    )
```

time: 140 us -> 64.5 us (0.46)
  waiting for transfers between devices: 90.8 us -> 26.2 us
  blocking collectives: 22.1 us -> 0 us
  starting transfers between devices: 0.08 us -> 21.2 us
  between operations: 15.5 us -> 2.3 us
  matrix products: 7.42 us -> 10.3 us
    reduce_scatter x1 -> x0, waiting for transfers between devices: 54.9 us -> none  [on_device(): lax.psum_scatter(lax.dot_general(masked, upstream, (((0,), (0,)), ((), ()...]
    psum x1 -> x0, waiting for transfers between devices: 35.8 us -> none  [on_device(): share = lax.psum(share, 'line')]
    ppermute x0 -> x17, waiting for transfers between devices: none -> 26.2 us  [swap(): return lax.ppermute(x, axis, [(i, i ^ distance) for i in range(size)])]
    psum x1 -> x0, blocking collectives: 22.1 us -> none  [on_device(): total = lax.psum(jnp.sum(share * share), ('mod', 'loop'))]
    ppermute x0 -> x17, starting transfers between devices: none -> 21.2 us  [swap(): return lax.ppermute(x, axis, [(i, i ^ distance) for i in range(size)])]
    dot_general x1 -> x4, matrix products: 3.95 us -> 6.85 us  [term(): lax.dot_general(masked, columns, (((0,), (0,)), ((), ())), preferred_elem...]
  transfers between devices with their start and end apart: 2 -> 17, of which waited for: 2 -> 10; matrix products, arithmetic and copies ran while one was open for 0% -> 16% of each run, Pallas kernels for 0% -> 0%
where the time goes in v1:
time: 64.5 us; the launch traced here: 64.1 us
  waiting for transfers between devices  26.2 us (41%)
  starting transfers between devices  21.2 us (33%)
  matrix products  10.3 us (16%)
  other arithmetic  2.67 us (4%)
  between operations  2.3 us (4%)
  local copies, waits for them, and re-layouts  1.57 us (2%)
    ppermute x17, waiting for transfers between devices, swap(): return lax.ppermute(x, axis, [(i, i ^ distance) for i in range(size)])  26.2 us
    ppermute x17, starting transfers between devices, swap(): return lax.ppermute(x, axis, [(i, i ^ distance) for i in range(size)])  21.2 us
    dot_general x4, matrix products, term(): lax.dot_general(masked, columns, (((0,), (0,)), ((), ())), preferred_elem...  6.85 us
    dot_general x1, matrix products, on_device(): lax.dot_general(upstream, weight, (((1,), (1,)), ((), ())), preferred_ele...  3.41 us
  transfers between devices with their start and end apart: 17, of which 10 were waited for; matrix products, arithmetic and copies ran while one was open for 16% of the time, Pallas kernels for 0%

profile of v1, /device:TPU:0, one launch (start us, length us, event | category | flops | bytes accessed | tf_op | source)
XLA Modules:
  0.0 64.1 jit_solution(5753843885124585432)
XLA Ops:
  0.6 0.0 copy-start
  0.6 0.0 copy-start.1
  1.5 0.7 %copy-done = bf16[1,768,1280]{2,1,0:T(8,128)(2,1)S(1)} copy-done((bf16[1,768,1280]{2,1,0:T(8,128)(2,1)S(1)}, bf16[1,768,1280]{2,1,0:T(8,128)(2,1)}, u32[]{:S(2)}) %copy-start) | copy-done | bytes 1966104
  2.2 2.5 %fusion.10 = f32[512,256]{1,0:T(8,128)} fusion(bf16[1,768,1280]{2,1,0:T(8,128)(2,1)S(1)} %copy-done, s32[]{:T(128)S(6)} %select_n.137, bf16[1,768,512]{2,1,0:T(8,128)(2,1)} %param.4, pred[768]{0:T(1024)(128)(4,1)S(1)} %iota_compare_fusion), kind=kOutput, calls=%fused_computation.7 | convolution fusion | flops 201719808 | bytes 1704964 | tf_op jit(solution)/shard_map/dot_general | solution.py:56
  4.7 0.5 collective-permute-start.6
  5.2 0.0 copy-done.1
  5.2 0.7 %fusion.13 = f32[512,384]{1,0:T(8,128)S(1)} fusion(bf16[1,768,1280]{2,1,0:T(8,128)(2,1)S(1)} %copy-done, s32[]{:T(128)S(6)} %select_n.127, bf16[1,768,512]{2,1,0:T(8,128)(2,1)S(1)} %copy-done.1, pred[768]{0:T(1024)(128)(4,1)S(1)} %iota_compare_fusion), kind=kOutput, calls=%fused_computation.10 | convolution fusion | flops 302383104 | bytes 2163716 | tf_op jit(solution)/shard_map/dot_general | solution.py:56
  5.9 0.1 collective-permute-start
  6.0 1.0 %collective-permute-done.6 = f32[512,256]{1,0:T(8,128)} collective-permute-done((f32[512,256]{1,0:T(8,128)}, f32[512,256]{1,0:T(8,128)}, u32[]{:S(2)}, u32[]{:S(2)}) %collective-permute-start.6) | collective-permute-done | bytes 524320 | tf_op jit(solution)/shard_map/ppermute | solution.py:11
  7.0 1.6 %convolution_add_fusion.1 = f32[512,256]{1,0:T(8,128)S(1)} fusion(f32[512,256]{1,0:T(8,128)} %collective-permute-done.6, bf16[1,768,1280]{2,1,0:T(8,128)(2,1)S(1)} %copy-done, s32[]{:T(128)S(6)} %select_n.136, bf16[1,768,512]{2,1,0:T(8,128)(2,1)S(1)} %copy-done.1, pred[768]{0:T(1024)(128)(4,1)S(1)} %iota_compare_fusion), kind=kOutput, calls=%fused_computation.6 | convolution fusion | flops 201850880 | bytes 2229252 | tf_op jit(solution)/shard_map/dot_general | solution.py:56
  8.7 3.0 %collective-permute-start.7 = (f32[128,256]{1,0:T(8,128)S(1)}, f32[128,256]{1,0:T(8,128)S(1)}, u32[]{:S(2)}, u32[]{:S(2)}) collective-permute-start(f32[128,256]{1,0:T(8,128)S(1)} %get-tuple-element.6), channel_id=1, source_target_pairs={{0,4},{4,0},{8,12},{12,8},{1,5},{5,1},{9,13},{13,9},{2,6},{6,2},{1... | collective-permute-start | bytes 393224 | tf_op jit(solution)/shard_map/ppermute | solution.py:11
  11.7 2.6 %collective-permute-start.8 = (f32[128,256]{1,0:T(8,128)S(1)}, f32[128,256]{1,0:T(8,128)S(1)}, u32[]{:S(2)}, u32[]{:S(2)}) collective-permute-start(f32[128,256]{1,0:T(8,128)S(1)} %get-tuple-element.8), channel_id=1, source_target_pairs={{0,8},{4,12},{8,0},{12,4},{1,9},{5,13},{9,1},{13,5},{2,10},{6,14},... | collective-permute-start | bytes 393224 | tf_op jit(solution)/shard_map/ppermute | solution.py:11
  14.3 0.0 collective-permute-start.9
  14.3 0.0 collective-permute-done
  14.3 2.1 %convolution_add_fusion = f32[512,384]{1,0:T(8,128)S(1)} fusion(f32[512,384]{1,0:T(8,128)} %collective-permute-done, bf16[1,768,1280]{2,1,0:T(8,128)(2,1)S(1)} %copy-done, s32[]{:T(128)S(6)} %select_n.126, bf16[1,768,512]{2,1,0:T(8,128)(2,1)} %param.4, pred[768]{0:T(1024)(128)(4,1)S(1)} %iota_compare_fusion), kind=kOutput, calls=%fused_computation.5 | convolution fusion | flops 302579712 | bytes 2950148 | tf_op jit(solution)/shard_map/dot_general | solution.py:56
  16.4 0.8 %dynamic-slice_bitcast_fusion = f32[4,64,384]{2,1,0:T(8,128)} fusion(f32[4,2,64,384]{3,2,1,0:T(8,128)S(1)} %bitcast.82, s32[]{:T(128)S(6)} %select_n.129), kind=kLoop, calls=%fused_computation.25 | loop fusion | bytes 786436 | tf_op jit(solution)/shard_map/jit(dynamic_index_in_dim)/squeeze | solution.py:22
  17.1 1.7 %collective-permute-start.1 = (f32[4,64,384]{2,1,0:T(8,128)}, f32[4,64,384]{2,1,0:T(8,128)S(1)}, u32[]{:S(2)}, u32[]{:S(2)}) collective-permute-start(f32[4,64,384]{2,1,0:T(8,128)} %dynamic-slice_bitcast_fusion), channel_id=1, source_target_pairs={{0,2},{1,3},{2,0},{3,1},{4,6},{5,7},{6,4},{7,5},{8,10},{9,11},{10,... | collective-permute-start | bytes 1179656 | tf_op jit(solution)/shard_map/ppermute | solution.py:11
  18.9 0.0 collective-permute-done.7
  18.9 5.7 %collective-permute-done.8 = f32[128,256]{1,0:T(8,128)S(1)} collective-permute-done((f32[128,256]{1,0:T(8,128)S(1)}, f32[128,256]{1,0:T(8,128)S(1)}, u32[]{:S(2)}, u32[]{:S(2)}) %collective-permute-start.8) | collective-permute-done | bytes 131104 | tf_op jit(solution)/shard_map/ppermute | solution.py:11
  24.6 0.0 collective-permute-done.9
  24.6 1.6 %collective-permute-start.10 = (f32[128,256]{1,0:T(8,128)S(1)}, f32[128,256]{1,0:T(8,128)}, u32[]{:S(2)}, u32[]{:S(2)}) collective-permute-start(f32[128,256]{1,0:T(8,128)S(1)} %fusion.26), channel_id=1, source_target_pairs={{0,2},{1,3},{2,0},{3,1},{4,6},{5,7},{6,4},{7,5},{8,10},{9,11},{10,... | collective-permute-start | bytes 393224 | tf_op jit(solution)/shard_map/ppermute | solution.py:11
  26.2 4.6 %collective-permute-done.10 = f32[128,256]{1,0:T(8,128)} collective-permute-done((f32[128,256]{1,0:T(8,128)S(1)}, f32[128,256]{1,0:T(8,128)}, u32[]{:S(2)}, u32[]{:S(2)}) %collective-permute-start.10) | collective-permute-done | bytes 131104 | tf_op jit(solution)/shard_map/ppermute | solution.py:11
  30.9 0.9 %multiply_reduce_fusion = (f32[256]{0:T(256)S(1)}, f32[128,256]{1,0:T(8,128)S(1)}) fusion(f32[128,256]{1,0:T(8,128)S(1)} %fusion.26, f32[128,256]{1,0:T(8,128)} %collective-permute-done.10), kind=kLoop, calls=%fused_computation.31 | loop fusion | flops 98048 | bytes 394240 | tf_op jit(solution)/shard_map/reduce_sum | solution.py:73
  31.8 0.0 collective-permute-done.1
  31.9 1.3 %collective-permute-start.2 = (f32[64,384]{1,0:T(8,128)S(1)}, f32[64,384]{1,0:T(8,128)S(1)}, u32[]{:S(2)}, u32[]{:S(2)}) collective-permute-start(f32[64,384]{1,0:T(8,128)S(1)} %get-tuple-element.9), channel_id=1, source_target_pairs={{0,4},{4,0},{8,12},{12,8},{1,5},{5,1},{9,13},{13,9},{2,6},{6,2},{1... | collective-permute-start | bytes 294920 | tf_op jit(solution)/shard_map/ppermute | solution.py:11
  33.2 2.9 %collective-permute-start.3 = (f32[64,384]{1,0:T(8,128)S(1)}, f32[64,384]{1,0:T(8,128)S(1)}, u32[]{:S(2)}, u32[]{:S(2)}) collective-permute-start(f32[64,384]{1,0:T(8,128)S(1)} %get-tuple-element.11), channel_id=1, source_target_pairs={{0,8},{4,12},{8,0},{12,4},{1,9},{5,13},{9,1},{13,5},{2,10},{6,14},... | collective-permute-start | bytes 294920 | tf_op jit(solution)/shard_map/ppermute | solution.py:11
  36.1 0.3 collective-permute-start.4
  36.4 0.5 collective-permute-done.2
  36.8 4.4 %collective-permute-done.3 = f32[64,384]{1,0:T(8,128)S(1)} collective-permute-done((f32[64,384]{1,0:T(8,128)S(1)}, f32[64,384]{1,0:T(8,128)S(1)}, u32[]{:S(2)}, u32[]{:S(2)}) %collective-permute-start.3) | collective-permute-done | bytes 98336 | tf_op jit(solution)/shard_map/ppermute | solution.py:11
  41.2 1.4 %collective-permute-done.4 = f32[64,384]{1,0:T(8,128)S(1)} collective-permute-done((f32[64,384]{1,0:T(8,128)S(1)}, f32[64,384]{1,0:T(8,128)S(1)}, u32[]{:S(2)}, u32[]{:S(2)}) %collective-permute-start.4) | collective-permute-done | bytes 98336 | tf_op jit(solution)/shard_map/ppermute | solution.py:11
  42.7 1.6 %collective-permute-start.5 = (f32[1,64,384]{2,1,0:T(8,128)S(1)}, f32[1,64,384]{2,1,0:T(8,128)S(1)}, u32[]{:S(2)}, u32[]{:S(2)}) collective-permute-start(f32[1,64,384]{2,1,0:T(8,128)S(1)} %bitcast.86), channel_id=1, source_target_pairs={{0,2},{1,3},{2,0},{3,1},{4,6},{5,7},{6,4},{7,5},{8,10},{9,11},{10,... | collective-permute-start | bytes 294920 | tf_op jit(solution)/shard_map/ppermute | solution.py:11
  44.2 0.0 collective-permute-start.12
  44.2 1.1 %collective-permute-done.12 = f32[1,128]{1,0:T(1,128)S(1)} collective-permute-done((f32[1,128]{1,0:T(1,128)S(1)}, f32[1,128]{1,0:T(1,128)S(1)}, u32[]{:S(2)}, u32[]{:S(2)}) %collective-permute-start.12) | collective-permute-done | bytes 544 | tf_op jit(solution)/shard_map/ppermute | solution.py:11
  45.4 0.5 collective-permute-start.13
  45.9 3.0 %collective-permute-done.13 = f32[1,128]{1,0:T(1,128)S(1)} collective-permute-done((f32[1,128]{1,0:T(1,128)S(1)}, f32[1,128]{1,0:T(1,128)S(1)}, u32[]{:S(2)}, u32[]{:S(2)}) %collective-permute-start.13) | collective-permute-done | bytes 544 | tf_op jit(solution)/shard_map/ppermute | solution.py:11
  48.9 1.3 %collective-permute-start.14 = (f32[1,128]{1,0:T(1,128)S(1)}, f32[1,128]{1,0:T(1,128)S(1)}, u32[]{:S(2)}, u32[]{:S(2)}) collective-permute-start(f32[1,128]{1,0:T(1,128)S(1)} %add.144), channel_id=1, source_target_pairs={{0,4},{4,0},{8,12},{12,8},{1,5},{5,1},{9,13},{13,9},{2,6},{6,2},{1... | collective-permute-start | bytes 1544 | tf_op jit(solution)/shard_map/ppermute | solution.py:11
  50.2 2.2 %collective-permute-done.14 = f32[1,128]{1,0:T(1,128)S(1)} collective-permute-done((f32[1,128]{1,0:T(1,128)S(1)}, f32[1,128]{1,0:T(1,128)S(1)}, u32[]{:S(2)}, u32[]{:S(2)}) %collective-permute-start.14) | collective-permute-done | bytes 544 | tf_op jit(solution)/shard_map/ppermute | solution.py:11
  52.5 2.3 %collective-permute-start.15 = (f32[1,128]{1,0:T(1,128)S(1)}, f32[1,128]{1,0:T(1,128)S(1)}, u32[]{:S(2)}, u32[]{:S(2)}) collective-permute-start(f32[1,128]{1,0:T(1,128)S(1)} %add.145), channel_id=1, source_target_pairs={{0,8},{4,12},{8,0},{12,4},{1,9},{5,13},{9,1},{13,5},{2,10},{6,14},... | collective-permute-start | bytes 1544 | tf_op jit(solution)/shard_map/ppermute | solution.py:11
  54.7 2.1 %collective-permute-done.15 = f32[1,128]{1,0:T(1,128)S(1)} collective-permute-done((f32[1,128]{1,0:T(1,128)S(1)}, f32[1,128]{1,0:T(1,128)S(1)}, u32[]{:S(2)}, u32[]{:S(2)}) %collective-permute-start.15) | collective-permute-done | bytes 544 | tf_op jit(solution)/shard_map/ppermute | solution.py:11
  56.9 1.5 %collective-permute-start.16 = (f32[1,128]{1,0:T(1,128)S(1)}, f32[1,128]{1,0:T(1,128)S(1)}, u32[]{:S(2)}, u32[]{:S(2)}) collective-permute-start(f32[1,128]{1,0:T(1,128)S(1)} %add.146), channel_id=1, source_target_pairs={{0,16},{16,0},{1,17},{17,1},{2,18},{18,2},{3,19},{19,3},{4,20},{20... | collective-permute-start | bytes 1544 | tf_op jit(solution)/shard_map/ppermute | solution.py:11
  58.4 0.0 collective-permute-done.5
  58.4 0.1 collective-permute-start.11
  58.5 3.4 %fusion.5 = bf16[1,768,512]{2,1,0:T(8,128)(2,1)} fusion(bf16[1,512,1280]{2,1,0:T(8,128)(2,1)} %param.6, bf16[1,768,1280]{2,1,0:T(8,128)(2,1)S(1)} %copy-done, pred[768]{0:T(1024)(128)(4,1)S(1)} %iota_compare_fusion), kind=kOutput, calls=%fused_computation.4 | convolution fusion | flops 1007419392 | bytes 4064000 | tf_op jit(solution)/shard_map/dot_general | solution.py:99
  61.9 0.0 collective-permute-done.16
  61.9 0.6 add_reduce_fusion
  63.2 0.0 collective-permute-done.11
  63.2 0.9 %fusion.16 = f32[1,128,1280]{2,1,0:T(8,128)} fusion(f32[1,128,256]{2,1,0:T(8,128)S(1)} %bitcast.81, f32[1,128,384]{2,1,0:T(8,128)S(1)} %bitcast.80, f32[1,128,640]{2,1,0:T(8,128)S(1)} %bitcast.88, f32[]{:T(128)S(6)} %sqrt.3, pred[]{:T(512)S(6)} %eq.12), kind=kLoop, calls=%fused_computation.15 | loop fusion | flops 983040 | bytes 1310725 | tf_op jit(solution)/shard_map/mul | solution.py:97
  (15 shorter events, 0.3 us)
Async XLA Ops:
  0.6 1.6 %copy-start = (bf16[1,768,1280]{2,1,0:T(8,128)(2,1)S(1)}, bf16[1,768,1280]{2,1,0:T(8,128)(2,1)}, u32[]{:S(2)}) copy-start(bf16[1,768,1280]{2,1,0:T(8,128)(2,1)} %param.5) | copy-start | bytes 5898244
  0.6 4.5 %copy-start.1 = (bf16[1,768,512]{2,1,0:T(8,128)(2,1)S(1)}, bf16[1,768,512]{2,1,0:T(8,128)(2,1)}, u32[]{:S(2)}) copy-start(bf16[1,768,512]{2,1,0:T(8,128)(2,1)} %param.4) | copy-start | bytes 2359300
  4.7 2.3 %collective-permute-start.6 = (f32[512,256]{1,0:T(8,128)}, f32[512,256]{1,0:T(8,128)}, u32[]{:S(2)}, u32[]{:S(2)}) collective-permute-start(f32[512,256]{1,0:T(8,128)} %fusion.10), channel_id=1, source_target_pairs={{0,1},{1,0},{2,3},{3,2},{4,5},{5,4},{6,7},{7,6},{8,9},{9,8},{10,11... | collective-permute-start | bytes 1572872 | tf_op jit(solution)/shard_map/ppermute | solution.py:11
  5.9 8.4 %collective-permute-start = (f32[512,384]{1,0:T(8,128)S(1)}, f32[512,384]{1,0:T(8,128)}, u32[]{:S(2)}, u32[]{:S(2)}) collective-permute-start(f32[512,384]{1,0:T(8,128)S(1)} %fusion.13), channel_id=1, source_target_pairs={{0,1},{1,0},{2,3},{3,2},{4,5},{5,4},{6,7},{7,6},{8,9},{9,8},{10,11... | collective-permute-start | bytes 2359304 | tf_op jit(solution)/shard_map/ppermute | solution.py:11
  8.7 10.2 %collective-permute-start.7 = (f32[128,256]{1,0:T(8,128)S(1)}, f32[128,256]{1,0:T(8,128)S(1)}, u32[]{:S(2)}, u32[]{:S(2)}) collective-permute-start(f32[128,256]{1,0:T(8,128)S(1)} %get-tuple-element.6), channel_id=1, source_target_pairs={{0,4},{4,0},{8,12},{12,8},{1,5},{5,1},{9,13},{13,9},{2,6},{6,2},{1... | collective-permute-start | bytes 393224 | tf_op jit(solution)/shard_map/ppermute | solution.py:11
  11.7 12.9 %collective-permute-start.8 = (f32[128,256]{1,0:T(8,128)S(1)}, f32[128,256]{1,0:T(8,128)S(1)}, u32[]{:S(2)}, u32[]{:S(2)}) collective-permute-start(f32[128,256]{1,0:T(8,128)S(1)} %get-tuple-element.8), channel_id=1, source_target_pairs={{0,8},{4,12},{8,0},{12,4},{1,9},{5,13},{9,1},{13,5},{2,10},{6,14},... | collective-permute-start | bytes 393224 | tf_op jit(solution)/shard_map/ppermute | solution.py:11
  14.3 10.3 %collective-permute-start.9 = (f32[128,256]{1,0:T(8,128)S(1)}, f32[128,256]{1,0:T(8,128)S(1)}, u32[]{:S(2)}, u32[]{:S(2)}) collective-permute-start(f32[128,256]{1,0:T(8,128)S(1)} %get-tuple-element.7), channel_id=1, source_target_pairs={{0,12},{4,8},{8,4},{12,0},{1,13},{5,9},{9,5},{13,1},{2,14},{6,10},... | collective-permute-start | bytes 393224 | tf_op jit(solution)/shard_map/ppermute | solution.py:11
  17.1 14.7 %collective-permute-start.1 = (f32[4,64,384]{2,1,0:T(8,128)}, f32[4,64,384]{2,1,0:T(8,128)S(1)}, u32[]{:S(2)}, u32[]{:S(2)}) collective-permute-start(f32[4,64,384]{2,1,0:T(8,128)} %dynamic-slice_bitcast_fusion), channel_id=1, source_target_pairs={{0,2},{1,3},{2,0},{3,1},{4,6},{5,7},{6,4},{7,5},{8,10},{9,11},{10,... | collective-permute-start | bytes 1179656 | tf_op jit(solution)/shard_map/ppermute | solution.py:11
  24.6 6.2 %collective-permute-start.10 = (f32[128,256]{1,0:T(8,128)S(1)}, f32[128,256]{1,0:T(8,128)}, u32[]{:S(2)}, u32[]{:S(2)}) collective-permute-start(f32[128,256]{1,0:T(8,128)S(1)} %fusion.26), channel_id=1, source_target_pairs={{0,2},{1,3},{2,0},{3,1},{4,6},{5,7},{6,4},{7,5},{8,10},{9,11},{10,... | collective-permute-start | bytes 393224 | tf_op jit(solution)/shard_map/ppermute | solution.py:11
  31.9 4.9 %collective-permute-start.2 = (f32[64,384]{1,0:T(8,128)S(1)}, f32[64,384]{1,0:T(8,128)S(1)}, u32[]{:S(2)}, u32[]{:S(2)}) collective-permute-start(f32[64,384]{1,0:T(8,128)S(1)} %get-tuple-element.9), channel_id=1, source_target_pairs={{0,4},{4,0},{8,12},{12,8},{1,5},{5,1},{9,13},{13,9},{2,6},{6,2},{1... | collective-permute-start | bytes 294920 | tf_op jit(solution)/shard_map/ppermute | solution.py:11
  33.2 8.1 %collective-permute-start.3 = (f32[64,384]{1,0:T(8,128)S(1)}, f32[64,384]{1,0:T(8,128)S(1)}, u32[]{:S(2)}, u32[]{:S(2)}) collective-permute-start(f32[64,384]{1,0:T(8,128)S(1)} %get-tuple-element.11), channel_id=1, source_target_pairs={{0,8},{4,12},{8,0},{12,4},{1,9},{5,13},{9,1},{13,5},{2,10},{6,14},... | collective-permute-start | bytes 294920 | tf_op jit(solution)/shard_map/ppermute | solution.py:11
  36.1 6.5 %collective-permute-start.4 = (f32[64,384]{1,0:T(8,128)S(1)}, f32[64,384]{1,0:T(8,128)S(1)}, u32[]{:S(2)}, u32[]{:S(2)}) collective-permute-start(f32[64,384]{1,0:T(8,128)S(1)} %get-tuple-element.10), channel_id=1, source_target_pairs={{0,12},{4,8},{8,4},{12,0},{1,13},{5,9},{9,5},{13,1},{2,14},{6,10},... | collective-permute-start | bytes 294920 | tf_op jit(solution)/shard_map/ppermute | solution.py:11
  42.7 15.7 %collective-permute-start.5 = (f32[1,64,384]{2,1,0:T(8,128)S(1)}, f32[1,64,384]{2,1,0:T(8,128)S(1)}, u32[]{:S(2)}, u32[]{:S(2)}) collective-permute-start(f32[1,64,384]{2,1,0:T(8,128)S(1)} %bitcast.86), channel_id=1, source_target_pairs={{0,2},{1,3},{2,0},{3,1},{4,6},{5,7},{6,4},{7,5},{8,10},{9,11},{10,... | collective-permute-start | bytes 294920 | tf_op jit(solution)/shard_map/ppermute | solution.py:11
  44.2 1.1 %collective-permute-start.12 = (f32[1,128]{1,0:T(1,128)S(1)}, f32[1,128]{1,0:T(1,128)S(1)}, u32[]{:S(2)}, u32[]{:S(2)}) collective-permute-start(f32[1,128]{1,0:T(1,128)S(1)} %fusion.34), channel_id=1, source_target_pairs={{0,1},{1,0},{2,3},{3,2},{4,5},{5,4},{6,7},{7,6},{8,9},{9,8},{10,11... | collective-permute-start | bytes 1544 | tf_op jit(solution)/shard_map/ppermute | solution.py:11
  45.4 3.5 %collective-permute-start.13 = (f32[1,128]{1,0:T(1,128)S(1)}, f32[1,128]{1,0:T(1,128)S(1)}, u32[]{:S(2)}, u32[]{:S(2)}) collective-permute-start(f32[1,128]{1,0:T(1,128)S(1)} %add.143), channel_id=1, source_target_pairs={{0,2},{1,3},{2,0},{3,1},{4,6},{5,7},{6,4},{7,5},{8,10},{9,11},{10,... | collective-permute-start | bytes 1544 | tf_op jit(solution)/shard_map/ppermute | solution.py:11
  48.9 3.5 %collective-permute-start.14 = (f32[1,128]{1,0:T(1,128)S(1)}, f32[1,128]{1,0:T(1,128)S(1)}, u32[]{:S(2)}, u32[]{:S(2)}) collective-permute-start(f32[1,128]{1,0:T(1,128)S(1)} %add.144), channel_id=1, source_target_pairs={{0,4},{4,0},{8,12},{12,8},{1,5},{5,1},{9,13},{13,9},{2,6},{6,2},{1... | collective-permute-start | bytes 1544 | tf_op jit(solution)/shard_map/ppermute | solution.py:11
  52.5 4.4 %collective-permute-start.15 = (f32[1,128]{1,0:T(1,128)S(1)}, f32[1,128]{1,0:T(1,128)S(1)}, u32[]{:S(2)}, u32[]{:S(2)}) collective-permute-start(f32[1,128]{1,0:T(1,128)S(1)} %add.145), channel_id=1, source_target_pairs={{0,8},{4,12},{8,0},{12,4},{1,9},{5,13},{9,1},{13,5},{2,10},{6,14},... | collective-permute-start | bytes 1544 | tf_op jit(solution)/shard_map/ppermute | solution.py:11
  56.9 5.0 %collective-permute-start.16 = (f32[1,128]{1,0:T(1,128)S(1)}, f32[1,128]{1,0:T(1,128)S(1)}, u32[]{:S(2)}, u32[]{:S(2)}) collective-permute-start(f32[1,128]{1,0:T(1,128)S(1)} %add.146), channel_id=1, source_target_pairs={{0,16},{16,0},{1,17},{17,1},{2,18},{18,2},{3,19},{19,3},{4,20},{20... | collective-permute-start | bytes 1544 | tf_op jit(solution)/shard_map/ppermute | solution.py:11
  58.4 4.8 %collective-permute-start.11 = (f32[128,640]{1,0:T(8,128)S(1)}, f32[128,640]{1,0:T(8,128)S(1)}, u32[]{:S(2)}, u32[]{:S(2)}) collective-permute-start(f32[128,640]{1,0:T(8,128)S(1)} %pad_maximum_fusion), channel_id=1, source_target_pairs={{0,1},{1,0},{2,3},{3,2},{4,5},{5,4},{6,7},{7,6},{8,9},{9,8},{10,11... | collective-permute-start | bytes 983048 | tf_op jit(solution)/shard_map/ppermute | solution.py:11

commit v2 on v1

--- a/solution.py
+++ b/solution.py
@@ -18,13 +18,18 @@
         distance *= 2
 
 
+def after(x, *ready):
+    return lax.optimization_barrier((x, *ready))[0]
+
+
 def piece(x, index):
     return lax.dynamic_index_in_dim(x, index, 0, keepdims=False)
 
 
 def scatter_sum(x, axis, index, stride=1):
     size = x.shape[0]
-    got = [swap(piece(x, index ^ d), axis, d * stride) for d in range(1, size)]
+    order = sorted(range(1, size), key=lambda d: -(d ^ 1))
+    got = [swap(piece(x, index ^ d), axis, d * stride) for d in order]
     total = piece(x, index)
     for part in got:
         total = total + part
@@ -51,38 +56,49 @@
     masked = jnp.where(live, tokens, jnp.zeros_like(tokens))
     entries = lax.axis_size("mod") * hidden * block
 
-    def term(start, width):
-        columns = lax.dynamic_slice_in_dim(upstream, start, width, 1)
+    def term(start, width, *ready):
+        columns = lax.dynamic_slice_in_dim(after(upstream, *ready), start, width, 1)
         return lax.dot_general(
             masked, columns, (((0,), (0,)), ((), ())), preferred_element_type=jnp.float32
         )
 
-    def chip_sum(start, width):
-        other = swap(term((1 - core) * half + start, width), "line", 1)
-        return term(core * half + start, width) + other
+    early_other = swap(term((1 - core) * half, first), "line", 1)
+    late_other = swap(term((1 - core) * half + first, half - first), "line", 1)
+    early = term(core * half, first) + early_other
+    late = term(core * half + first, half - first, early) + late_other
+    back = lax.dot_general(
+        after(upstream, late), weight, (((1,), (1,)), ((), ())), preferred_element_type=jnp.float32
+    )
+    hidden_grad = jnp.where(live, back, jnp.zeros_like(back)).astype(jnp.bfloat16)
 
-    late = chip_sum(first, half - first).reshape(n_loop, own_rows, half - first)
-    early = chip_sum(0, first).reshape(n_loop, n_y, own_rows // n_y, first)
-    early = scatter_sum(early.transpose(1, 0, 2, 3), "line", y, CORES)
-    late = scatter_sum(late, "loop", z)
+    early = early.reshape(n_loop, n_y, own_rows // n_y, first).transpose(1, 0, 2, 3)
+    early = scatter_sum(early, "line", y, CORES)
+    late = scatter_sum(late.reshape(n_loop, own_rows, half - first), "loop", z)
+    early_part = early
     early = scatter_sum(early, "loop", z)
+    late = after(late, early_part)
     for d in doubled(n_y):
         late = late + swap(late, "line", d * CORES)
 
     squares = jnp.sum(early * early, axis=0).reshape(-1, 128).sum(0)
     squares_late = jnp.sum(late * late, axis=0).reshape(-1, 128).sum(0)
     total = (squares + jnp.where(y == 0, squares_late, 0.0)).reshape(1, 128)
-    for d in doubled(n_y * CORES):
+    total = after(total, hidden_grad)
+    for d in doubled(CORES):
         total = total + swap(total, "line", d)
+    spread = total
     for d in doubled(n_loop):
         total = total + swap(total, "loop", d)
     for d in doubled(lax.axis_size("mod")):
         total = total + swap(total, "mod", d)
+    over_towers = total
+    for d in doubled(n_y):
+        total = total + swap(total, "line", d * CORES)
     factor = 1.0 / jnp.sqrt(jnp.sum(total) / entries + 1e-06)
 
-    early = early[None]
+    early = after(early, spread)[None]
     for d in doubled(n_y):
-        other = swap(early, "line", d * CORES)
+        other = after(swap(early, "line", d * CORES), over_towers)
         upper = (y // d) % 2 == 1
         early = jnp.where(
             upper, jnp.concatenate([other, early]), jnp.concatenate([early, other])
@@ -96,10 +112,6 @@
     )
     clipped = share * factor
 
-    back = lax.dot_general(
-        upstream, weight, (((1,), (1,)), ((), ())), preferred_element_type=jnp.float32
-    )
-    hidden_grad = jnp.where(live, back, jnp.zeros_like(back)).astype(jnp.bfloat16)
     return (clipped[None], hidden_grad[None])
 
 

time: 64.5 us -> 56.7 us (0.88)
  waiting for transfers between devices: 26.2 us -> 20.2 us
  matrix products: 10.3 us -> 8.71 us
  starting transfers between devices: 21.2 us -> 22.7 us
  other arithmetic: 2.67 us -> 1.78 us
  local copies, waits for them, and re-layouts: 1.57 us -> 0.84 us
    ppermute x17, waiting for transfers between devices: 26.2 us -> 20.2 us  [swap(): return lax.ppermute(x, axis, [(i, i ^ distance) for i in range(size)])]
    ppermute x17, starting transfers between devices: 21.2 us -> 22.7 us  [swap(): return lax.ppermute(x, axis, [(i, i ^ distance) for i in range(size)])]
    dot_general x1, matrix products: 3.41 us -> 2.09 us  [on_device(): lax.dot_general(after(upstream, late), weight, (((1,), (1,)), ((), ())),...]
    reduce_sum x2, other arithmetic: 0.96 us -> 0.06 us  [on_device(): squares_late = jnp.sum(late * late, axis=0).reshape(-1, 128).sum(0)]
    squeeze x3, local copies, waits for them, and re-layouts: 0.85 us -> 0.1 us  [piece(): return lax.dynamic_index_in_dim(x, index, 0, keepdims=False)]
  transfers between devices with their start and end apart: 17 -> 17, of which waited for: 10 -> 9; matrix products, arithmetic and copies ran while one was open for 16% -> 14% of each run, Pallas kernels for 0% -> 0%
where the time goes in v2:
time: 56.7 us; the launch traced here: 56.5 us
  starting transfers between devices  22.7 us (40%)
  waiting for transfers between devices  20.2 us (36%)
  matrix products  8.71 us (15%)
  between operations  2.29 us (4%)
  other arithmetic  1.78 us (3%)
  local copies, waits for them, and re-layouts  0.84 us (1%)
    ppermute x17, starting transfers between devices, swap(): return lax.ppermute(x, axis, [(i, i ^ distance) for i in range(size)])  22.7 us
    ppermute x17, waiting for transfers between devices, swap(): return lax.ppermute(x, axis, [(i, i ^ distance) for i in range(size)])  20.2 us
    dot_general x4, matrix products, term(): lax.dot_general(masked, columns, (((0,), (0,)), ((), ())), preferred_elem...  6.62 us
    dot_general x1, matrix products, on_device(): lax.dot_general(after(upstream, late), weight, (((1,), (1,)), ((), ())),...  2.09 us
  transfers between devices with their start and end apart: 17, of which 9 were waited for; matrix products, arithmetic and copies ran while one was open for 14% of the time, Pallas kernels for 0%

profile of v2, /device:TPU:0, one launch (start us, length us, event | category | flops | bytes accessed | tf_op | source)
XLA Modules:
  0.0 56.5 jit_solution(13236911285753307781)
XLA Ops:
  0.6 0.0 copy-start
  0.6 0.0 copy-start.2
  1.5 0.7 %copy-done = bf16[1,768,1280]{2,1,0:T(8,128)(2,1)S(1)} copy-done((bf16[1,768,1280]{2,1,0:T(8,128)(2,1)S(1)}, bf16[1,768,1280]{2,1,0:T(8,128)(2,1)}, u32[]{:S(2)}) %copy-start) | copy-done | bytes 1966104
  2.2 1.8 %fusion.2 = f32[512,384]{1,0:T(8,128)S(1)} fusion(bf16[768,1280]{1,0:T(8,128)(2,1)S(1)} %bitcast.60, s32[]{:T(128)S(6)} %select_n.120, bf16[1,768,512]{2,1,0:T(8,128)(2,1)} %param.4, pred[768]{0:T(1024)(128)(4,1)S(1)} %iota_compare_fusion), kind=kOutput, calls=%fused_computation.7 | convolution fusion | flops 302383104 | bytes 2163716 | tf_op jit(solution)/shard_map/dot_general | solution.py:61
  4.0 0.5 collective-permute-start
  4.5 0.0 copy-done.2
  4.5 1.4 %fusion.5 = f32[512,256]{1,0:T(8,128)} fusion(bf16[768,1280]{1,0:T(8,128)(2,1)S(1)} %bitcast.56, s32[]{:T(128)S(6)} %select_n.129, bf16[1,768,512]{2,1,0:T(8,128)(2,1)S(1)} %copy-done.2, pred[768]{0:T(1024)(128)(4,1)S(1)} %iota_compare_fusion), kind=kOutput, calls=%fused_computation.11 | convolution fusion | flops 201719808 | bytes 1704964 | tf_op jit(solution)/shard_map/dot_general | solution.py:61
  5.9 0.1 collective-permute-start.5
  6.0 0.6 %collective-permute-done = f32[512,384]{1,0:T(8,128)} collective-permute-done((f32[512,384]{1,0:T(8,128)S(1)}, f32[512,384]{1,0:T(8,128)}, u32[]{:S(2)}, u32[]{:S(2)}) %collective-permute-start) | collective-permute-done | bytes 786464 | tf_op jit(solution)/shard_map/ppermute | solution.py:11
  6.6 1.8 %convolution_add_fusion = f32[512,384]{1,0:T(8,128)S(1)} fusion(f32[512,384]{1,0:T(8,128)} %collective-permute-done, bf16[768,1280]{1,0:T(8,128)(2,1)S(1)} %bitcast.59, s32[]{:T(128)S(6)} %select_n.119, bf16[1,768,512]{2,1,0:T(8,128)(2,1)S(1)} %copy-done.2, pred[768]{0:T(1024)(128)(4,1)S(1)} %iota_compare_fusion), kind=kOutput, calls=%fused_computation.2 | convolution fusion | flops 302579712 | bytes 2950148 | tf_op jit(solution)/shard_map/dot_general | solution.py:61
  8.4 0.0 copy-start.1
  8.5 3.0 %collective-permute-start.1 = (f32[4,64,384]{2,1,0:T(8,128)S(1)}, f32[4,64,384]{2,1,0:T(8,128)S(1)}, u32[]{:S(2)}, u32[]{:S(2)}) collective-permute-start(f32[4,64,384]{2,1,0:T(8,128)S(1)} %dynamic-slice_bitcast_fusion), channel_id=1, source_target_pairs={{0,2},{1,3},{2,0},{3,1},{4,6},{5,7},{6,4},{7,5},{8,10},{9,11},{10,... | collective-permute-start | bytes 1179656 | tf_op jit(solution)/shard_map/ppermute | solution.py:11
  11.4 0.0 collective-permute-done.5
  11.4 1.6 %convolution_add_fusion.1 = f32[512,256]{1,0:T(8,128)S(1)} fusion(f32[512,256]{1,0:T(8,128)} %collective-permute-done.5, bf16[768,1280]{1,0:T(8,128)(2,1)S(1)} %bitcast.57, s32[]{:T(128)S(6)} %select_n.128, bf16[1,768,512]{2,1,0:T(8,128)(2,1)S(1)} %copy-done.2, pred[768]{0:T(1024)(128)(4,1)S(1)} %iota_compare_fusion), kind=kOutput, calls=%fused_computation.3 | convolution fusion | flops 201850880 | bytes 2229252 | tf_op jit(solution)/shard_map/dot_general | solution.py:61
  13.1 2.7 %collective-permute-start.6 = (f32[128,256]{1,0:T(8,128)S(1)}, f32[128,256]{1,0:T(8,128)S(1)}, u32[]{:S(2)}, u32[]{:S(2)}) collective-permute-start(f32[128,256]{1,0:T(8,128)S(1)} %get-tuple-element.18), channel_id=1, source_target_pairs={{0,8},{4,12},{8,0},{12,4},{1,9},{5,13},{9,1},{13,5},{2,10},{6,14},... | collective-permute-start | bytes 393224 | tf_op jit(solution)/shard_map/ppermute | solution.py:11
  15.8 1.3 %collective-permute-start.7 = (f32[128,256]{1,0:T(8,128)S(1)}, f32[128,256]{1,0:T(8,128)S(1)}, u32[]{:S(2)}, u32[]{:S(2)}) collective-permute-start(f32[128,256]{1,0:T(8,128)S(1)} %get-tuple-element.20), channel_id=1, source_target_pairs={{0,12},{4,8},{8,4},{12,0},{1,13},{5,9},{9,5},{13,1},{2,14},{6,10},... | collective-permute-start | bytes 393224 | tf_op jit(solution)/shard_map/ppermute | solution.py:11
  17.1 0.2 collective-permute-start.8
  17.3 0.0 copy-done.1
  17.3 2.1 %select_convert_fusion = bf16[768,512]{1,0:T(8,128)(2,1)} fusion(bf16[768,1280]{1,0:T(8,128)(2,1)S(1)} %bitcast.58, bf16[1,512,1280]{2,1,0:T(8,128)(2,1)S(1)} %copy-done.1, pred[768]{0:T(1024)(128)(4,1)S(1)} %iota_compare_fusion), kind=kOutput, calls=%fused_computation | convolution fusion | flops 1007419392 | bytes 4064000 | tf_op jit(solution)/shard_map/dot_general | solution.py:69
  19.4 1.4 %collective-permute-done.1 = f32[4,64,384]{2,1,0:T(8,128)S(1)} collective-permute-done((f32[4,64,384]{2,1,0:T(8,128)S(1)}, f32[4,64,384]{2,1,0:T(8,128)S(1)}, u32[]{:S(2)}, u32[]{:S(2)}) %collective-permute-start.1) | collective-permute-done | bytes 393248 | tf_op jit(solution)/shard_map/ppermute | solution.py:11
  20.9 2.9 %collective-permute-start.2 = (f32[64,384]{1,0:T(8,128)S(1)}, f32[64,384]{1,0:T(8,128)S(1)}, u32[]{:S(2)}, u32[]{:S(2)}) collective-permute-start(f32[64,384]{1,0:T(8,128)S(1)} %get-tuple-element.21), channel_id=1, source_target_pairs={{0,8},{4,12},{8,0},{12,4},{1,9},{5,13},{9,1},{13,5},{2,10},{6,14},... | collective-permute-start | bytes 294920 | tf_op jit(solution)/shard_map/ppermute | solution.py:11
  23.8 1.3 %collective-permute-start.3 = (f32[64,384]{1,0:T(8,128)S(1)}, f32[64,384]{1,0:T(8,128)S(1)}, u32[]{:S(2)}, u32[]{:S(2)}) collective-permute-start(f32[64,384]{1,0:T(8,128)S(1)} %get-tuple-element.23), channel_id=1, source_target_pairs={{0,12},{4,8},{8,4},{12,0},{1,13},{5,9},{9,5},{13,1},{2,14},{6,10},... | collective-permute-start | bytes 294920 | tf_op jit(solution)/shard_map/ppermute | solution.py:11
  25.2 1.7 %collective-permute-done.6 = f32[128,256]{1,0:T(8,128)S(1)} collective-permute-done((f32[128,256]{1,0:T(8,128)S(1)}, f32[128,256]{1,0:T(8,128)S(1)}, u32[]{:S(2)}, u32[]{:S(2)}) %collective-permute-start.6) | collective-permute-done | bytes 131104 | tf_op jit(solution)/shard_map/ppermute | solution.py:11
  26.9 0.0 collective-permute-start.4
  26.9 0.0 collective-permute-done.7
  26.9 0.0 collective-permute-done.8
  27.0 0.1 collective-permute-start.9
  27.0 8.1 %collective-permute-done.2 = f32[64,384]{1,0:T(8,128)S(1)} collective-permute-done((f32[64,384]{1,0:T(8,128)S(1)}, f32[64,384]{1,0:T(8,128)S(1)}, u32[]{:S(2)}, u32[]{:S(2)}) %collective-permute-start.2) | collective-permute-done | bytes 98336 | tf_op jit(solution)/shard_map/ppermute | solution.py:11
  35.2 0.0 collective-permute-done.3
  35.2 0.0 collective-permute-done.4
  35.2 0.0 collective-permute-done.9
  35.3 0.1 collective-permute-start.10
  35.4 1.1 %collective-permute-done.10 = f32[1,128]{1,0:T(1,128)S(1)} collective-permute-done((f32[1,128]{1,0:T(1,128)S(1)}, f32[1,128]{1,0:T(1,128)S(1)}, u32[]{:S(2)}, u32[]{:S(2)}) %collective-permute-start.10) | collective-permute-done | bytes 544 | tf_op jit(solution)/shard_map/ppermute | solution.py:11
  36.5 0.2 collective-permute-start.11
  36.7 3.5 %collective-permute-start.12 = (f32[1,128]{1,0:T(1,128)S(1)}, f32[1,128]{1,0:T(1,128)S(1)}, u32[]{:S(2)}, u32[]{:S(2)}) collective-permute-start(f32[1,128]{1,0:T(1,128)S(1)} %add.143), channel_id=1, source_target_pairs={{0,4},{4,0},{8,12},{12,8},{1,5},{5,1},{9,13},{13,9},{2,6},{6,2},{1... | collective-permute-start | bytes 1544 | tf_op jit(solution)/shard_map/ppermute | solution.py:11
  40.1 1.5 %collective-permute-done.12 = f32[1,128]{1,0:T(1,128)S(1)} collective-permute-done((f32[1,128]{1,0:T(1,128)S(1)}, f32[1,128]{1,0:T(1,128)S(1)}, u32[]{:S(2)}, u32[]{:S(2)}) %collective-permute-start.12) | collective-permute-done | bytes 544 | tf_op jit(solution)/shard_map/ppermute | solution.py:11
  41.7 3.8 %collective-permute-start.13 = (f32[1,128]{1,0:T(1,128)S(1)}, f32[1,128]{1,0:T(1,128)S(1)}, u32[]{:S(2)}, u32[]{:S(2)}) collective-permute-start(f32[1,128]{1,0:T(1,128)S(1)} %add.144), channel_id=1, source_target_pairs={{0,8},{4,12},{8,0},{12,4},{1,9},{5,13},{9,1},{13,5},{2,10},{6,14},... | collective-permute-start | bytes 1544 | tf_op jit(solution)/shard_map/ppermute | solution.py:11
  45.5 1.5 %collective-permute-done.13 = f32[1,128]{1,0:T(1,128)S(1)} collective-permute-done((f32[1,128]{1,0:T(1,128)S(1)}, f32[1,128]{1,0:T(1,128)S(1)}, u32[]{:S(2)}, u32[]{:S(2)}) %collective-permute-start.13) | collective-permute-done | bytes 544 | tf_op jit(solution)/shard_map/ppermute | solution.py:11
  47.0 1.5 %collective-permute-start.14 = (f32[1,128]{1,0:T(1,128)S(1)}, f32[1,128]{1,0:T(1,128)S(1)}, u32[]{:S(2)}, u32[]{:S(2)}) collective-permute-start(f32[1,128]{1,0:T(1,128)S(1)} %add.145), channel_id=1, source_target_pairs={{0,16},{16,0},{1,17},{17,1},{2,18},{18,2},{3,19},{19,3},{4,20},{20... | collective-permute-start | bytes 1544 | tf_op jit(solution)/shard_map/ppermute | solution.py:11
  48.5 2.0 %collective-permute-done.14 = f32[1,128]{1,0:T(1,128)S(1)} collective-permute-done((f32[1,128]{1,0:T(1,128)S(1)}, f32[1,128]{1,0:T(1,128)S(1)}, u32[]{:S(2)}, u32[]{:S(2)}) %collective-permute-start.14) | collective-permute-done | bytes 544 | tf_op jit(solution)/shard_map/ppermute | solution.py:11
  50.5 0.0 collective-permute-done.11
  50.6 0.1 collective-permute-start.15
  50.7 1.5 %collective-permute-start.16 = (f32[1,128]{1,0:T(1,128)S(1)}, f32[1,128]{1,0:T(1,128)S(1)}, u32[]{:S(2)}, u32[]{:S(2)}) collective-permute-start(f32[1,128]{1,0:T(1,128)S(1)} %add.146), channel_id=1, source_target_pairs={{0,2},{1,3},{2,0},{3,1},{4,6},{5,7},{6,4},{7,5},{8,10},{9,11},{10,... | collective-permute-start | bytes 1544 | tf_op jit(solution)/shard_map/ppermute | solution.py:11
  52.2 2.1 %collective-permute-done.16 = f32[1,128]{1,0:T(1,128)S(1)} collective-permute-done((f32[1,128]{1,0:T(1,128)S(1)}, f32[1,128]{1,0:T(1,128)S(1)}, u32[]{:S(2)}, u32[]{:S(2)}) %collective-permute-start.16) | collective-permute-done | bytes 544 | tf_op jit(solution)/shard_map/ppermute | solution.py:11
  54.3 0.6 %add_reduce_fusion = f32[]{:T(128)} fusion(f32[1,128]{1,0:T(1,128)S(1)} %add.146, f32[1,128]{1,0:T(1,128)S(1)} %collective-permute-done.16), kind=kLoop, calls=%fused_computation.41 | loop fusion | flops 255 | bytes 1028 | tf_op jit(solution)/shard_map/reduce_sum | solution.py:97
  55.6 0.0 collective-permute-done.15
  55.6 0.9 %fusion.1 = f32[1,128,1280]{2,1,0:T(8,128)} fusion(f32[1,128,256]{2,1,0:T(8,128)S(1)} %bitcast.63, f32[1,128,384]{2,1,0:T(8,128)S(1)} %bitcast.62, f32[1,128,640]{2,1,0:T(8,128)S(1)} %bitcast.70, f32[]{:T(128)S(6)} %sqrt.3, pred[]{:T(512)S(6)} %eq.12), kind=kLoop, calls=%fused_computation.6 | loop fusion | flops 983040 | bytes 1310725 | tf_op jit(solution)/shard_map/mul | solution.py:113
  (17 shorter events, 0.4 us)
Async XLA Ops:
  0.6 1.6 %copy-start = (bf16[1,768,1280]{2,1,0:T(8,128)(2,1)S(1)}, bf16[1,768,1280]{2,1,0:T(8,128)(2,1)}, u32[]{:S(2)}) copy-start(bf16[1,768,1280]{2,1,0:T(8,128)(2,1)} %param.5) | copy-start | bytes 5898244
  0.6 3.9 %copy-start.2 = (bf16[1,768,512]{2,1,0:T(8,128)(2,1)S(1)}, bf16[1,768,512]{2,1,0:T(8,128)(2,1)}, u32[]{:S(2)}) copy-start(bf16[1,768,512]{2,1,0:T(8,128)(2,1)} %param.4) | copy-start | bytes 2359300
  4.0 2.6 %collective-permute-start = (f32[512,384]{1,0:T(8,128)S(1)}, f32[512,384]{1,0:T(8,128)}, u32[]{:S(2)}, u32[]{:S(2)}) collective-permute-start(f32[512,384]{1,0:T(8,128)S(1)} %fusion.2), channel_id=1, source_target_pairs={{0,1},{1,0},{2,3},{3,2},{4,5},{5,4},{6,7},{7,6},{8,9},{9,8},{10,11... | collective-permute-start | bytes 2359304 | tf_op jit(solution)/shard_map/ppermute | solution.py:11
  5.9 5.5 %collective-permute-start.5 = (f32[512,256]{1,0:T(8,128)}, f32[512,256]{1,0:T(8,128)}, u32[]{:S(2)}, u32[]{:S(2)}) collective-permute-start(f32[512,256]{1,0:T(8,128)} %fusion.5), channel_id=1, source_target_pairs={{0,1},{1,0},{2,3},{3,2},{4,5},{5,4},{6,7},{7,6},{8,9},{9,8},{10,11... | collective-permute-start | bytes 1572872 | tf_op jit(solution)/shard_map/ppermute | solution.py:11
  8.4 8.9 %copy-start.1 = (bf16[1,512,1280]{2,1,0:T(8,128)(2,1)S(1)}, bf16[1,512,1280]{2,1,0:T(8,128)(2,1)}, u32[]{:S(2)}) copy-start(bf16[1,512,1280]{2,1,0:T(8,128)(2,1)} %param.6) | copy-start | bytes 3932164
  8.5 12.4 %collective-permute-start.1 = (f32[4,64,384]{2,1,0:T(8,128)S(1)}, f32[4,64,384]{2,1,0:T(8,128)S(1)}, u32[]{:S(2)}, u32[]{:S(2)}) collective-permute-start(f32[4,64,384]{2,1,0:T(8,128)S(1)} %dynamic-slice_bitcast_fusion), channel_id=1, source_target_pairs={{0,2},{1,3},{2,0},{3,1},{4,6},{5,7},{6,4},{7,5},{8,10},{9,11},{10,... | collective-permute-start | bytes 1179656 | tf_op jit(solution)/shard_map/ppermute | solution.py:11
  13.1 13.8 %collective-permute-start.6 = (f32[128,256]{1,0:T(8,128)S(1)}, f32[128,256]{1,0:T(8,128)S(1)}, u32[]{:S(2)}, u32[]{:S(2)}) collective-permute-start(f32[128,256]{1,0:T(8,128)S(1)} %get-tuple-element.18), channel_id=1, source_target_pairs={{0,8},{4,12},{8,0},{12,4},{1,9},{5,13},{9,1},{13,5},{2,10},{6,14},... | collective-permute-start | bytes 393224 | tf_op jit(solution)/shard_map/ppermute | solution.py:11
  15.8 11.2 %collective-permute-start.7 = (f32[128,256]{1,0:T(8,128)S(1)}, f32[128,256]{1,0:T(8,128)S(1)}, u32[]{:S(2)}, u32[]{:S(2)}) collective-permute-start(f32[128,256]{1,0:T(8,128)S(1)} %get-tuple-element.20), channel_id=1, source_target_pairs={{0,12},{4,8},{8,4},{12,0},{1,13},{5,9},{9,5},{13,1},{2,14},{6,10},... | collective-permute-start | bytes 393224 | tf_op jit(solution)/shard_map/ppermute | solution.py:11
  17.1 9.8 %collective-permute-start.8 = (f32[128,256]{1,0:T(8,128)S(1)}, f32[128,256]{1,0:T(8,128)S(1)}, u32[]{:S(2)}, u32[]{:S(2)}) collective-permute-start(f32[128,256]{1,0:T(8,128)S(1)} %get-tuple-element.19), channel_id=1, source_target_pairs={{0,4},{4,0},{8,12},{12,8},{1,5},{5,1},{9,13},{13,9},{2,6},{6,2},{1... | collective-permute-start | bytes 393224 | tf_op jit(solution)/shard_map/ppermute | solution.py:11
  20.9 14.2 %collective-permute-start.2 = (f32[64,384]{1,0:T(8,128)S(1)}, f32[64,384]{1,0:T(8,128)S(1)}, u32[]{:S(2)}, u32[]{:S(2)}) collective-permute-start(f32[64,384]{1,0:T(8,128)S(1)} %get-tuple-element.21), channel_id=1, source_target_pairs={{0,8},{4,12},{8,0},{12,4},{1,9},{5,13},{9,1},{13,5},{2,10},{6,14},... | collective-permute-start | bytes 294920 | tf_op jit(solution)/shard_map/ppermute | solution.py:11
  23.8 11.3 %collective-permute-start.3 = (f32[64,384]{1,0:T(8,128)S(1)}, f32[64,384]{1,0:T(8,128)S(1)}, u32[]{:S(2)}, u32[]{:S(2)}) collective-permute-start(f32[64,384]{1,0:T(8,128)S(1)} %get-tuple-element.23), channel_id=1, source_target_pairs={{0,12},{4,8},{8,4},{12,0},{1,13},{5,9},{9,5},{13,1},{2,14},{6,10},... | collective-permute-start | bytes 294920 | tf_op jit(solution)/shard_map/ppermute | solution.py:11
  26.9 8.3 %collective-permute-start.4 = (f32[64,384]{1,0:T(8,128)S(1)}, f32[64,384]{1,0:T(8,128)S(1)}, u32[]{:S(2)}, u32[]{:S(2)}) collective-permute-start(f32[64,384]{1,0:T(8,128)S(1)} %get-tuple-element.22), channel_id=1, source_target_pairs={{0,4},{4,0},{8,12},{12,8},{1,5},{5,1},{9,13},{13,9},{2,6},{6,2},{1... | collective-permute-start | bytes 294920 | tf_op jit(solution)/shard_map/ppermute | solution.py:11
  27.0 8.3 %collective-permute-start.9 = (f32[128,256]{1,0:T(8,128)S(1)}, f32[128,256]{1,0:T(8,128)S(1)}, u32[]{:S(2)}, u32[]{:S(2)}) collective-permute-start(f32[128,256]{1,0:T(8,128)S(1)} %fusion.9), channel_id=1, source_target_pairs={{0,2},{1,3},{2,0},{3,1},{4,6},{5,7},{6,4},{7,5},{8,10},{9,11},{10,... | collective-permute-start | bytes 393224 | tf_op jit(solution)/shard_map/ppermute | solution.py:11
  35.3 1.2 %collective-permute-start.10 = (f32[1,128]{1,0:T(1,128)S(1)}, f32[1,128]{1,0:T(1,128)S(1)}, u32[]{:S(2)}, u32[]{:S(2)}) collective-permute-start(f32[1,128]{1,0:T(1,128)S(1)} %fusion.17), channel_id=1, source_target_pairs={{0,1},{1,0},{2,3},{3,2},{4,5},{5,4},{6,7},{7,6},{8,9},{9,8},{10,11... | collective-permute-start | bytes 1544 | tf_op jit(solution)/shard_map/ppermute | solution.py:11
  36.5 14.0 %collective-permute-start.11 = (f32[1,64,384]{2,1,0:T(8,128)S(1)}, f32[1,64,384]{2,1,0:T(8,128)S(1)}, u32[]{:S(2)}, u32[]{:S(2)}) collective-permute-start(f32[1,64,384]{2,1,0:T(8,128)S(1)} %bitcast.68), channel_id=1, source_target_pairs={{0,2},{1,3},{2,0},{3,1},{4,6},{5,7},{6,4},{7,5},{8,10},{9,11},{10,... | collective-permute-start | bytes 294920 | tf_op jit(solution)/shard_map/ppermute | solution.py:11
  36.7 5.0 %collective-permute-start.12 = (f32[1,128]{1,0:T(1,128)S(1)}, f32[1,128]{1,0:T(1,128)S(1)}, u32[]{:S(2)}, u32[]{:S(2)}) collective-permute-start(f32[1,128]{1,0:T(1,128)S(1)} %add.143), channel_id=1, source_target_pairs={{0,4},{4,0},{8,12},{12,8},{1,5},{5,1},{9,13},{13,9},{2,6},{6,2},{1... | collective-permute-start | bytes 1544 | tf_op jit(solution)/shard_map/ppermute | solution.py:11
  41.7 5.3 %collective-permute-start.13 = (f32[1,128]{1,0:T(1,128)S(1)}, f32[1,128]{1,0:T(1,128)S(1)}, u32[]{:S(2)}, u32[]{:S(2)}) collective-permute-start(f32[1,128]{1,0:T(1,128)S(1)} %add.144), channel_id=1, source_target_pairs={{0,8},{4,12},{8,0},{12,4},{1,9},{5,13},{9,1},{13,5},{2,10},{6,14},... | collective-permute-start | bytes 1544 | tf_op jit(solution)/shard_map/ppermute | solution.py:11
  47.0 3.5 %collective-permute-start.14 = (f32[1,128]{1,0:T(1,128)S(1)}, f32[1,128]{1,0:T(1,128)S(1)}, u32[]{:S(2)}, u32[]{:S(2)}) collective-permute-start(f32[1,128]{1,0:T(1,128)S(1)} %add.145), channel_id=1, source_target_pairs={{0,16},{16,0},{1,17},{17,1},{2,18},{18,2},{3,19},{19,3},{4,20},{20... | collective-permute-start | bytes 1544 | tf_op jit(solution)/shard_map/ppermute | solution.py:11
  50.6 5.0 %collective-permute-start.15 = (f32[128,640]{1,0:T(8,128)S(1)}, f32[128,640]{1,0:T(8,128)S(1)}, u32[]{:S(2)}, u32[]{:S(2)}) collective-permute-start(f32[128,640]{1,0:T(8,128)S(1)} %pad_maximum_fusion), channel_id=1, source_target_pairs={{0,1},{1,0},{2,3},{3,2},{4,5},{5,4},{6,7},{7,6},{8,9},{9,8},{10,11... | collective-permute-start | bytes 983048 | tf_op jit(solution)/shard_map/ppermute | solution.py:11
  50.7 3.6 %collective-permute-start.16 = (f32[1,128]{1,0:T(1,128)S(1)}, f32[1,128]{1,0:T(1,128)S(1)}, u32[]{:S(2)}, u32[]{:S(2)}) collective-permute-start(f32[1,128]{1,0:T(1,128)S(1)} %add.146), channel_id=1, source_target_pairs={{0,2},{1,3},{2,0},{3,1},{4,6},{5,7},{6,4},{7,5},{8,10},{9,11},{10,... | collective-permute-start | bytes 1544 | tf_op jit(solution)/shard_map/ppermute | solution.py:11

commit v3 on v2

v3 whole, which is shorter than its diff:
```python
import jax
import jax.numpy as jnp
from jax import lax
from jax.experimental import pallas as pl
from jax.experimental.pallas import tpu as pltpu
from jax.sharding import PartitionSpec as P

CORES = 2
VMEM_BYTES = 12 * 2**20


def swap(x, axis, distance):
    size = lax.axis_size(axis)
    return lax.ppermute(x, axis, [(i, i ^ distance) for i in range(size)])


def doubled(size):
    distance = 1
    while distance < size:
        yield distance
        distance *= 2


def after(x, *ready):
    return lax.optimization_barrier((x, *ready))[0]


def piece(x, index):
    return lax.dynamic_index_in_dim(x, index, 0, keepdims=False)


def scatter_sum(x, axis, index, stride=1):
    size = x.shape[0]
    order = sorted(range(1, size), key=lambda d: -(d ^ 1))
    got = [swap(piece(x, index[d]), axis, d * stride) for d in order]
    total = piece(x, index[0])
    for part in got:
        total = total + part
    return total


def product(left, right):
    return lax.dot_general(
        left, right, (((0,), (0,)), ((), ())), preferred_element_type=jnp.float32
    )


def first_kernel(count, core, act, dy, out, masked, late, own, tokens, early, sems):
    half = own.shape[1]
    first = early.shape[1]
    other = pl.multiple_of((1 - core[0]) * half, 128)
    mine = pl.multiple_of(core[0] * half, 128)
    copies = [
        pltpu.make_async_copy(act, tokens, sems.at[0]),
        pltpu.make_async_copy(dy.at[:, pl.ds(other, first)], early, sems.at[1]),
        pltpu.make_async_copy(dy.at[:, pl.ds(other + first, half - first)], late, sems.at[2]),
        pltpu.make_async_copy(dy.at[:, pl.ds(mine, half)], own, sems.at[3]),
    ]
    for copy in copies:
        copy.start()
    copies[0].wait()
    live = lax.broadcasted_iota(jnp.int32, (act.shape[0], 1), 0) < count[0, 0, 0]
    masked[...] = jnp.where(live, tokens[...], jnp.zeros_like(tokens))
    copies[1].wait()
    out[...] = product(masked[...], early[...])
    copies[2].wait()
    copies[3].wait()


def first_term(counts, core, act, dy, half, first):
    rows, hidden = act.shape
    smem = pl.BlockSpec(memory_space=pltpu.SMEM)
    vmem = pl.BlockSpec(memory_space=pltpu.VMEM)
    hbm = pl.BlockSpec(memory_space=pltpu.HBM)
    return pl.pallas_call(
        first_kernel,
        out_shape=(
            jax.ShapeDtypeStruct((hidden, first), jnp.float32),
            jax.ShapeDtypeStruct((rows, hidden), act.dtype),
            jax.ShapeDtypeStruct((rows, half - first), dy.dtype),
            jax.ShapeDtypeStruct((rows, half), dy.dtype),
        ),
        in_specs=[smem, smem, hbm, hbm],
        out_specs=(vmem,) * 4,
        scratch_shapes=[
            pltpu.VMEM((rows, hidden), act.dtype),
            pltpu.VMEM((rows, first), dy.dtype),
            pltpu.SemaphoreType.DMA((4,)),
        ],
        compiler_params=pltpu.CompilerParams(vmem_limit_bytes=VMEM_BYTES),
    )(
        counts,
        core,
        pltpu.with_memory_space_constraint(act, pltpu.HBM),
        pltpu.with_memory_space_constraint(dy, pltpu.HBM),
    )


def terms_kernel(masked, columns, *outs):
    start = 0
    for out in outs:
        width = out.shape[1]
        out[...] = product(masked[...], columns[:, start : start + width])
        start += width


def terms(masked, columns, *widths):
    vmem = pl.BlockSpec(memory_space=pltpu.VMEM)
    hidden = masked.shape[1]
    return pl.pallas_call(
        terms_kernel,
        out_shape=tuple(jax.ShapeDtypeStruct((hidden, w), jnp.float32) for w in widths),
        in_specs=[vmem, vmem],
        out_specs=(vmem,) * len(widths),
        compiler_params=pltpu.CompilerParams(vmem_limit_bytes=VMEM_BYTES),
    )(masked, columns)


def on_device(act, dy, w_out, counts):
    tokens = act[0]
    upstream = dy[0]
    weight = w_out[0]
    rows, hidden = tokens.shape
    block = weight.shape[1]
    n_loop = lax.axis_size("loop")
    n_y = lax.axis_size("line") // CORES
    z = lax.axis_index("loop").astype(jnp.uint32)
    line = lax.axis_index("line").astype(jnp.uint32)
    y = line // CORES
    core, low_core, low_y, over_z, over_y, upper = lax.optimization_barrier(
        (
            (line % CORES).astype(jnp.int32).reshape(1),
            line % CORES == 0,
            y == 0,
            [z ^ d for d in range(n_loop)],
            [y ^ d for d in range(n_y)],
            [(y // d) % 2 == 1 for d in doubled(n_y)],
        )
    )
    own_rows = hidden // n_loop
    half = block // CORES
    first = half * 3 // 5 // 128 * 128

    live = lax.broadcasted_iota(jnp.int32, (rows, 1), 0) < counts[0, 0]
    entries = lax.axis_size("mod") * hidden * block

    early_other, masked, late_columns, own_columns = first_term(
        counts, core, tokens, upstream, half, first
    )
    early_other = swap(early_other, "line", 1)
    (late_other,) = terms(masked, late_columns, half - first)
    late_other = swap(late_other, "line", 1)
    early, late = terms(masked, own_columns, first, half - first)
    early = early + early_other
    late = late + late_other
    back = lax.dot_general(
        after(upstream, late), weight, (((1,), (1,)), ((), ())), preferred_element_type=jnp.float32
    )
    hidden_grad = jnp.where(live, back, jnp.zeros_like(back)).astype(jnp.bfloat16)

    early = early.reshape(n_loop, n_y, own_rows // n_y, first).transpose(1, 0, 2, 3)
    early = scatter_sum(early, "line", over_y, CORES)
    late = scatter_sum(late.reshape(n_loop, own_rows, half - first), "loop", over_z)
    early_part = early
    early = scatter_sum(early, "loop", over_z)
    late = after(late, early_part)
    for d in doubled(n_y):
        late = late + swap(late, "line", d * CORES)

    squares = jnp.sum(early * early, axis=0).reshape(-1, 128).sum(0)
    squares_late = jnp.sum(late * late, axis=0).reshape(-1, 128).sum(0)
    total = (squares + jnp.where(low_y, squares_late, 0.0)).reshape(1, 128)
    total = after(total, hidden_grad)
    for d in doubled(CORES):
        total = total + swap(total, "line", d)
    spread = total
    for d in doubled(n_loop):
        total = total + swap(total, "loop", d)
    for d in doubled(lax.axis_size("mod")):
        total = total + swap(total, "mod", d)
    over_towers = total
    for d in doubled(n_y):
        total = total + swap(total, "line", d * CORES)
    factor = 1.0 / jnp.sqrt(jnp.sum(total) / entries + 1e-06)

    early = after(early, spread)[None]
    for d, is_upper in zip(doubled(n_y), upper):
        other = after(swap(early, "line", d * CORES), over_towers)
        early = jnp.where(
            is_upper, jnp.concatenate([other, early]), jnp.concatenate([early, other])
        )
    mine = jnp.concatenate([early.reshape(own_rows, first), late], axis=1)
    other = swap(mine, "line", 1)
    share = jnp.where(
        low_core,
        jnp.concatenate([mine, other], axis=1),
        jnp.concatenate([other, mine], axis=1),
    )
    clipped = share * factor

    return (clipped[None], hidden_grad[None])


def solution(mesh):
    in_specs = (
        P("mod", ("loop", "line"), None),
        P("mod", ("loop", "line"), None),
        P("mod", None, None),
        P("mod", "loop", "line"),
    )
    out_specs = (P("mod", "loop", None), P("mod", ("loop", "line"), None))
    return jax.shard_map(
        on_device, mesh=mesh, in_specs=in_specs, out_specs=out_specs, check_vma=False
    )
```

time: 56.7 us -> 53 us (0.935)
  matrix products: 8.71 us -> 2.09 us
  Pallas kernels: 0 us -> 3.17 us
  starting transfers between devices: 22.7 us -> 24.5 us
  waiting for transfers between devices: 20.2 us -> 18.9 us
  local copies, waits for them, and re-layouts: 0.84 us -> 0.11 us
    dot_general x4 -> x0, matrix products: 6.62 us -> none  [term(): lax.dot_general(masked, columns, (((0,), (0,)), ((), ())), preferred_elem...]
    pallas_call x0 -> x3, Pallas kernels: none -> 3.17 us  [the longest x1 1.94 us: first_term(): pl.pallas_call(first_kernel, out_shape=(jax.ShapeDtypeStruct((hidden, fir...]
    ppermute x17, starting transfers between devices: 22.7 us -> 24.5 us  [swap(): return lax.ppermute(x, axis, [(i, i ^ distance) for i in range(size)])]
    ppermute x17, waiting for transfers between devices: 20.2 us -> 18.9 us  [swap(): return lax.ppermute(x, axis, [(i, i ^ distance) for i in range(size)])]
    unnamed x6 -> x4, local copies, waits for them, and re-layouts: 0.73 us -> 0.02 us
  transfers between devices with their start and end apart: 17 -> 17, of which waited for: 9 -> 8; matrix products, arithmetic and copies ran while one was open for 14% -> 6% of each run, Pallas kernels for 0% -> 2%
where the time goes in v3:
time: 53 us; the launch traced here: 52.9 us
  starting transfers between devices  24.5 us (46%)
  waiting for transfers between devices  18.9 us (36%)
  Pallas kernels  3.17 us (6%)
  between operations  2.23 us (4%)
  matrix products  2.09 us (4%)
  other arithmetic  1.92 us (4%)
    ppermute x17, starting transfers between devices, swap(): return lax.ppermute(x, axis, [(i, i ^ distance) for i in range(size)])  24.5 us
    ppermute x17, waiting for transfers between devices, swap(): return lax.ppermute(x, axis, [(i, i ^ distance) for i in range(size)])  18.9 us
    dot_general x1, matrix products, on_device(): lax.dot_general(after(upstream, late), weight, (((1,), (1,)), ((), ())),...  2.09 us
    pallas_call x1, Pallas kernels, first_term(): pl.pallas_call(first_kernel, out_shape=(jax.ShapeDtypeStruct((hidden, fir...  1.94 us
    pallas_call x2, Pallas kernels, terms(): pl.pallas_call(terms_kernel, out_shape=tuple((jax.ShapeDtypeStruct((hidde...  1.23 us
  transfers between devices with their start and end apart: 17, of which 8 were waited for; matrix products, arithmetic and copies ran while one was open for 6% of the time, Pallas kernels for 2%

profile of v3, /device:TPU:0, one launch (start us, length us, event | category | flops | bytes accessed | tf_op | source)
XLA Modules:
  0.0 52.9 jit_solution(145988011621426778)
XLA Ops:
  0.6 0.0 copy-start
  1.4 1.9 %shard_map.59 = (f32[512,384]{1,0:T(8,128)S(1)}, bf16[768,512]{1,0:T(8,128)(2,1)S(1)}, bf16[768,256]{1,0:T(8,128)(2,1)S(1)}, bf16[768,640]{1,0:T(8,128)(2,1)S(1)}) custom-call(s32[1,1,1]{2,1,0:T(1,128)} %copy.6.count, s32[1]{0:T(128)} %bitcast.core, bf16[768,512]{1,0:T(8,128)(2,1)} %bitcast.61, bf16[768,1280]{1,0:T(8,128)(2,1)} %bitcast.56), custom_call_target="tpu_custom_call" | custom-call | tf_op jit(solution)/shard_map/pallas_call | solution.py:75
  3.4 0.5 collective-permute-start
  3.9 0.4 shard_map.61
  4.3 0.1 collective-permute-start.5
  4.4 0.8 %shard_map.60 = (f32[512,384]{1,0:T(8,128)S(1)}, f32[512,256]{1,0:T(8,128)S(1)}) custom-call(bf16[768,512]{1,0:T(8,128)(2,1)S(1)} %get-tuple-element.26.masked, bf16[768,640]{1,0:T(8,128)(2,1)S(1)} %get-tuple-element.27.columns), custom_call_target="tpu_custom_call" | custom-call | tf_op jit(solution)/shard_map/pallas_call | solution.py:110
  5.2 1.3 %collective-permute-done.5 = f32[512,256]{1,0:T(8,128)S(1)} collective-permute-done((f32[512,256]{1,0:T(8,128)S(1)}, f32[512,256]{1,0:T(8,128)S(1)}, u32[]{:S(2)}, u32[]{:S(2)}) %collective-permute-start.5) | collective-permute-done | bytes 524320 | tf_op jit(solution)/shard_map/ppermute | solution.py:14
  6.5 0.1 add.70
  6.6 0.0 collective-permute-done
  6.6 0.0 copy-start.1
  6.6 0.1 add.65
  6.8 3.0 %collective-permute-start.1 = (f32[4,64,384]{2,1,0:T(8,128)S(1)}, f32[4,64,384]{2,1,0:T(8,128)S(1)}, u32[]{:S(2)}, u32[]{:S(2)}) collective-permute-start(f32[4,64,384]{2,1,0:T(8,128)S(1)} %dynamic-slice_bitcast_fusion), channel_id=1, source_target_pairs={{0,2},{1,3},{2,0},{3,1},{4,6},{5,7},{6,4},{7,5},{8,10},{9,11},{10,... | collective-permute-start | bytes 1179656 | tf_op jit(solution)/shard_map/ppermute | solution.py:14
  9.7 2.7 %collective-permute-start.6 = (f32[128,256]{1,0:T(8,128)S(1)}, f32[128,256]{1,0:T(8,128)S(1)}, u32[]{:S(2)}, u32[]{:S(2)}) collective-permute-start(f32[128,256]{1,0:T(8,128)S(1)} %get-tuple-element.48), channel_id=1, source_target_pairs={{0,8},{4,12},{8,0},{12,4},{1,9},{5,13},{9,1},{13,5},{2,10},{6,14},... | collective-permute-start | bytes 393224 | tf_op jit(solution)/shard_map/ppermute | solution.py:14
  12.4 1.3 %collective-permute-start.7 = (f32[128,256]{1,0:T(8,128)S(1)}, f32[128,256]{1,0:T(8,128)S(1)}, u32[]{:S(2)}, u32[]{:S(2)}) collective-permute-start(f32[128,256]{1,0:T(8,128)S(1)} %get-tuple-element.50), channel_id=1, source_target_pairs={{0,12},{4,8},{8,4},{12,0},{1,13},{5,9},{9,5},{13,1},{2,14},{6,10},... | collective-permute-start | bytes 393224 | tf_op jit(solution)/shard_map/ppermute | solution.py:14
  13.7 0.2 collective-permute-start.8
  14.0 0.0 copy-done
  14.0 0.0 copy-done.1
  14.0 2.1 %select_convert_fusion = bf16[768,512]{1,0:T(8,128)(2,1)} fusion(bf16[768,1280]{1,0:T(8,128)(2,1)S(1)} %bitcast.57, bf16[1,512,1280]{2,1,0:T(8,128)(2,1)S(1)} %copy-done, pred[768]{0:T(1024)(128)(4,1)S(1)} %iota_compare_fusion), kind=kOutput, calls=%fused_computation | convolution fusion | flops 1007419392 | bytes 4064000 | tf_op jit(solution)/shard_map/dot_general | solution.py:156
  16.1 3.0 %collective-permute-done.1 = f32[4,64,384]{2,1,0:T(8,128)S(1)} collective-permute-done((f32[4,64,384]{2,1,0:T(8,128)S(1)}, f32[4,64,384]{2,1,0:T(8,128)S(1)}, u32[]{:S(2)}, u32[]{:S(2)}) %collective-permute-start.1) | collective-permute-done | bytes 393248 | tf_op jit(solution)/shard_map/ppermute | solution.py:14
  19.2 2.9 %collective-permute-start.2 = (f32[64,384]{1,0:T(8,128)S(1)}, f32[64,384]{1,0:T(8,128)S(1)}, u32[]{:S(2)}, u32[]{:S(2)}) collective-permute-start(f32[64,384]{1,0:T(8,128)S(1)} %get-tuple-element.51), channel_id=1, source_target_pairs={{0,8},{4,12},{8,0},{12,4},{1,9},{5,13},{9,1},{13,5},{2,10},{6,14},... | collective-permute-start | bytes 294920 | tf_op jit(solution)/shard_map/ppermute | solution.py:14
  22.1 1.3 %collective-permute-start.3 = (f32[64,384]{1,0:T(8,128)S(1)}, f32[64,384]{1,0:T(8,128)S(1)}, u32[]{:S(2)}, u32[]{:S(2)}) collective-permute-start(f32[64,384]{1,0:T(8,128)S(1)} %get-tuple-element.53), channel_id=1, source_target_pairs={{0,12},{4,8},{8,4},{12,0},{1,13},{5,9},{9,5},{13,1},{2,14},{6,10},... | collective-permute-start | bytes 294920 | tf_op jit(solution)/shard_map/ppermute | solution.py:14
  23.4 0.0 collective-permute-done.6
  23.4 0.2 collective-permute-start.4
  23.7 0.0 collective-permute-done.7
  23.7 0.0 collective-permute-done.8
  23.7 1.6 %collective-permute-start.9 = (f32[128,256]{1,0:T(8,128)S(1)}, f32[128,256]{1,0:T(8,128)S(1)}, u32[]{:S(2)}, u32[]{:S(2)}) collective-permute-start(f32[128,256]{1,0:T(8,128)S(1)} %fusion.3), channel_id=1, source_target_pairs={{0,2},{1,3},{2,0},{3,1},{4,6},{5,7},{6,4},{7,5},{8,10},{9,11},{10,... | collective-permute-start | bytes 393224 | tf_op jit(solution)/shard_map/ppermute | solution.py:14
  25.3 6.5 %collective-permute-done.2 = f32[64,384]{1,0:T(8,128)S(1)} collective-permute-done((f32[64,384]{1,0:T(8,128)S(1)}, f32[64,384]{1,0:T(8,128)S(1)}, u32[]{:S(2)}, u32[]{:S(2)}) %collective-permute-start.2) | collective-permute-done | bytes 98336 | tf_op jit(solution)/shard_map/ppermute | solution.py:14
  31.8 0.0 collective-permute-done.3
  31.8 0.0 collective-permute-done.4
  31.9 0.0 collective-permute-done.9
  32.0 0.1 collective-permute-start.10
  32.0 1.1 %collective-permute-done.10 = f32[1,128]{1,0:T(1,128)S(1)} collective-permute-done((f32[1,128]{1,0:T(1,128)S(1)}, f32[1,128]{1,0:T(1,128)S(1)}, u32[]{:S(2)}, u32[]{:S(2)}) %collective-permute-start.10) | collective-permute-done | bytes 544 | tf_op jit(solution)/shard_map/ppermute | solution.py:14
  33.1 0.4 collective-permute-start.11
  33.5 3.2 %collective-permute-start.12 = (f32[1,128]{1,0:T(1,128)S(1)}, f32[1,128]{1,0:T(1,128)S(1)}, u32[]{:S(2)}, u32[]{:S(2)}) collective-permute-start(f32[1,128]{1,0:T(1,128)S(1)} %add.77), channel_id=1, source_target_pairs={{0,4},{4,0},{8,12},{12,8},{1,5},{5,1},{9,13},{13,9},{2,6},{6,2},{1... | collective-permute-start | bytes 1544 | tf_op jit(solution)/shard_map/ppermute | solution.py:14
  36.7 1.5 %collective-permute-done.12 = f32[1,128]{1,0:T(1,128)S(1)} collective-permute-done((f32[1,128]{1,0:T(1,128)S(1)}, f32[1,128]{1,0:T(1,128)S(1)}, u32[]{:S(2)}, u32[]{:S(2)}) %collective-permute-start.12) | collective-permute-done | bytes 544 | tf_op jit(solution)/shard_map/ppermute | solution.py:14
  38.2 3.7 %collective-permute-start.13 = (f32[1,128]{1,0:T(1,128)S(1)}, f32[1,128]{1,0:T(1,128)S(1)}, u32[]{:S(2)}, u32[]{:S(2)}) collective-permute-start(f32[1,128]{1,0:T(1,128)S(1)} %add.78), channel_id=1, source_target_pairs={{0,8},{4,12},{8,0},{12,4},{1,9},{5,13},{9,1},{13,5},{2,10},{6,14},... | collective-permute-start | bytes 1544 | tf_op jit(solution)/shard_map/ppermute | solution.py:14
  41.9 1.5 %collective-permute-done.13 = f32[1,128]{1,0:T(1,128)S(1)} collective-permute-done((f32[1,128]{1,0:T(1,128)S(1)}, f32[1,128]{1,0:T(1,128)S(1)}, u32[]{:S(2)}, u32[]{:S(2)}) %collective-permute-start.13) | collective-permute-done | bytes 544 | tf_op jit(solution)/shard_map/ppermute | solution.py:14
  43.4 1.5 %collective-permute-start.14 = (f32[1,128]{1,0:T(1,128)S(1)}, f32[1,128]{1,0:T(1,128)S(1)}, u32[]{:S(2)}, u32[]{:S(2)}) collective-permute-start(f32[1,128]{1,0:T(1,128)S(1)} %add.79), channel_id=1, source_target_pairs={{0,16},{16,0},{1,17},{17,1},{2,18},{18,2},{3,19},{19,3},{4,20},{20... | collective-permute-start | bytes 1544 | tf_op jit(solution)/shard_map/ppermute | solution.py:14
  44.9 2.1 %collective-permute-done.14 = f32[1,128]{1,0:T(1,128)S(1)} collective-permute-done((f32[1,128]{1,0:T(1,128)S(1)}, f32[1,128]{1,0:T(1,128)S(1)}, u32[]{:S(2)}, u32[]{:S(2)}) %collective-permute-start.14) | collective-permute-done | bytes 544 | tf_op jit(solution)/shard_map/ppermute | solution.py:14
  46.9 0.0 collective-permute-done.11
  47.0 0.1 collective-permute-start.15
  47.1 1.8 %collective-permute-start.16 = (f32[1,128]{1,0:T(1,128)S(1)}, f32[1,128]{1,0:T(1,128)S(1)}, u32[]{:S(2)}, u32[]{:S(2)}) collective-permute-start(f32[1,128]{1,0:T(1,128)S(1)} %add.80), channel_id=1, source_target_pairs={{0,2},{1,3},{2,0},{3,1},{4,6},{5,7},{6,4},{7,5},{8,10},{9,11},{10,... | collective-permute-start | bytes 1544 | tf_op jit(solution)/shard_map/ppermute | solution.py:14
  48.9 1.8 %collective-permute-done.16 = f32[1,128]{1,0:T(1,128)S(1)} collective-permute-done((f32[1,128]{1,0:T(1,128)S(1)}, f32[1,128]{1,0:T(1,128)S(1)}, u32[]{:S(2)}, u32[]{:S(2)}) %collective-permute-start.16) | collective-permute-done | bytes 544 | tf_op jit(solution)/shard_map/ppermute | solution.py:14
  50.7 0.6 %add_reduce_fusion = f32[]{:T(128)} fusion(f32[1,128]{1,0:T(1,128)S(1)} %add.80, f32[1,128]{1,0:T(1,128)S(1)} %collective-permute-done.16), kind=kLoop, calls=%fused_computation.28 | loop fusion | flops 255 | bytes 1028 | tf_op jit(solution)/shard_map/reduce_sum | solution.py:184
  52.0 0.0 collective-permute-done.15
  52.0 0.9 %fusion.1 = f32[1,128,1280]{2,1,0:T(8,128)} fusion(f32[1,128,640]{2,1,0:T(8,128)S(1)} %bitcast.64, f32[1,128,256]{2,1,0:T(8,128)S(1)} %bitcast.60, f32[1,128,384]{2,1,0:T(8,128)S(1)} %bitcast.59, f32[]{:T(128)S(6)} %sqrt.3, pred[]{:T(512)S(6)} %eq.13), kind=kLoop, calls=%fused_computation.3 | loop fusion | flops 983040 | bytes 1310725 | tf_op jit(solution)/shard_map/mul | solution.py:199
  (17 shorter events, 0.4 us)
Async XLA Ops:
  0.6 13.4 %copy-start = (bf16[1,512,1280]{2,1,0:T(8,128)(2,1)S(1)}, bf16[1,512,1280]{2,1,0:T(8,128)(2,1)}, u32[]{:S(2)}) copy-start(bf16[1,512,1280]{2,1,0:T(8,128)(2,1)} %param.6) | copy-start | bytes 3932164
  3.4 3.3 %collective-permute-start = (f32[512,384]{1,0:T(8,128)S(1)}, f32[512,384]{1,0:T(8,128)S(1)}, u32[]{:S(2)}, u32[]{:S(2)}) collective-permute-start(f32[512,384]{1,0:T(8,128)S(1)} %get-tuple-element.29), channel_id=1, source_target_pairs={{0,1},{1,0},{2,3},{3,2},{4,5},{5,4},{6,7},{7,6},{8,9},{9,8},{10,11... | collective-permute-start | bytes 2359304 | tf_op jit(solution)/shard_map/ppermute | solution.py:14
  4.3 2.2 %collective-permute-start.5 = (f32[512,256]{1,0:T(8,128)S(1)}, f32[512,256]{1,0:T(8,128)S(1)}, u32[]{:S(2)}, u32[]{:S(2)}) collective-permute-start(f32[512,256]{1,0:T(8,128)S(1)} %shard_map.61), channel_id=1, source_target_pairs={{0,1},{1,0},{2,3},{3,2},{4,5},{5,4},{6,7},{7,6},{8,9},{9,8},{10,11... | collective-permute-start | bytes 1572872 | tf_op jit(solution)/shard_map/ppermute | solution.py:14
  6.6 7.4 %copy-start.1 = (bf16[1,768,1280]{2,1,0:T(8,128)(2,1)S(1)}, bf16[1,768,1280]{2,1,0:T(8,128)(2,1)}, u32[]{:S(2)}) copy-start(bf16[1,768,1280]{2,1,0:T(8,128)(2,1)} %param.5) | copy-start | bytes 5898244
  6.8 12.4 %collective-permute-start.1 = (f32[4,64,384]{2,1,0:T(8,128)S(1)}, f32[4,64,384]{2,1,0:T(8,128)S(1)}, u32[]{:S(2)}, u32[]{:S(2)}) collective-permute-start(f32[4,64,384]{2,1,0:T(8,128)S(1)} %dynamic-slice_bitcast_fusion), channel_id=1, source_target_pairs={{0,2},{1,3},{2,0},{3,1},{4,6},{5,7},{6,4},{7,5},{8,10},{9,11},{10,... | collective-permute-start | bytes 1179656 | tf_op jit(solution)/shard_map/ppermute | solution.py:14
  9.7 13.7 %collective-permute-start.6 = (f32[128,256]{1,0:T(8,128)S(1)}, f32[128,256]{1,0:T(8,128)S(1)}, u32[]{:S(2)}, u32[]{:S(2)}) collective-permute-start(f32[128,256]{1,0:T(8,128)S(1)} %get-tuple-element.48), channel_id=1, source_target_pairs={{0,8},{4,12},{8,0},{12,4},{1,9},{5,13},{9,1},{13,5},{2,10},{6,14},... | collective-permute-start | bytes 393224 | tf_op jit(solution)/shard_map/ppermute | solution.py:14
  12.4 11.3 %collective-permute-start.7 = (f32[128,256]{1,0:T(8,128)S(1)}, f32[128,256]{1,0:T(8,128)S(1)}, u32[]{:S(2)}, u32[]{:S(2)}) collective-permute-start(f32[128,256]{1,0:T(8,128)S(1)} %get-tuple-element.50), channel_id=1, source_target_pairs={{0,12},{4,8},{8,4},{12,0},{1,13},{5,9},{9,5},{13,1},{2,14},{6,10},... | collective-permute-start | bytes 393224 | tf_op jit(solution)/shard_map/ppermute | solution.py:14
  13.7 9.9 %collective-permute-start.8 = (f32[128,256]{1,0:T(8,128)S(1)}, f32[128,256]{1,0:T(8,128)S(1)}, u32[]{:S(2)}, u32[]{:S(2)}) collective-permute-start(f32[128,256]{1,0:T(8,128)S(1)} %get-tuple-element.49), channel_id=1, source_target_pairs={{0,4},{4,0},{8,12},{12,8},{1,5},{5,1},{9,13},{13,9},{2,6},{6,2},{1... | collective-permute-start | bytes 393224 | tf_op jit(solution)/shard_map/ppermute | solution.py:14
  19.2 12.6 %collective-permute-start.2 = (f32[64,384]{1,0:T(8,128)S(1)}, f32[64,384]{1,0:T(8,128)S(1)}, u32[]{:S(2)}, u32[]{:S(2)}) collective-permute-start(f32[64,384]{1,0:T(8,128)S(1)} %get-tuple-element.51), channel_id=1, source_target_pairs={{0,8},{4,12},{8,0},{12,4},{1,9},{5,13},{9,1},{13,5},{2,10},{6,14},... | collective-permute-start | bytes 294920 | tf_op jit(solution)/shard_map/ppermute | solution.py:14
  22.1 9.7 %collective-permute-start.3 = (f32[64,384]{1,0:T(8,128)S(1)}, f32[64,384]{1,0:T(8,128)S(1)}, u32[]{:S(2)}, u32[]{:S(2)}) collective-permute-start(f32[64,384]{1,0:T(8,128)S(1)} %get-tuple-element.53), channel_id=1, source_target_pairs={{0,12},{4,8},{8,4},{12,0},{1,13},{5,9},{9,5},{13,1},{2,14},{6,10},... | collective-permute-start | bytes 294920 | tf_op jit(solution)/shard_map/ppermute | solution.py:14
  23.4 8.4 %collective-permute-start.4 = (f32[64,384]{1,0:T(8,128)S(1)}, f32[64,384]{1,0:T(8,128)S(1)}, u32[]{:S(2)}, u32[]{:S(2)}) collective-permute-start(f32[64,384]{1,0:T(8,128)S(1)} %get-tuple-element.52), channel_id=1, source_target_pairs={{0,4},{4,0},{8,12},{12,8},{1,5},{5,1},{9,13},{13,9},{2,6},{6,2},{1... | collective-permute-start | bytes 294920 | tf_op jit(solution)/shard_map/ppermute | solution.py:14
  23.7 8.2 %collective-permute-start.9 = (f32[128,256]{1,0:T(8,128)S(1)}, f32[128,256]{1,0:T(8,128)S(1)}, u32[]{:S(2)}, u32[]{:S(2)}) collective-permute-start(f32[128,256]{1,0:T(8,128)S(1)} %fusion.3), channel_id=1, source_target_pairs={{0,2},{1,3},{2,0},{3,1},{4,6},{5,7},{6,4},{7,5},{8,10},{9,11},{10,... | collective-permute-start | bytes 393224 | tf_op jit(solution)/shard_map/ppermute | solution.py:14
  32.0 1.2 %collective-permute-start.10 = (f32[1,128]{1,0:T(1,128)S(1)}, f32[1,128]{1,0:T(1,128)S(1)}, u32[]{:S(2)}, u32[]{:S(2)}) collective-permute-start(f32[1,128]{1,0:T(1,128)S(1)} %fusion.7), channel_id=1, source_target_pairs={{0,1},{1,0},{2,3},{3,2},{4,5},{5,4},{6,7},{7,6},{8,9},{9,8},{10,11... | collective-permute-start | bytes 1544 | tf_op jit(solution)/shard_map/ppermute | solution.py:14
  33.1 13.8 %collective-permute-start.11 = (f32[1,64,384]{2,1,0:T(8,128)S(1)}, f32[1,64,384]{2,1,0:T(8,128)S(1)}, u32[]{:S(2)}, u32[]{:S(2)}) collective-permute-start(f32[1,64,384]{2,1,0:T(8,128)S(1)} %bitcast.62), channel_id=1, source_target_pairs={{0,2},{1,3},{2,0},{3,1},{4,6},{5,7},{6,4},{7,5},{8,10},{9,11},{10,... | collective-permute-start | bytes 294920 | tf_op jit(solution)/shard_map/ppermute | solution.py:14
  33.5 4.7 %collective-permute-start.12 = (f32[1,128]{1,0:T(1,128)S(1)}, f32[1,128]{1,0:T(1,128)S(1)}, u32[]{:S(2)}, u32[]{:S(2)}) collective-permute-start(f32[1,128]{1,0:T(1,128)S(1)} %add.77), channel_id=1, source_target_pairs={{0,4},{4,0},{8,12},{12,8},{1,5},{5,1},{9,13},{13,9},{2,6},{6,2},{1... | collective-permute-start | bytes 1544 | tf_op jit(solution)/shard_map/ppermute | solution.py:14
  38.2 5.2 %collective-permute-start.13 = (f32[1,128]{1,0:T(1,128)S(1)}, f32[1,128]{1,0:T(1,128)S(1)}, u32[]{:S(2)}, u32[]{:S(2)}) collective-permute-start(f32[1,128]{1,0:T(1,128)S(1)} %add.78), channel_id=1, source_target_pairs={{0,8},{4,12},{8,0},{12,4},{1,9},{5,13},{9,1},{13,5},{2,10},{6,14},... | collective-permute-start | bytes 1544 | tf_op jit(solution)/shard_map/ppermute | solution.py:14
  43.4 3.5 %collective-permute-start.14 = (f32[1,128]{1,0:T(1,128)S(1)}, f32[1,128]{1,0:T(1,128)S(1)}, u32[]{:S(2)}, u32[]{:S(2)}) collective-permute-start(f32[1,128]{1,0:T(1,128)S(1)} %add.79), channel_id=1, source_target_pairs={{0,16},{16,0},{1,17},{17,1},{2,18},{18,2},{3,19},{19,3},{4,20},{20... | collective-permute-start | bytes 1544 | tf_op jit(solution)/shard_map/ppermute | solution.py:14
  47.0 5.0 %collective-permute-start.15 = (f32[128,640]{1,0:T(8,128)S(1)}, f32[128,640]{1,0:T(8,128)S(1)}, u32[]{:S(2)}, u32[]{:S(2)}) collective-permute-start(f32[128,640]{1,0:T(8,128)S(1)} %pad_maximum_fusion), channel_id=1, source_target_pairs={{0,1},{1,0},{2,3},{3,2},{4,5},{5,4},{6,7},{7,6},{8,9},{9,8},{10,11... | collective-permute-start | bytes 983048 | tf_op jit(solution)/shard_map/ppermute | solution.py:14
  47.1 3.6 %collective-permute-start.16 = (f32[1,128]{1,0:T(1,128)S(1)}, f32[1,128]{1,0:T(1,128)S(1)}, u32[]{:S(2)}, u32[]{:S(2)}) collective-permute-start(f32[1,128]{1,0:T(1,128)S(1)} %add.80), channel_id=1, source_target_pairs={{0,2},{1,3},{2,0},{3,1},{4,6},{5,7},{6,4},{7,5},{8,10},{9,11},{10,... | collective-permute-start | bytes 1544 | tf_op jit(solution)/shard_map/ppermute | solution.py:14

commit v4 on v3

--- a/solution.py
+++ b/solution.py
@@ -1,3 +1,5 @@
+import functools
+
 import jax
 import jax.numpy as jnp
 from jax import lax
@@ -45,11 +47,12 @@
     )
 
 
-def first_kernel(count, core, act, dy, out, masked, late, own, tokens, early, sems):
+def first_kernel(count, place, act, dy, out, masked, late, own, tokens, early, sems):
     half = own.shape[1]
     first = early.shape[1]
-    other = pl.multiple_of((1 - core[0]) * half, 128)
-    mine = pl.multiple_of(core[0] * half, 128)
+    core = place[0] % CORES
+    other = pl.multiple_of((1 - core) * half, 128)
+    mine = pl.multiple_of(core * half, 128)
     copies = [
         pltpu.make_async_copy(act, tokens, sems.at[0]),
         pltpu.make_async_copy(dy.at[:, pl.ds(other, first)], early, sems.at[1]),
@@ -67,7 +70,7 @@
     copies[3].wait()
 
 
-def first_term(counts, core, act, dy, half, first):
+def first_term(counts, place, act, dy, half, first):
     rows, hidden = act.shape
     smem = pl.BlockSpec(memory_space=pltpu.SMEM)
     vmem = pl.BlockSpec(memory_space=pltpu.VMEM)
@@ -90,7 +93,7 @@
         compiler_params=pltpu.CompilerParams(vmem_limit_bytes=VMEM_BYTES),
     )(
         counts,
-        core,
+        place,
         pltpu.with_memory_space_constraint(act, pltpu.HBM),
         pltpu.with_memory_space_constraint(dy, pltpu.HBM),
     )
@@ -114,6 +117,39 @@
         out_specs=(vmem,) * len(widths),
         compiler_params=pltpu.CompilerParams(vmem_limit_bytes=VMEM_BYTES),
     )(masked, columns)
+
+
+def scaled_kernel(entries, place, totals, *refs):
+    *pieces, out, ordered = refs
+    rows, block = out.shape
+    half = block // CORES
+    first = pieces[0].shape[1]
+    lates, earlies = pieces[-CORES:], pieces[:-CORES]
+    factor = 1.0 / jnp.sqrt(jnp.sum(totals[...]) / entries + 1e-06)
+    height = rows // (len(earlies) // CORES)
+    for d, piece in enumerate(earlies):
+        ordered[place[0] ^ d] = piece[...] * factor
+    for member in range(len(earlies)):
+        row, column = member // CORES * height, member % CORES * half
+        out[row : row + height, column : column + first] = ordered[member]
+    for d, piece in enumerate(lates):
+        column = pl.multiple_of((place[0] ^ d) % CORES * half + first, 128)
+        out[:, pl.ds(column, half - first)] = piece[...] * factor
+
+
+def scaled(place, totals, early, late, entries):
+    smem = pl.BlockSpec(memory_space=pltpu.SMEM)
+    vmem = pl.BlockSpec(memory_space=pltpu.VMEM)
+    rows = late[0].shape[0]
+    block = CORES * (early[0].shape[1] + late[0].shape[1])
+    return pl.pallas_call(
+        functools.partial(scaled_kernel, entries),
+        out_shape=jax.ShapeDtypeStruct((rows, block), jnp.float32),
+        in_specs=[smem] + [vmem] * (1 + len(early) + len(late)),
+        out_specs=vmem,
+        scratch_shapes=[pltpu.VMEM((len(early), *early[0].shape), jnp.float32)],
+        compiler_params=pltpu.CompilerParams(vmem_limit_bytes=VMEM_BYTES),
+    )(place, totals.reshape(-1, 128), *early, *late)
 
 
 def on_device(act, dy, w_out, counts):
@@ -127,14 +163,12 @@
     z = lax.axis_index("loop").astype(jnp.uint32)
     line = lax.axis_index("line").astype(jnp.uint32)
     y = line // CORES
-    core, low_core, low_y, over_z, over_y, upper = lax.optimization_barrier(
+    place, low_y, over_z, over_y = lax.optimization_barrier(
         (
-            (line % CORES).astype(jnp.int32).reshape(1),
-            line % CORES == 0,
+            line.astype(jnp.int32).reshape(1),
             y == 0,
             [z ^ d for d in range(n_loop)],
             [y ^ d for d in range(n_y)],
-            [(y // d) % 2 == 1 for d in doubled(n_y)],
         )
     )
     own_rows = hidden // n_loop
@@ -145,14 +179,14 @@
     entries = lax.axis_size("mod") * hidden * block
 
     early_other, masked, late_columns, own_columns = first_term(
-        counts, core, tokens, upstream, half, first
+        counts, place, tokens, upstream, half, first
     )
     early_other = swap(early_other, "line", 1)
     (late_other,) = terms(masked, late_columns, half - first)
     late_other = swap(late_other, "line", 1)
     early, late = terms(masked, own_columns, first, half - first)
     early = early + early_other
-    late = late + late_other
+    late = late + after(late_other, early)
     back = lax.dot_general(
         after(upstream, late), weight, (((1,), (1,)), ((), ())), preferred_element_type=jnp.float32
     )
@@ -171,33 +205,14 @@
     squares_late = jnp.sum(late * late, axis=0).reshape(-1, 128).sum(0)
     total = (squares + jnp.where(low_y, squares_late, 0.0)).reshape(1, 128)
     total = after(total, hidden_grad)
-    for d in doubled(CORES):
-        total = total + swap(total, "line", d)
-    spread = total
-    for d in doubled(n_loop):
-        total = total + swap(total, "loop", d)
-    for d in doubled(lax.axis_size("mod")):
-        total = total + swap(total, "mod", d)
-    over_towers = total
-    for d in doubled(n_y):
-        total = total + swap(total, "line", d * CORES)
-    factor = 1.0 / jnp.sqrt(jnp.sum(total) / entries + 1e-06)
-
-    early = after(early, spread)[None]
-    for d, is_upper in zip(doubled(n_y), upper):
-        other = after(swap(early, "line", d * CORES), over_towers)
-        early = jnp.where(
-            is_upper, jnp.concatenate([other, early]), jnp.concatenate([early, other])
-        )
-    mine = jnp.concatenate([early.reshape(own_rows, first), late], axis=1)
-    other = swap(mine, "line", 1)
-    share = jnp.where(
-        low_core,
-        jnp.concatenate([mine, other], axis=1),
-        jnp.concatenate([other, mine], axis=1),
-    )
-    clipped = share * factor
-
+    everyone = ("mod", "loop", "line")
+    members = lax.axis_size(everyone)
+    early = [early] + [swap(early, "line", d) for d in range(1, n_y * CORES)]
+    late = [late] + [swap(late, "line", d) for d in range(1, CORES)]
+    totals = lax.all_to_all(
+        jnp.broadcast_to(total[None], (members, 1, 128)), everyone, 0, 0, tiled=True
+    )
+    clipped = scaled(place, totals, early, late, entries)
     return (clipped[None], hidden_grad[None])
 
 

time: 53 us -> 47.4 us (0.89)
  blocking collectives: 0 us -> 11.9 us
  starting transfers between devices: 24.5 us -> 16.2 us
  waiting for transfers between devices: 18.9 us -> 10.8 us
  other arithmetic: 1.92 us -> 0.36 us
  Pallas kernels: 3.17 us -> 4.29 us
  between operations: 2.23 us -> 1.49 us
    all_to_all x0 -> x1, blocking collectives: none -> 11.9 us  [on_device(): lax.all_to_all(jnp.broadcast_to(total[None], (members, 1, 128)), everyone...]
    ppermute x17 -> x14, starting transfers between devices: 24.5 us -> 16.2 us  [swap(): return lax.ppermute(x, axis, [(i, i ^ distance) for i in range(size)])]
    ppermute x17 -> x14, waiting for transfers between devices: 18.9 us -> 10.8 us  [swap(): return lax.ppermute(x, axis, [(i, i ^ distance) for i in range(size)])]
    pallas_call x0 -> x1, Pallas kernels: none -> 1.12 us  [scaled(): pl.pallas_call(functools.partial(scaled_kernel, entries), out_shape=jax.S...]
    mul x1 -> x0, other arithmetic: 0.91 us -> none  [on_device(): clipped = share * factor]
    reduce_sum x1 -> x0, other arithmetic: 0.6 us -> none  [on_device(): factor = 1.0 / jnp.sqrt(jnp.sum(total) / entries + 1e-06)]
  transfers between devices with their start and end apart: 17 -> 14, of which waited for: 8 -> 4; matrix products, arithmetic and copies ran while one was open for 6% -> 5% of each run, Pallas kernels for 2% -> 3%
where the time goes in v4:
time: 47.4 us; the launch traced here: 47.2 us
  starting transfers between devices  16.2 us (34%)
  blocking collectives  11.9 us (25%)
  waiting for transfers between devices  10.8 us (23%)
  Pallas kernels  4.29 us (9%)
  matrix products  2.09 us (4%)
  between operations  1.49 us (3%)
    ppermute x14, starting transfers between devices, swap(): return lax.ppermute(x, axis, [(i, i ^ distance) for i in range(size)])  16.2 us
    all_to_all x1, blocking collectives, on_device(): lax.all_to_all(jnp.broadcast_to(total[None], (members, 1, 128)), everyone...  11.9 us
    ppermute x14, waiting for transfers between devices, swap(): return lax.ppermute(x, axis, [(i, i ^ distance) for i in range(size)])  10.8 us
    dot_general x1, matrix products, on_device(): lax.dot_general(after(upstream, late), weight, (((1,), (1,)), ((), ())),...  2.09 us
    pallas_call x1, Pallas kernels, first_term(): pl.pallas_call(first_kernel, out_shape=(jax.ShapeDtypeStruct((hidden, fir...  1.95 us
    pallas_call x2, Pallas kernels, terms(): pl.pallas_call(terms_kernel, out_shape=tuple((jax.ShapeDtypeStruct((hidde...  1.23 us
    pallas_call x1, Pallas kernels, scaled(): pl.pallas_call(functools.partial(scaled_kernel, entries), out_shape=jax.S...  1.12 us
  transfers between devices with their start and end apart: 14, of which 4 were waited for; matrix products, arithmetic and copies ran while one was open for 5% of the time, Pallas kernels for 3%

profile of v4, /device:TPU:0, one launch (start us, length us, event | category | flops | bytes accessed | tf_op | source)
XLA Modules:
  0.0 47.2 jit_solution(887889602048397317)
XLA Ops:
  0.6 0.0 copy-start
  1.4 1.9 %shard_map.59 = (f32[512,384]{1,0:T(8,128)S(1)}, bf16[768,512]{1,0:T(8,128)(2,1)S(1)}, bf16[768,256]{1,0:T(8,128)(2,1)S(1)}, bf16[768,640]{1,0:T(8,128)(2,1)S(1)}) custom-call(s32[1,1,1]{2,1,0:T(1,128)} %copy.6.count, s32[1]{0:T(128)} %bitcast.place, bf16[768,512]{1,0:T(8,128)(2,1)} %bitcast.57, bf16[768,1280]{1,0:T(8,128)(2,1)} %bitcast.55), custom_call_target="tpu_custom_call" | custom-call | tf_op jit(solution)/shard_map/pallas_call | solution.py:78
  3.4 0.5 %collective-permute-start = (f32[512,384]{1,0:T(8,128)S(1)}, f32[512,384]{1,0:T(8,128)S(1)}, u32[]{:S(2)}, u32[]{:S(2)}) collective-permute-start(f32[512,384]{1,0:T(8,128)S(1)} %get-tuple-element.24), channel_id=1, source_target_pairs={{0,1},{1,0},{2,3},{3,2},{4,5},{5,4},{6,7},{7,6},{8,9},{9,8},{10,11... | collective-permute-start | bytes 2359304 | tf_op jit(solution)/shard_map/ppermute | solution.py:16
  3.9 0.4 shard_map.61
  4.3 0.1 collective-permute-start.5
  4.4 0.8 %shard_map.60 = (f32[512,384]{1,0:T(8,128)S(1)}, f32[512,256]{1,0:T(8,128)S(1)}) custom-call(bf16[768,512]{1,0:T(8,128)(2,1)S(1)} %get-tuple-element.21.masked, bf16[768,640]{1,0:T(8,128)(2,1)S(1)} %get-tuple-element.22.columns), custom_call_target="tpu_custom_call" | custom-call | tf_op jit(solution)/shard_map/pallas_call | solution.py:113
  5.2 0.5 %collective-permute-done = f32[512,384]{1,0:T(8,128)S(1)} collective-permute-done((f32[512,384]{1,0:T(8,128)S(1)}, f32[512,384]{1,0:T(8,128)S(1)}, u32[]{:S(2)}, u32[]{:S(2)}) %collective-permute-start) | collective-permute-done | bytes 786464 | tf_op jit(solution)/shard_map/ppermute | solution.py:16
  5.8 0.1 add.43
  5.9 0.7 %collective-permute-done.5 = f32[512,256]{1,0:T(8,128)S(1)} collective-permute-done((f32[512,256]{1,0:T(8,128)S(1)}, f32[512,256]{1,0:T(8,128)S(1)}, u32[]{:S(2)}, u32[]{:S(2)}) %collective-permute-start.5) | collective-permute-done | bytes 524320 | tf_op jit(solution)/shard_map/ppermute | solution.py:16
  6.5 0.0 copy-start.1
  6.6 3.0 %collective-permute-start.1 = (f32[4,64,384]{2,1,0:T(8,128)S(1)}, f32[4,64,384]{2,1,0:T(8,128)S(1)}, u32[]{:S(2)}, u32[]{:S(2)}) collective-permute-start(f32[4,64,384]{2,1,0:T(8,128)S(1)} %dynamic-slice_bitcast_fusion), channel_id=1, source_target_pairs={{0,2},{1,3},{2,0},{3,1},{4,6},{5,7},{6,4},{7,5},{8,10},{9,11},{10,... | collective-permute-start | bytes 1179656 | tf_op jit(solution)/shard_map/ppermute | solution.py:16
  9.5 0.1 add.48
  9.6 2.7 %collective-permute-start.6 = (f32[128,256]{1,0:T(8,128)S(1)}, f32[128,256]{1,0:T(8,128)S(1)}, u32[]{:S(2)}, u32[]{:S(2)}) collective-permute-start(f32[128,256]{1,0:T(8,128)S(1)} %get-tuple-element.42), channel_id=1, source_target_pairs={{0,8},{4,12},{8,0},{12,4},{1,9},{5,13},{9,1},{13,5},{2,10},{6,14},... | collective-permute-start | bytes 393224 | tf_op jit(solution)/shard_map/ppermute | solution.py:16
  12.3 1.3 %collective-permute-start.7 = (f32[128,256]{1,0:T(8,128)S(1)}, f32[128,256]{1,0:T(8,128)S(1)}, u32[]{:S(2)}, u32[]{:S(2)}) collective-permute-start(f32[128,256]{1,0:T(8,128)S(1)} %get-tuple-element.44), channel_id=1, source_target_pairs={{0,12},{4,8},{8,4},{12,0},{1,13},{5,9},{9,5},{13,1},{2,14},{6,10},... | collective-permute-start | bytes 393224 | tf_op jit(solution)/shard_map/ppermute | solution.py:16
  13.6 0.2 collective-permute-start.8
  13.9 0.0 copy-done
  13.9 0.0 copy-done.1
  13.9 2.1 %select_convert_fusion = bf16[768,512]{1,0:T(8,128)(2,1)} fusion(bf16[768,1280]{1,0:T(8,128)(2,1)S(1)} %bitcast.56, bf16[1,512,1280]{2,1,0:T(8,128)(2,1)S(1)} %copy-done, pred[768]{0:T(1024)(128)(4,1)S(1)} %iota_compare_fusion), kind=kOutput, calls=%fused_computation | convolution fusion | flops 1007419392 | bytes 4064000 | tf_op jit(solution)/shard_map/dot_general | solution.py:190
  16.0 3.0 %collective-permute-done.1 = f32[4,64,384]{2,1,0:T(8,128)S(1)} collective-permute-done((f32[4,64,384]{2,1,0:T(8,128)S(1)}, f32[4,64,384]{2,1,0:T(8,128)S(1)}, u32[]{:S(2)}, u32[]{:S(2)}) %collective-permute-start.1) | collective-permute-done | bytes 393248 | tf_op jit(solution)/shard_map/ppermute | solution.py:16
  19.0 2.9 %collective-permute-start.2 = (f32[64,384]{1,0:T(8,128)S(1)}, f32[64,384]{1,0:T(8,128)S(1)}, u32[]{:S(2)}, u32[]{:S(2)}) collective-permute-start(f32[64,384]{1,0:T(8,128)S(1)} %get-tuple-element.45), channel_id=1, source_target_pairs={{0,8},{4,12},{8,0},{12,4},{1,9},{5,13},{9,1},{13,5},{2,10},{6,14},... | collective-permute-start | bytes 294920 | tf_op jit(solution)/shard_map/ppermute | solution.py:16
  21.9 1.3 %collective-permute-start.3 = (f32[64,384]{1,0:T(8,128)S(1)}, f32[64,384]{1,0:T(8,128)S(1)}, u32[]{:S(2)}, u32[]{:S(2)}) collective-permute-start(f32[64,384]{1,0:T(8,128)S(1)} %get-tuple-element.47), channel_id=1, source_target_pairs={{0,12},{4,8},{8,4},{12,0},{1,13},{5,9},{9,5},{13,1},{2,14},{6,10},... | collective-permute-start | bytes 294920 | tf_op jit(solution)/shard_map/ppermute | solution.py:16
  23.2 0.0 collective-permute-done.6
  23.3 0.2 collective-permute-start.4
  23.5 0.0 collective-permute-done.7
  23.5 0.0 collective-permute-done.8
  23.5 1.6 %collective-permute-start.9 = (f32[128,256]{1,0:T(8,128)S(1)}, f32[128,256]{1,0:T(8,128)S(1)}, u32[]{:S(2)}, u32[]{:S(2)}) collective-permute-start(f32[128,256]{1,0:T(8,128)S(1)} %fusion.2), channel_id=1, source_target_pairs={{0,2},{1,3},{2,0},{3,1},{4,6},{5,7},{6,4},{7,5},{8,10},{9,11},{10,... | collective-permute-start | bytes 393224 | tf_op jit(solution)/shard_map/ppermute | solution.py:16
  25.1 6.6 %collective-permute-done.2 = f32[64,384]{1,0:T(8,128)S(1)} collective-permute-done((f32[64,384]{1,0:T(8,128)S(1)}, f32[64,384]{1,0:T(8,128)S(1)}, u32[]{:S(2)}, u32[]{:S(2)}) %collective-permute-start.2) | collective-permute-done | bytes 98336 | tf_op jit(solution)/shard_map/ppermute | solution.py:16
  31.7 0.0 collective-permute-done.3
  31.7 0.0 collective-permute-done.4
  31.8 0.1 collective-permute-start.10
  31.8 0.4 collective-permute-start.11
  32.2 1.5 %collective-permute-start.12 = (f32[64,384]{1,0:T(8,128)S(1)}, f32[64,384]{1,0:T(8,128)S(1)}, u32[]{:S(2)}, u32[]{:S(2)}) collective-permute-start(f32[64,384]{1,0:T(8,128)S(1)} %get-tuple-element.41.refs_0_), channel_id=1, source_target_pairs={{0,3},{1,2},{2,1},{3,0},{4,7},{5,6},{6,5},{7,4},{8,11},{9,10},{10,... | collective-permute-start | bytes 294920 | tf_op jit(solution)/shard_map/ppermute | solution.py:16
  33.7 0.0 collective-permute-done.9
  33.8 0.4 collective-permute-start.13
  34.2 11.9 %all_to_all.5 = f32[32,1,128]{2,1,0:T(1,128)S(1)} all-to-all(f32[32,1,128]{2,1,0:T(1,128)S(1)} %broadcast_in_dim.33), channel_id=1, replica_groups=mesh['mod'=2,'loop'=4,'line'=4] {'mod','loop','line'}, dimensions={0} | all-to-all | bytes 32768 | tf_op jit(solution)/shard_map/all_to_all | solution.py:212
  46.1 0.0 collective-permute-done.10.refs_1_
  46.1 0.0 collective-permute-done.11.refs_2_
  46.1 0.0 collective-permute-done.12.refs_3_
  46.1 0.0 collective-permute-done.13.refs_5_
  46.1 1.1 %shard_map.62 = f32[128,1280]{1,0:T(8,128)} custom-call(s32[1]{0:T(128)} %bitcast.place, f32[32,128]{1,0:T(8,128)S(1)} %bitcast.50, f32[64,384]{1,0:T(8,128)S(1)} %get-tuple-element.41.refs_0_, f32[64,384]{1,0:T(8,128)S(1)} %collective-permute-done.10.refs_1_, f32[64,384]{1,0:T(8,128)S(1)} %collective-permute-done.11.refs_2_, ...), custom_call_target="tpu_custom_call" | custom-call | tf_op jit(solution)/shard_map/pallas_call | solution.py:145
  (12 shorter events, 0.3 us)
Async XLA Ops:
  0.6 13.2 %copy-start = (bf16[1,512,1280]{2,1,0:T(8,128)(2,1)S(1)}, bf16[1,512,1280]{2,1,0:T(8,128)(2,1)}, u32[]{:S(2)}) copy-start(bf16[1,512,1280]{2,1,0:T(8,128)(2,1)} %param.6) | copy-start | bytes 3932164
  3.4 2.4 %collective-permute-start = (f32[512,384]{1,0:T(8,128)S(1)}, f32[512,384]{1,0:T(8,128)S(1)}, u32[]{:S(2)}, u32[]{:S(2)}) collective-permute-start(f32[512,384]{1,0:T(8,128)S(1)} %get-tuple-element.24), channel_id=1, source_target_pairs={{0,1},{1,0},{2,3},{3,2},{4,5},{5,4},{6,7},{7,6},{8,9},{9,8},{10,11... | collective-permute-start | bytes 2359304 | tf_op jit(solution)/shard_map/ppermute | solution.py:16
  4.3 2.2 %collective-permute-start.5 = (f32[512,256]{1,0:T(8,128)S(1)}, f32[512,256]{1,0:T(8,128)S(1)}, u32[]{:S(2)}, u32[]{:S(2)}) collective-permute-start(f32[512,256]{1,0:T(8,128)S(1)} %shard_map.61), channel_id=1, source_target_pairs={{0,1},{1,0},{2,3},{3,2},{4,5},{5,4},{6,7},{7,6},{8,9},{9,8},{10,11... | collective-permute-start | bytes 1572872 | tf_op jit(solution)/shard_map/ppermute | solution.py:16
  6.5 7.3 %copy-start.1 = (bf16[1,768,1280]{2,1,0:T(8,128)(2,1)S(1)}, bf16[1,768,1280]{2,1,0:T(8,128)(2,1)}, u32[]{:S(2)}) copy-start(bf16[1,768,1280]{2,1,0:T(8,128)(2,1)} %param.5) | copy-start | bytes 5898244
  6.6 12.4 %collective-permute-start.1 = (f32[4,64,384]{2,1,0:T(8,128)S(1)}, f32[4,64,384]{2,1,0:T(8,128)S(1)}, u32[]{:S(2)}, u32[]{:S(2)}) collective-permute-start(f32[4,64,384]{2,1,0:T(8,128)S(1)} %dynamic-slice_bitcast_fusion), channel_id=1, source_target_pairs={{0,2},{1,3},{2,0},{3,1},{4,6},{5,7},{6,4},{7,5},{8,10},{9,11},{10,... | collective-permute-start | bytes 1179656 | tf_op jit(solution)/shard_map/ppermute | solution.py:16
  9.6 13.6 %collective-permute-start.6 = (f32[128,256]{1,0:T(8,128)S(1)}, f32[128,256]{1,0:T(8,128)S(1)}, u32[]{:S(2)}, u32[]{:S(2)}) collective-permute-start(f32[128,256]{1,0:T(8,128)S(1)} %get-tuple-element.42), channel_id=1, source_target_pairs={{0,8},{4,12},{8,0},{12,4},{1,9},{5,13},{9,1},{13,5},{2,10},{6,14},... | collective-permute-start | bytes 393224 | tf_op jit(solution)/shard_map/ppermute | solution.py:16
  12.3 11.2 %collective-permute-start.7 = (f32[128,256]{1,0:T(8,128)S(1)}, f32[128,256]{1,0:T(8,128)S(1)}, u32[]{:S(2)}, u32[]{:S(2)}) collective-permute-start(f32[128,256]{1,0:T(8,128)S(1)} %get-tuple-element.44), channel_id=1, source_target_pairs={{0,12},{4,8},{8,4},{12,0},{1,13},{5,9},{9,5},{13,1},{2,14},{6,10},... | collective-permute-start | bytes 393224 | tf_op jit(solution)/shard_map/ppermute | solution.py:16
  13.6 9.8 %collective-permute-start.8 = (f32[128,256]{1,0:T(8,128)S(1)}, f32[128,256]{1,0:T(8,128)S(1)}, u32[]{:S(2)}, u32[]{:S(2)}) collective-permute-start(f32[128,256]{1,0:T(8,128)S(1)} %get-tuple-element.43), channel_id=1, source_target_pairs={{0,4},{4,0},{8,12},{12,8},{1,5},{5,1},{9,13},{13,9},{2,6},{6,2},{1... | collective-permute-start | bytes 393224 | tf_op jit(solution)/shard_map/ppermute | solution.py:16
  19.0 12.7 %collective-permute-start.2 = (f32[64,384]{1,0:T(8,128)S(1)}, f32[64,384]{1,0:T(8,128)S(1)}, u32[]{:S(2)}, u32[]{:S(2)}) collective-permute-start(f32[64,384]{1,0:T(8,128)S(1)} %get-tuple-element.45), channel_id=1, source_target_pairs={{0,8},{4,12},{8,0},{12,4},{1,9},{5,13},{9,1},{13,5},{2,10},{6,14},... | collective-permute-start | bytes 294920 | tf_op jit(solution)/shard_map/ppermute | solution.py:16
  21.9 9.8 %collective-permute-start.3 = (f32[64,384]{1,0:T(8,128)S(1)}, f32[64,384]{1,0:T(8,128)S(1)}, u32[]{:S(2)}, u32[]{:S(2)}) collective-permute-start(f32[64,384]{1,0:T(8,128)S(1)} %get-tuple-element.47), channel_id=1, source_target_pairs={{0,12},{4,8},{8,4},{12,0},{1,13},{5,9},{9,5},{13,1},{2,14},{6,10},... | collective-permute-start | bytes 294920 | tf_op jit(solution)/shard_map/ppermute | solution.py:16
  23.3 8.5 %collective-permute-start.4 = (f32[64,384]{1,0:T(8,128)S(1)}, f32[64,384]{1,0:T(8,128)S(1)}, u32[]{:S(2)}, u32[]{:S(2)}) collective-permute-start(f32[64,384]{1,0:T(8,128)S(1)} %get-tuple-element.46), channel_id=1, source_target_pairs={{0,4},{4,0},{8,12},{12,8},{1,5},{5,1},{9,13},{13,9},{2,6},{6,2},{1... | collective-permute-start | bytes 294920 | tf_op jit(solution)/shard_map/ppermute | solution.py:16
  23.5 10.2 %collective-permute-start.9 = (f32[128,256]{1,0:T(8,128)S(1)}, f32[128,256]{1,0:T(8,128)S(1)}, u32[]{:S(2)}, u32[]{:S(2)}) collective-permute-start(f32[128,256]{1,0:T(8,128)S(1)} %fusion.2), channel_id=1, source_target_pairs={{0,2},{1,3},{2,0},{3,1},{4,6},{5,7},{6,4},{7,5},{8,10},{9,11},{10,... | collective-permute-start | bytes 393224 | tf_op jit(solution)/shard_map/ppermute | solution.py:16
  31.8 14.3 %collective-permute-start.10 = (f32[64,384]{1,0:T(8,128)S(1)}, f32[64,384]{1,0:T(8,128)S(1)}, u32[]{:S(2)}, u32[]{:S(2)}) collective-permute-start(f32[64,384]{1,0:T(8,128)S(1)} %get-tuple-element.41.refs_0_), channel_id=1, source_target_pairs={{0,1},{1,0},{2,3},{3,2},{4,5},{5,4},{6,7},{7,6},{8,9},{9,8},{10,11... | collective-permute-start | bytes 294920 | tf_op jit(solution)/shard_map/ppermute | solution.py:16
  31.8 14.2 %collective-permute-start.11 = (f32[64,384]{1,0:T(8,128)S(1)}, f32[64,384]{1,0:T(8,128)S(1)}, u32[]{:S(2)}, u32[]{:S(2)}) collective-permute-start(f32[64,384]{1,0:T(8,128)S(1)} %get-tuple-element.41.refs_0_), channel_id=1, source_target_pairs={{0,2},{1,3},{2,0},{3,1},{4,6},{5,7},{6,4},{7,5},{8,10},{9,11},{10,... | collective-permute-start | bytes 294920 | tf_op jit(solution)/shard_map/ppermute | solution.py:16
  32.2 13.9 %collective-permute-start.12 = (f32[64,384]{1,0:T(8,128)S(1)}, f32[64,384]{1,0:T(8,128)S(1)}, u32[]{:S(2)}, u32[]{:S(2)}) collective-permute-start(f32[64,384]{1,0:T(8,128)S(1)} %get-tuple-element.41.refs_0_), channel_id=1, source_target_pairs={{0,3},{1,2},{2,1},{3,0},{4,7},{5,6},{6,5},{7,4},{8,11},{9,10},{10,... | collective-permute-start | bytes 294920 | tf_op jit(solution)/shard_map/ppermute | solution.py:16
  33.8 12.3 %collective-permute-start.13 = (f32[128,256]{1,0:T(8,128)S(1)}, f32[128,256]{1,0:T(8,128)S(1)}, u32[]{:S(2)}, u32[]{:S(2)}) collective-permute-start(f32[128,256]{1,0:T(8,128)S(1)} %get-tuple-element.39.refs_4_), channel_id=1, source_target_pairs={{0,1},{1,0},{2,3},{3,2},{4,5},{5,4},{6,7},{7,6},{8,9},{9,8},{10,11... | collective-permute-start | bytes 393224 | tf_op jit(solution)/shard_map/ppermute | solution.py:16

commit v5 on v4

--- a/solution.py
+++ b/solution.py
@@ -31,14 +31,22 @@
     return lax.dynamic_index_in_dim(x, index, 0, keepdims=False)
 
 
-def scatter_sum(x, axis, index, stride=1):
-    size = x.shape[0]
-    order = sorted(range(1, size), key=lambda d: -(d ^ 1))
-    got = [swap(piece(x, index[d]), axis, d * stride) for d in order]
-    total = piece(x, index[0])
-    for part in got:
-        total = total + part
-    return total
+def farthest_first(size):
+    return sorted(range(1, size), key=lambda d: -(d ^ 1))
+
+
+def parcels(x, index):
+    return {d: piece(x, index[d]) for d in farthest_first(x.shape[0])}
+
+
+def exchanged(sends, axis, stride=1):
+    return [swap(x, axis, d * stride) for d, x in sends.items()]
+
+
+def summed(own, parts):
+    for part in parts:
+        own = own + part
+    return own
 
 
 def product(left, right):
@@ -119,37 +127,44 @@
     )(masked, columns)
 
 
-def scaled_kernel(entries, place, totals, *refs):
-    *pieces, out, ordered = refs
+def scaled_kernel(entries, side, place, totals, late, early, parcel, *refs):
+    *far, out, ordered = refs
     rows, block = out.shape
     half = block // CORES
-    first = pieces[0].shape[1]
-    lates, earlies = pieces[-CORES:], pieces[:-CORES]
+    middle = late.shape[1]
+    height, width = early.shape
     factor = 1.0 / jnp.sqrt(jnp.sum(totals[...]) / entries + 1e-06)
-    height = rows // (len(earlies) // CORES)
-    for d, piece in enumerate(earlies):
-        ordered[place[0] ^ d] = piece[...] * factor
-    for member in range(len(earlies)):
+    pieces = [early[...], parcel[:, :width], *(x[...] for x in far)]
+    for d, x in enumerate(pieces):
+        ordered[place[0] ^ d] = x * factor
+    for member in range(len(pieces)):
         row, column = member // CORES * height, member % CORES * half
-        out[row : row + height, column : column + first] = ordered[member]
-    for d, piece in enumerate(lates):
-        column = pl.multiple_of((place[0] ^ d) % CORES * half + first, 128)
-        out[:, pl.ds(column, half - first)] = piece[...] * factor
-
-
-def scaled(place, totals, early, late, entries):
+        out[row : row + height, column : column + side] = ordered[member, :, :side]
+        column += side + middle
+        out[row : row + height, column : column + width - side] = ordered[member, :, side:]
+    core = place[0] % CORES
+    mine = pl.multiple_of(core * half + side, 128)
+    other = pl.multiple_of((1 - core) * half + side, 128)
+    out[:, pl.ds(mine, middle)] = late[...] * factor
+    for part in range(rows // height):
+        start = width + part * middle
+        x = parcel[:, start : start + middle] * factor
+        out[part * height : (part + 1) * height, pl.ds(other, middle)] = x
+
+
+def scaled(place, totals, late, early, parcel, far, side, entries):
     smem = pl.BlockSpec(memory_space=pltpu.SMEM)
     vmem = pl.BlockSpec(memory_space=pltpu.VMEM)
-    rows = late[0].shape[0]
-    block = CORES * (early[0].shape[1] + late[0].shape[1])
+    rows, middle = late.shape
+    height, width = early.shape
     return pl.pallas_call(
-        functools.partial(scaled_kernel, entries),
-        out_shape=jax.ShapeDtypeStruct((rows, block), jnp.float32),
-        in_specs=[smem] + [vmem] * (1 + len(early) + len(late)),
+        functools.partial(scaled_kernel, entries, side),
+        out_shape=jax.ShapeDtypeStruct((rows, CORES * (width + middle)), jnp.float32),
+        in_specs=[smem] + [vmem] * (4 + len(far)),
         out_specs=vmem,
-        scratch_shapes=[pltpu.VMEM((len(early), *early[0].shape), jnp.float32)],
+        scratch_shapes=[pltpu.VMEM((CORES + len(far), height, width), jnp.float32)],
         compiler_params=pltpu.CompilerParams(vmem_limit_bytes=VMEM_BYTES),
-    )(place, totals.reshape(-1, 128), *early, *late)
+    )(place, totals.reshape(-1, 128), late, early, parcel, *far)
 
 
 def on_device(act, dy, w_out, counts):
@@ -173,46 +188,72 @@
     )
     own_rows = hidden // n_loop
     half = block // CORES
-    first = half * 3 // 5 // 128 * 128
+    tile = half // 5 // 128 * 128
+    widths = (2 * tile, 2 * tile, half - 4 * tile)
 
     live = lax.broadcasted_iota(jnp.int32, (rows, 1), 0) < counts[0, 0]
     entries = lax.axis_size("mod") * hidden * block
 
-    early_other, masked, late_columns, own_columns = first_term(
-        counts, place, tokens, upstream, half, first
-    )
-    early_other = swap(early_other, "line", 1)
-    (late_other,) = terms(masked, late_columns, half - first)
+    def by_row_part(x):
+        return x.reshape(n_loop, n_y, own_rows // n_y, -1).transpose(1, 0, 2, 3)
+
+    first_other, masked, columns, own_columns = first_term(
+        counts, place, tokens, upstream, half, widths[0]
+    )
+    first_other = swap(first_other, "line", 1)
+    late_other, second_other = terms(masked, columns, *widths[1:])
     late_other = swap(late_other, "line", 1)
-    early, late = terms(masked, own_columns, first, half - first)
-    early = early + early_other
-    late = late + after(late_other, early)
+    second_other = swap(second_other, "line", 1)
+    first_sum, late, second_sum = terms(masked, own_columns, *widths)
+    first_sum = by_row_part(first_sum + first_other)
+    sends = parcels(first_sum, over_y)
+    first_parts = exchanged(sends, "line", CORES)
+    late = late + after(late_other, *sends.values())
+    late = late.reshape(n_loop, own_rows, widths[1])
+    sends = parcels(late, over_z)
+    late_parts = exchanged(sends, "loop")
+    second_sum = by_row_part(second_sum + after(second_other, *sends.values()))
+    sends = parcels(second_sum, over_y)
+    second_parts = exchanged(sends, "line", CORES)
+    first_parts = [after(part, *sends.values()) for part in first_parts]
     back = lax.dot_general(
-        after(upstream, late), weight, (((1,), (1,)), ((), ())), preferred_element_type=jnp.float32
+        after(upstream, *sends.values()),
+        weight,
+        (((1,), (1,)), ((), ())),
+        preferred_element_type=jnp.float32,
     )
     hidden_grad = jnp.where(live, back, jnp.zeros_like(back)).astype(jnp.bfloat16)
 
-    early = early.reshape(n_loop, n_y, own_rows // n_y, first).transpose(1, 0, 2, 3)
-    early = scatter_sum(early, "line", over_y, CORES)
-    late = scatter_sum(late.reshape(n_loop, own_rows, half - first), "loop", over_z)
-    early_part = early
-    early = scatter_sum(early, "loop", over_z)
-    late = after(late, early_part)
+    early = jnp.concatenate(
+        [
+            summed(piece(x, over_y[0]), parts)
+            for x, parts in ((first_sum, first_parts), (second_sum, second_parts))
+        ],
+        axis=-1,
+    )
+    sends = parcels(early, over_z)
+    early_parts = exchanged(sends, "loop")
+    late_parts = [after(part, *sends.values()) for part in late_parts]
+    late = summed(piece(late, over_z[0]), late_parts)
+    late = after(late, *sends.values())
     for d in doubled(n_y):
         late = late + swap(late, "line", d * CORES)
+    early = summed(piece(early, over_z[0]), early_parts)
 
     squares = jnp.sum(early * early, axis=0).reshape(-1, 128).sum(0)
     squares_late = jnp.sum(late * late, axis=0).reshape(-1, 128).sum(0)
     total = (squares + jnp.where(low_y, squares_late, 0.0)).reshape(1, 128)
     total = after(total, hidden_grad)
+    height = own_rows // n_y
+    rows_late = [late[start : start + height] for start in range(0, own_rows, height)]
+    parcel = swap(jnp.concatenate([early, *rows_late], axis=1), "line", 1)
+    far = [swap(early, "line", d) for d in range(CORES, n_y * CORES)]
     everyone = ("mod", "loop", "line")
     members = lax.axis_size(everyone)
-    early = [early] + [swap(early, "line", d) for d in range(1, n_y * CORES)]
-    late = [late] + [swap(late, "line", d) for d in range(1, CORES)]
     totals = lax.all_to_all(
         jnp.broadcast_to(total[None], (members, 1, 128)), everyone, 0, 0, tiled=True
     )
-    clipped = scaled(place, totals, early, late, entries)
+    clipped = scaled(place, totals, late, early, parcel, far, widths[0], entries)
     return (clipped[None], hidden_grad[None])
 
 

time: 47.4 us -> 46.7 us (0.985)
  waiting for transfers between devices: 10.8 us -> 8.94 us
  starting transfers between devices: 16.2 us -> 16.9 us
    ppermute x14 -> x15, waiting for transfers between devices: 10.8 us -> 8.94 us  [swap(): return lax.ppermute(x, axis, [(i, i ^ distance) for i in range(size)])]
    ppermute x14 -> x15, starting transfers between devices: 16.2 us -> 16.9 us  [swap(): return lax.ppermute(x, axis, [(i, i ^ distance) for i in range(size)])]
  transfers between devices with their start and end apart: 14 -> 15, of which waited for: 4 -> 2; matrix products, arithmetic and copies ran while one was open for 5% -> 6% of each run, Pallas kernels for 3% -> 3%
where the time goes in v5:
time: 46.7 us; the launch traced here: 46.6 us
  starting transfers between devices  16.9 us (36%)
  blocking collectives  12.3 us (26%)
  waiting for transfers between devices  8.94 us (19%)
  Pallas kernels  4.32 us (9%)
  matrix products  2.09 us (4%)
  between operations  1.52 us (3%)
    ppermute x15, starting transfers between devices, swap(): return lax.ppermute(x, axis, [(i, i ^ distance) for i in range(size)])  16.9 us
    all_to_all x1, blocking collectives, on_device(): lax.all_to_all(jnp.broadcast_to(total[None], (members, 1, 128)), everyone...  12.3 us
    ppermute x15, waiting for transfers between devices, swap(): return lax.ppermute(x, axis, [(i, i ^ distance) for i in range(size)])  8.94 us
    dot_general x1, matrix products, on_device(): lax.dot_general(after(upstream, *sends.values()), weight, (((1,), (1,)),...  2.09 us
    pallas_call x1, Pallas kernels, first_term(): pl.pallas_call(first_kernel, out_shape=(jax.ShapeDtypeStruct((hidden, fir...  1.79 us
    pallas_call x2, Pallas kernels, terms(): pl.pallas_call(terms_kernel, out_shape=tuple((jax.ShapeDtypeStruct((hidde...  1.42 us
    pallas_call x1, Pallas kernels, scaled(): pl.pallas_call(functools.partial(scaled_kernel, entries, side), out_shape...  1.12 us
  transfers between devices with their start and end apart: 15, of which 2 were waited for; matrix products, arithmetic and copies ran while one was open for 6% of the time, Pallas kernels for 3%

profile of v5, /device:TPU:0, one launch (start us, length us, event | category | flops | bytes accessed | tf_op | source)
XLA Modules:
  0.0 46.6 jit_solution(7869992655872394472)
XLA Ops:
  0.6 0.0 copy-start
  1.4 1.8 %shard_map.59 = (f32[512,256]{1,0:T(8,128)S(1)}, bf16[768,512]{1,0:T(8,128)(2,1)S(1)}, bf16[768,384]{1,0:T(8,128)(2,1)S(1)}, bf16[768,640]{1,0:T(8,128)(2,1)S(1)}) custom-call(s32[1,1,1]{2,1,0:T(1,128)} %copy.6.count, s32[1]{0:T(128)} %bitcast.place, bf16[768,512]{1,0:T(8,128)(2,1)} %bitcast.66, bf16[768,1280]{1,0:T(8,128)(2,1)} %bitcast.62), custom_call_target="tpu_custom_call" | custom-call | tf_op jit(solution)/shard_map/pallas_call | solution.py:86
  3.2 0.5 %collective-permute-start = (f32[512,256]{1,0:T(8,128)S(1)}, f32[512,256]{1,0:T(8,128)S(1)}, u32[]{:S(2)}, u32[]{:S(2)}) collective-permute-start(f32[512,256]{1,0:T(8,128)S(1)} %get-tuple-element.32), channel_id=1, source_target_pairs={{0,1},{1,0},{2,3},{3,2},{4,5},{5,4},{6,7},{7,6},{8,9},{9,8},{10,11... | collective-permute-start | bytes 1572872 | tf_op jit(solution)/shard_map/ppermute | solution.py:16
  3.7 0.6 %shard_map.61 = (f32[512,256]{1,0:T(8,128)S(1)}, f32[512,128]{1,0:T(8,128)S(1)}) custom-call(bf16[768,512]{1,0:T(8,128)(2,1)S(1)} %get-tuple-element.29.masked, bf16[768,384]{1,0:T(8,128)(2,1)S(1)} %get-tuple-element.36.columns), custom_call_target="tpu_custom_call" | custom-call | tf_op jit(solution)/shard_map/pallas_call | solution.py:121
  4.3 0.1 collective-permute-start.3
  4.5 0.4 collective-permute-start.2
  4.9 0.8 %shard_map.60 = (f32[512,256]{1,0:T(8,128)S(1)}, f32[512,256]{1,0:T(8,128)S(1)}, f32[512,128]{1,0:T(8,128)S(1)}) custom-call(bf16[768,512]{1,0:T(8,128)(2,1)S(1)} %get-tuple-element.29.masked, bf16[768,640]{1,0:T(8,128)(2,1)S(1)} %get-tuple-element.30.columns), custom_call_target="tpu_custom_call" | custom-call | tf_op jit(solution)/shard_map/pallas_call | solution.py:121
  5.7 0.0 collective-permute-done
  5.7 0.1 add.49
  5.8 2.7 %collective-permute-start.1 = (f32[4,64,256]{2,1,0:T(8,128)S(1)}, f32[4,64,256]{2,1,0:T(8,128)S(1)}, u32[]{:S(2)}, u32[]{:S(2)}) collective-permute-start(f32[4,64,256]{2,1,0:T(8,128)S(1)} %dynamic-slice_bitcast_fusion), channel_id=1, source_target_pairs={{0,2},{1,3},{2,0},{3,1},{4,6},{5,7},{6,4},{7,5},{8,10},{9,11},{10,... | collective-permute-start | bytes 786440 | tf_op jit(solution)/shard_map/ppermute | solution.py:16
  8.5 0.0 collective-permute-done.3
  8.5 0.0 copy-start.1
  8.5 0.1 add.50
  8.6 2.7 %collective-permute-start.8 = (f32[128,256]{1,0:T(8,128)S(1)}, f32[128,256]{1,0:T(8,128)S(1)}, u32[]{:S(2)}, u32[]{:S(2)}) collective-permute-start(f32[128,256]{1,0:T(8,128)S(1)} %get-tuple-element.60), channel_id=1, source_target_pairs={{0,8},{4,12},{8,0},{12,4},{1,9},{5,13},{9,1},{13,5},{2,10},{6,14},... | collective-permute-start | bytes 393224 | tf_op jit(solution)/shard_map/ppermute | solution.py:16
  11.3 1.4 %collective-permute-start.9 = (f32[128,256]{1,0:T(8,128)S(1)}, f32[128,256]{1,0:T(8,128)S(1)}, u32[]{:S(2)}, u32[]{:S(2)}) collective-permute-start(f32[128,256]{1,0:T(8,128)S(1)} %get-tuple-element.59), channel_id=1, source_target_pairs={{0,12},{4,8},{8,4},{12,0},{1,13},{5,9},{9,5},{13,1},{2,14},{6,10},... | collective-permute-start | bytes 393224 | tf_op jit(solution)/shard_map/ppermute | solution.py:16
  12.6 0.2 collective-permute-start.10
  12.9 0.0 collective-permute-done.2
  12.9 0.6 %collective-permute-start.4 = (f32[4,64,128]{2,1,0:T(8,128)S(1)}, f32[4,64,128]{2,1,0:T(8,128)S(1)}, u32[]{:S(2)}, u32[]{:S(2)}) collective-permute-start(f32[4,64,128]{2,1,0:T(8,128)S(1)} %dynamic-slice_bitcast_fusion.1), channel_id=1, source_target_pairs={{0,2},{1,3},{2,0},{3,1},{4,6},{5,7},{6,4},{7,5},{8,10},{9,11},{10,... | collective-permute-start | bytes 393224 | tf_op jit(solution)/shard_map/ppermute | solution.py:16
  13.5 0.0 copy-done
  13.5 0.0 copy-done.1
  13.5 2.1 %select_convert_fusion = bf16[768,512]{1,0:T(8,128)(2,1)} fusion(bf16[768,1280]{1,0:T(8,128)(2,1)S(1)} %bitcast.63, bf16[1,512,1280]{2,1,0:T(8,128)(2,1)S(1)} %copy-done, pred[768]{0:T(1024)(128)(4,1)S(1)} %iota_compare_fusion), kind=kOutput, calls=%fused_computation | convolution fusion | flops 1007419392 | bytes 4064000 | tf_op jit(solution)/shard_map/dot_general | solution.py:219
  15.6 2.6 %collective-permute-done.4 = f32[4,64,128]{2,1,0:T(8,128)S(1)} collective-permute-done((f32[4,64,128]{2,1,0:T(8,128)S(1)}, f32[4,64,128]{2,1,0:T(8,128)S(1)}, u32[]{:S(2)}, u32[]{:S(2)}) %collective-permute-start.4) | collective-permute-done | bytes 131104 | tf_op jit(solution)/shard_map/ppermute | solution.py:16
  18.2 0.0 collective-permute-done.1
  18.3 2.9 %collective-permute-start.5 = (f32[64,384]{1,0:T(8,128)S(1)}, f32[64,384]{1,0:T(8,128)S(1)}, u32[]{:S(2)}, u32[]{:S(2)}) collective-permute-start(f32[64,384]{1,0:T(8,128)S(1)} %get-tuple-element.61), channel_id=1, source_target_pairs={{0,8},{4,12},{8,0},{12,4},{1,9},{5,13},{9,1},{13,5},{2,10},{6,14},... | collective-permute-start | bytes 294920 | tf_op jit(solution)/shard_map/ppermute | solution.py:16
  21.2 1.3 %collective-permute-start.6 = (f32[64,384]{1,0:T(8,128)S(1)}, f32[64,384]{1,0:T(8,128)S(1)}, u32[]{:S(2)}, u32[]{:S(2)}) collective-permute-start(f32[64,384]{1,0:T(8,128)S(1)} %get-tuple-element.62), channel_id=1, source_target_pairs={{0,12},{4,8},{8,4},{12,0},{1,13},{5,9},{9,5},{13,1},{2,14},{6,10},... | collective-permute-start | bytes 294920 | tf_op jit(solution)/shard_map/ppermute | solution.py:16
  22.6 0.0 collective-permute-done.8
  22.6 0.2 collective-permute-start.7
  22.8 0.0 collective-permute-done.9
  22.8 0.0 collective-permute-done.10
  22.9 1.6 %collective-permute-start.11 = (f32[128,256]{1,0:T(8,128)S(1)}, f32[128,256]{1,0:T(8,128)S(1)}, u32[]{:S(2)}, u32[]{:S(2)}) collective-permute-start(f32[128,256]{1,0:T(8,128)S(1)} %fusion.2), channel_id=1, source_target_pairs={{0,2},{1,3},{2,0},{3,1},{4,6},{5,7},{6,4},{7,5},{8,10},{9,11},{10,... | collective-permute-start | bytes 393224 | tf_op jit(solution)/shard_map/ppermute | solution.py:16
  24.4 6.3 %collective-permute-done.5 = f32[64,384]{1,0:T(8,128)S(1)} collective-permute-done((f32[64,384]{1,0:T(8,128)S(1)}, f32[64,384]{1,0:T(8,128)S(1)}, u32[]{:S(2)}, u32[]{:S(2)}) %collective-permute-start.5) | collective-permute-done | bytes 98336 | tf_op jit(solution)/shard_map/ppermute | solution.py:16
  30.7 0.0 collective-permute-done.6
  30.7 0.0 collective-permute-done.7
  30.8 1.0 %collective-permute-start.13 = (f32[64,384]{1,0:T(8,128)S(1)}, f32[64,384]{1,0:T(8,128)S(1)}, u32[]{:S(2)}, u32[]{:S(2)}) collective-permute-start(f32[64,384]{1,0:T(8,128)S(1)} %get-tuple-element.57.early), channel_id=1, source_target_pairs={{0,2},{1,3},{2,0},{3,1},{4,6},{5,7},{6,4},{7,5},{8,10},{9,11},{10,... | collective-permute-start | bytes 294920 | tf_op jit(solution)/shard_map/ppermute | solution.py:16
  31.8 0.0 collective-permute-start.14
  31.8 0.0 collective-permute-done.11
  31.9 1.2 %collective-permute-start.12 = (f32[64,896]{1,0:T(8,128)S(1)}, f32[64,896]{1,0:T(8,128)S(1)}, u32[]{:S(2)}, u32[]{:S(2)}) collective-permute-start(f32[64,896]{1,0:T(8,128)S(1)} %pad_maximum_fusion), channel_id=1, source_target_pairs={{0,1},{1,0},{2,3},{3,2},{4,5},{5,4},{6,7},{7,6},{8,9},{9,8},{10,11... | collective-permute-start | bytes 688136 | tf_op jit(solution)/shard_map/ppermute | solution.py:16
  33.2 12.3 %all_to_all.5 = f32[32,1,128]{2,1,0:T(1,128)S(1)} all-to-all(f32[32,1,128]{2,1,0:T(1,128)S(1)} %broadcast_in_dim.33), channel_id=1, replica_groups=mesh['mod'=2,'loop'=4,'line'=4] {'mod','loop','line'}, dimensions={0} | all-to-all | bytes 32768 | tf_op jit(solution)/shard_map/all_to_all | solution.py:253
  45.4 0.0 collective-permute-done.13.refs_0_
  45.4 0.0 collective-permute-done.14.refs_1_
  45.5 0.0 collective-permute-done.12.parcel
  45.5 1.1 %shard_map.62 = f32[128,1280]{1,0:T(8,128)} custom-call(s32[1]{0:T(128)} %bitcast.place, f32[32,128]{1,0:T(8,128)S(1)} %bitcast.57, f32[128,256]{1,0:T(8,128)S(1)} %get-tuple-element.55.late, f32[64,384]{1,0:T(8,128)S(1)} %get-tuple-element.57.early, f32[64,896]{1,0:T(8,128)S(1)} %collective-permute-done.12.parcel, ...), custom_call_target="tpu_custom_call" | custom-call | tf_op jit(solution)/shard_map/pallas_call | solution.py:160
  (17 shorter events, 0.4 us)
Async XLA Ops:
  0.6 12.9 %copy-start = (bf16[1,512,1280]{2,1,0:T(8,128)(2,1)S(1)}, bf16[1,512,1280]{2,1,0:T(8,128)(2,1)}, u32[]{:S(2)}) copy-start(bf16[1,512,1280]{2,1,0:T(8,128)(2,1)} %param.6) | copy-start | bytes 3932164
  3.2 2.5 %collective-permute-start = (f32[512,256]{1,0:T(8,128)S(1)}, f32[512,256]{1,0:T(8,128)S(1)}, u32[]{:S(2)}, u32[]{:S(2)}) collective-permute-start(f32[512,256]{1,0:T(8,128)S(1)} %get-tuple-element.32), channel_id=1, source_target_pairs={{0,1},{1,0},{2,3},{3,2},{4,5},{5,4},{6,7},{7,6},{8,9},{9,8},{10,11... | collective-permute-start | bytes 1572872 | tf_op jit(solution)/shard_map/ppermute | solution.py:16
  4.3 4.2 %collective-permute-start.3 = (f32[512,256]{1,0:T(8,128)S(1)}, f32[512,256]{1,0:T(8,128)S(1)}, u32[]{:S(2)}, u32[]{:S(2)}) collective-permute-start(f32[512,256]{1,0:T(8,128)S(1)} %get-tuple-element.39), channel_id=1, source_target_pairs={{0,1},{1,0},{2,3},{3,2},{4,5},{5,4},{6,7},{7,6},{8,9},{9,8},{10,11... | collective-permute-start | bytes 1572872 | tf_op jit(solution)/shard_map/ppermute | solution.py:16
  4.5 8.4 %collective-permute-start.2 = (f32[512,128]{1,0:T(8,128)S(1)}, f32[512,128]{1,0:T(8,128)S(1)}, u32[]{:S(2)}, u32[]{:S(2)}) collective-permute-start(f32[512,128]{1,0:T(8,128)S(1)} %get-tuple-element.37), channel_id=1, source_target_pairs={{0,1},{1,0},{2,3},{3,2},{4,5},{5,4},{6,7},{7,6},{8,9},{9,8},{10,11... | collective-permute-start | bytes 786440 | tf_op jit(solution)/shard_map/ppermute | solution.py:16
  5.8 12.4 %collective-permute-start.1 = (f32[4,64,256]{2,1,0:T(8,128)S(1)}, f32[4,64,256]{2,1,0:T(8,128)S(1)}, u32[]{:S(2)}, u32[]{:S(2)}) collective-permute-start(f32[4,64,256]{2,1,0:T(8,128)S(1)} %dynamic-slice_bitcast_fusion), channel_id=1, source_target_pairs={{0,2},{1,3},{2,0},{3,1},{4,6},{5,7},{6,4},{7,5},{8,10},{9,11},{10,... | collective-permute-start | bytes 786440 | tf_op jit(solution)/shard_map/ppermute | solution.py:16
  8.5 5.0 %copy-start.1 = (bf16[1,768,1280]{2,1,0:T(8,128)(2,1)S(1)}, bf16[1,768,1280]{2,1,0:T(8,128)(2,1)}, u32[]{:S(2)}) copy-start(bf16[1,768,1280]{2,1,0:T(8,128)(2,1)} %param.5) | copy-start | bytes 5898244
  8.6 13.9 %collective-permute-start.8 = (f32[128,256]{1,0:T(8,128)S(1)}, f32[128,256]{1,0:T(8,128)S(1)}, u32[]{:S(2)}, u32[]{:S(2)}) collective-permute-start(f32[128,256]{1,0:T(8,128)S(1)} %get-tuple-element.60), channel_id=1, source_target_pairs={{0,8},{4,12},{8,0},{12,4},{1,9},{5,13},{9,1},{13,5},{2,10},{6,14},... | collective-permute-start | bytes 393224 | tf_op jit(solution)/shard_map/ppermute | solution.py:16
  11.3 11.5 %collective-permute-start.9 = (f32[128,256]{1,0:T(8,128)S(1)}, f32[128,256]{1,0:T(8,128)S(1)}, u32[]{:S(2)}, u32[]{:S(2)}) collective-permute-start(f32[128,256]{1,0:T(8,128)S(1)} %get-tuple-element.59), channel_id=1, source_target_pairs={{0,12},{4,8},{8,4},{12,0},{1,13},{5,9},{9,5},{13,1},{2,14},{6,10},... | collective-permute-start | bytes 393224 | tf_op jit(solution)/shard_map/ppermute | solution.py:16
  12.6 10.2 %collective-permute-start.10 = (f32[128,256]{1,0:T(8,128)S(1)}, f32[128,256]{1,0:T(8,128)S(1)}, u32[]{:S(2)}, u32[]{:S(2)}) collective-permute-start(f32[128,256]{1,0:T(8,128)S(1)} %get-tuple-element.58), channel_id=1, source_target_pairs={{0,4},{4,0},{8,12},{12,8},{1,5},{5,1},{9,13},{13,9},{2,6},{6,2},{1... | collective-permute-start | bytes 393224 | tf_op jit(solution)/shard_map/ppermute | solution.py:16
  12.9 5.3 %collective-permute-start.4 = (f32[4,64,128]{2,1,0:T(8,128)S(1)}, f32[4,64,128]{2,1,0:T(8,128)S(1)}, u32[]{:S(2)}, u32[]{:S(2)}) collective-permute-start(f32[4,64,128]{2,1,0:T(8,128)S(1)} %dynamic-slice_bitcast_fusion.1), channel_id=1, source_target_pairs={{0,2},{1,3},{2,0},{3,1},{4,6},{5,7},{6,4},{7,5},{8,10},{9,11},{10,... | collective-permute-start | bytes 393224 | tf_op jit(solution)/shard_map/ppermute | solution.py:16
  18.3 12.4 %collective-permute-start.5 = (f32[64,384]{1,0:T(8,128)S(1)}, f32[64,384]{1,0:T(8,128)S(1)}, u32[]{:S(2)}, u32[]{:S(2)}) collective-permute-start(f32[64,384]{1,0:T(8,128)S(1)} %get-tuple-element.61), channel_id=1, source_target_pairs={{0,8},{4,12},{8,0},{12,4},{1,9},{5,13},{9,1},{13,5},{2,10},{6,14},... | collective-permute-start | bytes 294920 | tf_op jit(solution)/shard_map/ppermute | solution.py:16
  21.2 9.5 %collective-permute-start.6 = (f32[64,384]{1,0:T(8,128)S(1)}, f32[64,384]{1,0:T(8,128)S(1)}, u32[]{:S(2)}, u32[]{:S(2)}) collective-permute-start(f32[64,384]{1,0:T(8,128)S(1)} %get-tuple-element.62), channel_id=1, source_target_pairs={{0,12},{4,8},{8,4},{12,0},{1,13},{5,9},{9,5},{13,1},{2,14},{6,10},... | collective-permute-start | bytes 294920 | tf_op jit(solution)/shard_map/ppermute | solution.py:16
  22.6 8.2 %collective-permute-start.7 = (f32[64,384]{1,0:T(8,128)S(1)}, f32[64,384]{1,0:T(8,128)S(1)}, u32[]{:S(2)}, u32[]{:S(2)}) collective-permute-start(f32[64,384]{1,0:T(8,128)S(1)} %get-tuple-element.63), channel_id=1, source_target_pairs={{0,4},{4,0},{8,12},{12,8},{1,5},{5,1},{9,13},{13,9},{2,6},{6,2},{1... | collective-permute-start | bytes 294920 | tf_op jit(solution)/shard_map/ppermute | solution.py:16
  22.9 9.0 %collective-permute-start.11 = (f32[128,256]{1,0:T(8,128)S(1)}, f32[128,256]{1,0:T(8,128)S(1)}, u32[]{:S(2)}, u32[]{:S(2)}) collective-permute-start(f32[128,256]{1,0:T(8,128)S(1)} %fusion.2), channel_id=1, source_target_pairs={{0,2},{1,3},{2,0},{3,1},{4,6},{5,7},{6,4},{7,5},{8,10},{9,11},{10,... | collective-permute-start | bytes 393224 | tf_op jit(solution)/shard_map/ppermute | solution.py:16
  30.8 14.7 %collective-permute-start.13 = (f32[64,384]{1,0:T(8,128)S(1)}, f32[64,384]{1,0:T(8,128)S(1)}, u32[]{:S(2)}, u32[]{:S(2)}) collective-permute-start(f32[64,384]{1,0:T(8,128)S(1)} %get-tuple-element.57.early), channel_id=1, source_target_pairs={{0,2},{1,3},{2,0},{3,1},{4,6},{5,7},{6,4},{7,5},{8,10},{9,11},{10,... | collective-permute-start | bytes 294920 | tf_op jit(solution)/shard_map/ppermute | solution.py:16
  31.8 13.6 %collective-permute-start.14 = (f32[64,384]{1,0:T(8,128)S(1)}, f32[64,384]{1,0:T(8,128)S(1)}, u32[]{:S(2)}, u32[]{:S(2)}) collective-permute-start(f32[64,384]{1,0:T(8,128)S(1)} %get-tuple-element.57.early), channel_id=1, source_target_pairs={{0,3},{1,2},{2,1},{3,0},{4,7},{5,6},{6,5},{7,4},{8,11},{9,10},{10,... | collective-permute-start | bytes 294920 | tf_op jit(solution)/shard_map/ppermute | solution.py:16
  31.9 13.5 %collective-permute-start.12 = (f32[64,896]{1,0:T(8,128)S(1)}, f32[64,896]{1,0:T(8,128)S(1)}, u32[]{:S(2)}, u32[]{:S(2)}) collective-permute-start(f32[64,896]{1,0:T(8,128)S(1)} %pad_maximum_fusion), channel_id=1, source_target_pairs={{0,1},{1,0},{2,3},{3,2},{4,5},{5,4},{6,7},{7,6},{8,9},{9,8},{10,11... | collective-permute-start | bytes 688136 | tf_op jit(solution)/shard_map/ppermute | solution.py:16

commit v6 on v5

--- a/solution.py
+++ b/solution.py
@@ -55,48 +55,55 @@
     )
 
 
-def first_kernel(count, place, act, dy, out, masked, late, own, tokens, early, sems):
-    half = own.shape[1]
-    first = early.shape[1]
+def first_kernel(widths, count, place, act, dy, out, masked, x, y, tokens, middle_dy, sems):
+    side, middle, last = widths
     core = place[0] % CORES
-    other = pl.multiple_of((1 - core) * half, 128)
-    mine = pl.multiple_of(core * half, 128)
-    copies = [
-        pltpu.make_async_copy(act, tokens, sems.at[0]),
-        pltpu.make_async_copy(dy.at[:, pl.ds(other, first)], early, sems.at[1]),
-        pltpu.make_async_copy(dy.at[:, pl.ds(other + first, half - first)], late, sems.at[2]),
-        pltpu.make_async_copy(dy.at[:, pl.ds(mine, half)], own, sems.at[3]),
+    other = pl.multiple_of((1 - core) * sum(widths), 128)
+    mine = pl.multiple_of(core * sum(widths), 128)
+    moves = [
+        (other + side, middle_dy, 0, middle),
+        (other, x, 0, side),
+        (mine + side, x, side, middle),
+        (mine, y, 0, side),
+        (other + side + middle, y, side, last),
+        (mine + side + middle, y, side + last, last),
     ]
+    copies = [pltpu.make_async_copy(act, tokens, sems.at[0])]
+    for column, target, start, width in moves:
+        source = dy.at[:, pl.ds(column, width)]
+        target = target.at[:, start : start + width]
+        copies.append(pltpu.make_async_copy(source, target, sems.at[len(copies)]))
     for copy in copies:
         copy.start()
     copies[0].wait()
     live = lax.broadcasted_iota(jnp.int32, (act.shape[0], 1), 0) < count[0, 0, 0]
     masked[...] = jnp.where(live, tokens[...], jnp.zeros_like(tokens))
     copies[1].wait()
-    out[...] = product(masked[...], early[...])
-    copies[2].wait()
-    copies[3].wait()
-
-
-def first_term(counts, place, act, dy, half, first):
+    out[...] = product(masked[...], middle_dy[...])
+    for copy in copies[2:]:
+        copy.wait()
+
+
+def first_term(counts, place, act, dy, widths):
     rows, hidden = act.shape
+    side, middle, last = widths
     smem = pl.BlockSpec(memory_space=pltpu.SMEM)
     vmem = pl.BlockSpec(memory_space=pltpu.VMEM)
     hbm = pl.BlockSpec(memory_space=pltpu.HBM)
     return pl.pallas_call(
-        first_kernel,
+        functools.partial(first_kernel, widths),
         out_shape=(
-            jax.ShapeDtypeStruct((hidden, first), jnp.float32),
+            jax.ShapeDtypeStruct((hidden, middle), jnp.float32),
             jax.ShapeDtypeStruct((rows, hidden), act.dtype),
-            jax.ShapeDtypeStruct((rows, half - first), dy.dtype),
-            jax.ShapeDtypeStruct((rows, half), dy.dtype),
+            jax.ShapeDtypeStruct((rows, side + middle), dy.dtype),
+            jax.ShapeDtypeStruct((rows, side + 2 * last), dy.dtype),
         ),
         in_specs=[smem, smem, hbm, hbm],
         out_specs=(vmem,) * 4,
         scratch_shapes=[
             pltpu.VMEM((rows, hidden), act.dtype),
-            pltpu.VMEM((rows, first), dy.dtype),
-            pltpu.SemaphoreType.DMA((4,)),
+            pltpu.VMEM((rows, middle), dy.dtype),
+            pltpu.SemaphoreType.DMA((7,)),
         ],
         compiler_params=pltpu.CompilerParams(vmem_limit_bytes=VMEM_BYTES),
     )(
@@ -197,22 +204,23 @@
     def by_row_part(x):
         return x.reshape(n_loop, n_y, own_rows // n_y, -1).transpose(1, 0, 2, 3)
 
-    first_other, masked, columns, own_columns = first_term(
-        counts, place, tokens, upstream, half, widths[0]
-    )
+    late_other, masked, columns, more_columns = first_term(
+        counts, place, tokens, upstream, widths
+    )
+    late_other = swap(late_other, "line", 1)
+    first_other, late = terms(masked, columns, *widths[:2])
     first_other = swap(first_other, "line", 1)
-    late_other, second_other = terms(masked, columns, *widths[1:])
-    late_other = swap(late_other, "line", 1)
+    first_sum, second_both = terms(masked, more_columns, widths[0], 2 * widths[2])
+    second_other, second_sum = second_both[:, : widths[2]], second_both[:, widths[2] :]
     second_other = swap(second_other, "line", 1)
-    first_sum, late, second_sum = terms(masked, own_columns, *widths)
-    first_sum = by_row_part(first_sum + first_other)
+    late = (late + late_other).reshape(n_loop, own_rows, widths[1])
+    late_sends = parcels(late, over_z)
+    farthest, *others = late_sends
+    first_sum = by_row_part(first_sum + after(first_other, late_sends[farthest]))
     sends = parcels(first_sum, over_y)
     first_parts = exchanged(sends, "line", CORES)
-    late = late + after(late_other, *sends.values())
-    late = late.reshape(n_loop, own_rows, widths[1])
-    sends = parcels(late, over_z)
-    late_parts = exchanged(sends, "loop")
-    second_sum = by_row_part(second_sum + after(second_other, *sends.values()))
+    late_parts = exchanged(late_sends, "loop")
+    second_sum = by_row_part(second_sum + after(second_other, *late_sends.values(), *sends.values()))
     sends = parcels(second_sum, over_y)
     second_parts = exchanged(sends, "line", CORES)
     first_parts = [after(part, *sends.values()) for part in first_parts]

time: 46.7 us -> 46.3 us (level)
  waiting for transfers between devices: 8.94 us -> 10.3 us
  blocking collectives: 12.3 us -> 11 us
    ppermute x15, waiting for transfers between devices: 8.94 us -> 10.3 us  [swap(): return lax.ppermute(x, axis, [(i, i ^ distance) for i in range(size)])]
    all_to_all x1, blocking collectives: 12.3 us -> 11 us  [on_device(): lax.all_to_all(jnp.broadcast_to(total[None], (members, 1, 128)), everyone...]
  transfers between devices with their start and end apart: 15 -> 15, of which waited for: 2 -> 3; matrix products, arithmetic and copies ran while one was open for 6% -> 6% of each run, Pallas kernels for 3% -> 3%
where the time goes in v6:
time: 46.3 us; the launch traced here: 46.1 us
  starting transfers between devices  16.5 us (36%)
  blocking collectives  11 us (24%)
  waiting for transfers between devices  10.3 us (22%)
  Pallas kernels  4.15 us (9%)
  matrix products  2.09 us (5%)
  between operations  1.53 us (3%)
    ppermute x15, starting transfers between devices, swap(): return lax.ppermute(x, axis, [(i, i ^ distance) for i in range(size)])  16.5 us
    all_to_all x1, blocking collectives, on_device(): lax.all_to_all(jnp.broadcast_to(total[None], (members, 1, 128)), everyone...  11 us
    ppermute x15, waiting for transfers between devices, swap(): return lax.ppermute(x, axis, [(i, i ^ distance) for i in range(size)])  10.3 us
    dot_general x1, matrix products, on_device(): lax.dot_general(after(upstream, *sends.values()), weight, (((1,), (1,)),...  2.09 us
    pallas_call x1, Pallas kernels, first_term(): pl.pallas_call(functools.partial(first_kernel, widths), out_shape=(jax.Sh...  1.79 us
    pallas_call x2, Pallas kernels, terms(): pl.pallas_call(terms_kernel, out_shape=tuple((jax.ShapeDtypeStruct((hidde...  1.24 us
    pallas_call x1, Pallas kernels, scaled(): pl.pallas_call(functools.partial(scaled_kernel, entries, side), out_shape...  1.12 us
  transfers between devices with their start and end apart: 15, of which 3 were waited for; matrix products, arithmetic and copies ran while one was open for 6% of the time, Pallas kernels for 3%

profile of v6, /device:TPU:0, one launch (start us, length us, event | category | flops | bytes accessed | tf_op | source)
XLA Modules:
  0.0 46.1 jit_solution(12370120911482975767)
XLA Ops:
  0.6 0.0 copy-start
  1.4 1.8 %shard_map.59 = (f32[512,256]{1,0:T(8,128)S(1)}, bf16[768,512]{1,0:T(8,128)(2,1)S(1)}, bf16[768,512]{1,0:T(8,128)(2,1)S(1)}, bf16[768,512]{1,0:T(8,128)(2,1)S(1)}) custom-call(s32[1,1,1]{2,1,0:T(1,128)} %copy.6.count, s32[1]{0:T(128)} %bitcast.place, bf16[768,512]{1,0:T(8,128)(2,1)} %bitcast.66, bf16[768,1280]{1,0:T(8,128)(2,1)} %bitcast.62), custom_call_target="tpu_custom_call" | custom-call | tf_op jit(solution)/shard_map/pallas_call | solution.py:93
  3.2 0.5 %collective-permute-start.1 = (f32[512,256]{1,0:T(8,128)S(1)}, f32[512,256]{1,0:T(8,128)S(1)}, u32[]{:S(2)}, u32[]{:S(2)}) collective-permute-start(f32[512,256]{1,0:T(8,128)S(1)} %get-tuple-element.34), channel_id=1, source_target_pairs={{0,1},{1,0},{2,3},{3,2},{4,5},{5,4},{6,7},{7,6},{8,9},{9,8},{10,11... | collective-permute-start | bytes 1572872 | tf_op jit(solution)/shard_map/ppermute | solution.py:16
  3.7 0.6 %shard_map.61 = (f32[512,256]{1,0:T(8,128)S(1)}, f32[512,256]{1,0:T(8,128)S(1)}) custom-call(bf16[768,512]{1,0:T(8,128)(2,1)S(1)} %get-tuple-element.28.masked, bf16[768,512]{1,0:T(8,128)(2,1)S(1)} %get-tuple-element.31.columns), custom_call_target="tpu_custom_call" | custom-call | tf_op jit(solution)/shard_map/pallas_call | solution.py:128
  4.3 0.1 collective-permute-start
  4.5 0.6 %shard_map.60 = (f32[512,256]{1,0:T(8,128)S(1)}, f32[512,256]{1,0:T(8,128)S(1)}) custom-call(bf16[768,512]{1,0:T(8,128)(2,1)S(1)} %get-tuple-element.28.masked, bf16[768,512]{1,0:T(8,128)(2,1)S(1)} %get-tuple-element.29.columns), custom_call_target="tpu_custom_call" | custom-call | tf_op jit(solution)/shard_map/pallas_call | solution.py:128
  5.1 0.5 %collective-permute-start.3 = (f32[512,128]{1,0:T(8,128)S(1)}, f32[512,128]{1,0:T(8,128)S(1)}, u32[]{:S(2)}, u32[]{:S(2)}) collective-permute-start(f32[512,128]{1,0:T(8,128)S(1)} %slice.13), channel_id=1, source_target_pairs={{0,1},{1,0},{2,3},{3,2},{4,5},{5,4},{6,7},{7,6},{8,9},{9,8},{10,11... | collective-permute-start | bytes 786440 | tf_op jit(solution)/shard_map/ppermute | solution.py:16
  5.6 0.0 collective-permute-done.1
  5.6 0.1 add.49
  5.8 3.7 %collective-permute-start.8 = (f32[128,256]{1,0:T(8,128)S(1)}, f32[128,256]{1,0:T(8,128)S(1)}, u32[]{:S(2)}, u32[]{:S(2)}) collective-permute-start(f32[128,256]{1,0:T(8,128)S(1)} %get-tuple-element.58), channel_id=1, source_target_pairs={{0,8},{4,12},{8,0},{12,4},{1,9},{5,13},{9,1},{13,5},{2,10},{6,14},... | collective-permute-start | bytes 393224 | tf_op jit(solution)/shard_map/ppermute | solution.py:16
  9.4 0.0 collective-permute-done
  9.4 0.0 copy-start.1
  9.4 0.1 add.50
  9.6 1.6 %collective-permute-start.2 = (f32[4,64,256]{2,1,0:T(8,128)S(1)}, f32[4,64,256]{2,1,0:T(8,128)S(1)}, u32[]{:S(2)}, u32[]{:S(2)}) collective-permute-start(f32[4,64,256]{2,1,0:T(8,128)S(1)} %dynamic-slice_bitcast_fusion), channel_id=1, source_target_pairs={{0,2},{1,3},{2,0},{3,1},{4,6},{5,7},{6,4},{7,5},{8,10},{9,11},{10,... | collective-permute-start | bytes 786440 | tf_op jit(solution)/shard_map/ppermute | solution.py:16
  11.1 1.6 %collective-permute-start.9 = (f32[128,256]{1,0:T(8,128)S(1)}, f32[128,256]{1,0:T(8,128)S(1)}, u32[]{:S(2)}, u32[]{:S(2)}) collective-permute-start(f32[128,256]{1,0:T(8,128)S(1)} %get-tuple-element.57), channel_id=1, source_target_pairs={{0,12},{4,8},{8,4},{12,0},{1,13},{5,9},{9,5},{13,1},{2,14},{6,10},... | collective-permute-start | bytes 393224 | tf_op jit(solution)/shard_map/ppermute | solution.py:16
  12.8 0.0 collective-permute-start.10
  12.8 0.0 collective-permute-done.3
  12.8 0.6 %collective-permute-start.4 = (f32[4,64,128]{2,1,0:T(8,128)S(1)}, f32[4,64,128]{2,1,0:T(8,128)S(1)}, u32[]{:S(2)}, u32[]{:S(2)}) collective-permute-start(f32[4,64,128]{2,1,0:T(8,128)S(1)} %dynamic-slice_bitcast_fusion.1), channel_id=1, source_target_pairs={{0,2},{1,3},{2,0},{3,1},{4,6},{5,7},{6,4},{7,5},{8,10},{9,11},{10,... | collective-permute-start | bytes 393224 | tf_op jit(solution)/shard_map/ppermute | solution.py:16
  13.4 0.0 copy-done
  13.4 0.0 copy-done.1
  13.4 2.1 %select_convert_fusion = bf16[768,512]{1,0:T(8,128)(2,1)} fusion(bf16[768,1280]{1,0:T(8,128)(2,1)S(1)} %bitcast.63, bf16[1,512,1280]{2,1,0:T(8,128)(2,1)S(1)} %copy-done, pred[768]{0:T(1024)(128)(4,1)S(1)} %iota_compare_fusion), kind=kOutput, calls=%fused_computation | convolution fusion | flops 1007419392 | bytes 4064000 | tf_op jit(solution)/shard_map/dot_general | solution.py:227
  15.5 5.3 %collective-permute-done.4 = f32[4,64,128]{2,1,0:T(8,128)S(1)} collective-permute-done((f32[4,64,128]{2,1,0:T(8,128)S(1)}, f32[4,64,128]{2,1,0:T(8,128)S(1)}, u32[]{:S(2)}, u32[]{:S(2)}) %collective-permute-start.4) | collective-permute-done | bytes 131104 | tf_op jit(solution)/shard_map/ppermute | solution.py:16
  20.9 0.0 collective-permute-done.2
  20.9 0.8 %collective-permute-start.5 = (f32[64,384]{1,0:T(8,128)S(1)}, f32[64,384]{1,0:T(8,128)S(1)}, u32[]{:S(2)}, u32[]{:S(2)}) collective-permute-start(f32[64,384]{1,0:T(8,128)S(1)} %get-tuple-element.59), channel_id=1, source_target_pairs={{0,8},{4,12},{8,0},{12,4},{1,9},{5,13},{9,1},{13,5},{2,10},{6,14},... | collective-permute-start | bytes 294920 | tf_op jit(solution)/shard_map/ppermute | solution.py:16
  21.8 3.2 %collective-permute-start.6 = (f32[64,384]{1,0:T(8,128)S(1)}, f32[64,384]{1,0:T(8,128)S(1)}, u32[]{:S(2)}, u32[]{:S(2)}) collective-permute-start(f32[64,384]{1,0:T(8,128)S(1)} %get-tuple-element.60), channel_id=1, source_target_pairs={{0,12},{4,8},{8,4},{12,0},{1,13},{5,9},{9,5},{13,1},{2,14},{6,10},... | collective-permute-start | bytes 294920 | tf_op jit(solution)/shard_map/ppermute | solution.py:16
  24.9 0.0 collective-permute-done.8
  25.0 0.0 collective-permute-start.7
  25.0 0.0 collective-permute-done.9
  25.0 0.0 collective-permute-done.10
  25.0 1.6 %collective-permute-start.11 = (f32[128,256]{1,0:T(8,128)S(1)}, f32[128,256]{1,0:T(8,128)S(1)}, u32[]{:S(2)}, u32[]{:S(2)}) collective-permute-start(f32[128,256]{1,0:T(8,128)S(1)} %fusion.2), channel_id=1, source_target_pairs={{0,2},{1,3},{2,0},{3,1},{4,6},{5,7},{6,4},{7,5},{8,10},{9,11},{10,... | collective-permute-start | bytes 393224 | tf_op jit(solution)/shard_map/ppermute | solution.py:16
  26.6 4.7 %collective-permute-done.5 = f32[64,384]{1,0:T(8,128)S(1)} collective-permute-done((f32[64,384]{1,0:T(8,128)S(1)}, f32[64,384]{1,0:T(8,128)S(1)}, u32[]{:S(2)}, u32[]{:S(2)}) %collective-permute-start.5) | collective-permute-done | bytes 98336 | tf_op jit(solution)/shard_map/ppermute | solution.py:16
  31.3 0.0 collective-permute-done.6
  31.3 0.2 collective-permute-done.7
  31.5 1.6 %collective-permute-start.13 = (f32[64,384]{1,0:T(8,128)S(1)}, f32[64,384]{1,0:T(8,128)S(1)}, u32[]{:S(2)}, u32[]{:S(2)}) collective-permute-start(f32[64,384]{1,0:T(8,128)S(1)} %get-tuple-element.55.early), channel_id=1, source_target_pairs={{0,2},{1,3},{2,0},{3,1},{4,6},{5,7},{6,4},{7,5},{8,10},{9,11},{10,... | collective-permute-start | bytes 294920 | tf_op jit(solution)/shard_map/ppermute | solution.py:16
  33.1 0.0 collective-permute-start.14
  33.1 0.0 collective-permute-done.11
  33.2 0.7 %collective-permute-start.12 = (f32[64,896]{1,0:T(8,128)S(1)}, f32[64,896]{1,0:T(8,128)S(1)}, u32[]{:S(2)}, u32[]{:S(2)}) collective-permute-start(f32[64,896]{1,0:T(8,128)S(1)} %pad_maximum_fusion), channel_id=1, source_target_pairs={{0,1},{1,0},{2,3},{3,2},{4,5},{5,4},{6,7},{7,6},{8,9},{9,8},{10,11... | collective-permute-start | bytes 688136 | tf_op jit(solution)/shard_map/ppermute | solution.py:16
  33.9 11.0 %all_to_all.5 = f32[32,1,128]{2,1,0:T(1,128)S(1)} all-to-all(f32[32,1,128]{2,1,0:T(1,128)S(1)} %broadcast_in_dim.33), channel_id=1, replica_groups=mesh['mod'=2,'loop'=4,'line'=4] {'mod','loop','line'}, dimensions={0} | all-to-all | bytes 32768 | tf_op jit(solution)/shard_map/all_to_all | solution.py:261
  45.0 0.0 collective-permute-done.13.refs_0_
  45.0 0.0 collective-permute-done.14.refs_1_
  45.0 0.0 collective-permute-done.12.parcel
  45.0 1.1 %shard_map.62 = f32[128,1280]{1,0:T(8,128)} custom-call(s32[1]{0:T(128)} %bitcast.place, f32[32,128]{1,0:T(8,128)S(1)} %bitcast.57, f32[128,256]{1,0:T(8,128)S(1)} %get-tuple-element.53.late, f32[64,384]{1,0:T(8,128)S(1)} %get-tuple-element.55.early, f32[64,896]{1,0:T(8,128)S(1)} %collective-permute-done.12.parcel, ...), custom_call_target="tpu_custom_call" | custom-call | tf_op jit(solution)/shard_map/pallas_call | solution.py:167
  (18 shorter events, 0.4 us)
Async XLA Ops:
  0.6 12.8 %copy-start = (bf16[1,512,1280]{2,1,0:T(8,128)(2,1)S(1)}, bf16[1,512,1280]{2,1,0:T(8,128)(2,1)}, u32[]{:S(2)}) copy-start(bf16[1,512,1280]{2,1,0:T(8,128)(2,1)} %param.6) | copy-start | bytes 3932164
  3.2 2.4 %collective-permute-start.1 = (f32[512,256]{1,0:T(8,128)S(1)}, f32[512,256]{1,0:T(8,128)S(1)}, u32[]{:S(2)}, u32[]{:S(2)}) collective-permute-start(f32[512,256]{1,0:T(8,128)S(1)} %get-tuple-element.34), channel_id=1, source_target_pairs={{0,1},{1,0},{2,3},{3,2},{4,5},{5,4},{6,7},{7,6},{8,9},{9,8},{10,11... | collective-permute-start | bytes 1572872 | tf_op jit(solution)/shard_map/ppermute | solution.py:16
  4.3 5.1 %collective-permute-start = (f32[512,256]{1,0:T(8,128)S(1)}, f32[512,256]{1,0:T(8,128)S(1)}, u32[]{:S(2)}, u32[]{:S(2)}) collective-permute-start(f32[512,256]{1,0:T(8,128)S(1)} %get-tuple-element.32), channel_id=1, source_target_pairs={{0,1},{1,0},{2,3},{3,2},{4,5},{5,4},{6,7},{7,6},{8,9},{9,8},{10,11... | collective-permute-start | bytes 1572872 | tf_op jit(solution)/shard_map/ppermute | solution.py:16
  5.1 7.6 %collective-permute-start.3 = (f32[512,128]{1,0:T(8,128)S(1)}, f32[512,128]{1,0:T(8,128)S(1)}, u32[]{:S(2)}, u32[]{:S(2)}) collective-permute-start(f32[512,128]{1,0:T(8,128)S(1)} %slice.13), channel_id=1, source_target_pairs={{0,1},{1,0},{2,3},{3,2},{4,5},{5,4},{6,7},{7,6},{8,9},{9,8},{10,11... | collective-permute-start | bytes 786440 | tf_op jit(solution)/shard_map/ppermute | solution.py:16
  5.8 19.2 %collective-permute-start.8 = (f32[128,256]{1,0:T(8,128)S(1)}, f32[128,256]{1,0:T(8,128)S(1)}, u32[]{:S(2)}, u32[]{:S(2)}) collective-permute-start(f32[128,256]{1,0:T(8,128)S(1)} %get-tuple-element.58), channel_id=1, source_target_pairs={{0,8},{4,12},{8,0},{12,4},{1,9},{5,13},{9,1},{13,5},{2,10},{6,14},... | collective-permute-start | bytes 393224 | tf_op jit(solution)/shard_map/ppermute | solution.py:16
  9.4 4.0 %copy-start.1 = (bf16[1,768,1280]{2,1,0:T(8,128)(2,1)S(1)}, bf16[1,768,1280]{2,1,0:T(8,128)(2,1)}, u32[]{:S(2)}) copy-start(bf16[1,768,1280]{2,1,0:T(8,128)(2,1)} %param.5) | copy-start | bytes 5898244
  9.6 11.3 %collective-permute-start.2 = (f32[4,64,256]{2,1,0:T(8,128)S(1)}, f32[4,64,256]{2,1,0:T(8,128)S(1)}, u32[]{:S(2)}, u32[]{:S(2)}) collective-permute-start(f32[4,64,256]{2,1,0:T(8,128)S(1)} %dynamic-slice_bitcast_fusion), channel_id=1, source_target_pairs={{0,2},{1,3},{2,0},{3,1},{4,6},{5,7},{6,4},{7,5},{8,10},{9,11},{10,... | collective-permute-start | bytes 786440 | tf_op jit(solution)/shard_map/ppermute | solution.py:16
  11.1 13.8 %collective-permute-start.9 = (f32[128,256]{1,0:T(8,128)S(1)}, f32[128,256]{1,0:T(8,128)S(1)}, u32[]{:S(2)}, u32[]{:S(2)}) collective-permute-start(f32[128,256]{1,0:T(8,128)S(1)} %get-tuple-element.57), channel_id=1, source_target_pairs={{0,12},{4,8},{8,4},{12,0},{1,13},{5,9},{9,5},{13,1},{2,14},{6,10},... | collective-permute-start | bytes 393224 | tf_op jit(solution)/shard_map/ppermute | solution.py:16
  12.8 12.2 %collective-permute-start.10 = (f32[128,256]{1,0:T(8,128)S(1)}, f32[128,256]{1,0:T(8,128)S(1)}, u32[]{:S(2)}, u32[]{:S(2)}) collective-permute-start(f32[128,256]{1,0:T(8,128)S(1)} %get-tuple-element.56), channel_id=1, source_target_pairs={{0,4},{4,0},{8,12},{12,8},{1,5},{5,1},{9,13},{13,9},{2,6},{6,2},{1... | collective-permute-start | bytes 393224 | tf_op jit(solution)/shard_map/ppermute | solution.py:16
  12.8 8.0 %collective-permute-start.4 = (f32[4,64,128]{2,1,0:T(8,128)S(1)}, f32[4,64,128]{2,1,0:T(8,128)S(1)}, u32[]{:S(2)}, u32[]{:S(2)}) collective-permute-start(f32[4,64,128]{2,1,0:T(8,128)S(1)} %dynamic-slice_bitcast_fusion.1), channel_id=1, source_target_pairs={{0,2},{1,3},{2,0},{3,1},{4,6},{5,7},{6,4},{7,5},{8,10},{9,11},{10,... | collective-permute-start | bytes 393224 | tf_op jit(solution)/shard_map/ppermute | solution.py:16
  20.9 10.3 %collective-permute-start.5 = (f32[64,384]{1,0:T(8,128)S(1)}, f32[64,384]{1,0:T(8,128)S(1)}, u32[]{:S(2)}, u32[]{:S(2)}) collective-permute-start(f32[64,384]{1,0:T(8,128)S(1)} %get-tuple-element.59), channel_id=1, source_target_pairs={{0,8},{4,12},{8,0},{12,4},{1,9},{5,13},{9,1},{13,5},{2,10},{6,14},... | collective-permute-start | bytes 294920 | tf_op jit(solution)/shard_map/ppermute | solution.py:16
  21.8 9.5 %collective-permute-start.6 = (f32[64,384]{1,0:T(8,128)S(1)}, f32[64,384]{1,0:T(8,128)S(1)}, u32[]{:S(2)}, u32[]{:S(2)}) collective-permute-start(f32[64,384]{1,0:T(8,128)S(1)} %get-tuple-element.60), channel_id=1, source_target_pairs={{0,12},{4,8},{8,4},{12,0},{1,13},{5,9},{9,5},{13,1},{2,14},{6,10},... | collective-permute-start | bytes 294920 | tf_op jit(solution)/shard_map/ppermute | solution.py:16
  25.0 6.5 %collective-permute-start.7 = (f32[64,384]{1,0:T(8,128)S(1)}, f32[64,384]{1,0:T(8,128)S(1)}, u32[]{:S(2)}, u32[]{:S(2)}) collective-permute-start(f32[64,384]{1,0:T(8,128)S(1)} %get-tuple-element.61), channel_id=1, source_target_pairs={{0,4},{4,0},{8,12},{12,8},{1,5},{5,1},{9,13},{13,9},{2,6},{6,2},{1... | collective-permute-start | bytes 294920 | tf_op jit(solution)/shard_map/ppermute | solution.py:16
  25.0 8.1 %collective-permute-start.11 = (f32[128,256]{1,0:T(8,128)S(1)}, f32[128,256]{1,0:T(8,128)S(1)}, u32[]{:S(2)}, u32[]{:S(2)}) collective-permute-start(f32[128,256]{1,0:T(8,128)S(1)} %fusion.2), channel_id=1, source_target_pairs={{0,2},{1,3},{2,0},{3,1},{4,6},{5,7},{6,4},{7,5},{8,10},{9,11},{10,... | collective-permute-start | bytes 393224 | tf_op jit(solution)/shard_map/ppermute | solution.py:16
  31.5 13.4 %collective-permute-start.13 = (f32[64,384]{1,0:T(8,128)S(1)}, f32[64,384]{1,0:T(8,128)S(1)}, u32[]{:S(2)}, u32[]{:S(2)}) collective-permute-start(f32[64,384]{1,0:T(8,128)S(1)} %get-tuple-element.55.early), channel_id=1, source_target_pairs={{0,2},{1,3},{2,0},{3,1},{4,6},{5,7},{6,4},{7,5},{8,10},{9,11},{10,... | collective-permute-start | bytes 294920 | tf_op jit(solution)/shard_map/ppermute | solution.py:16
  33.1 11.9 %collective-permute-start.14 = (f32[64,384]{1,0:T(8,128)S(1)}, f32[64,384]{1,0:T(8,128)S(1)}, u32[]{:S(2)}, u32[]{:S(2)}) collective-permute-start(f32[64,384]{1,0:T(8,128)S(1)} %get-tuple-element.55.early), channel_id=1, source_target_pairs={{0,3},{1,2},{2,1},{3,0},{4,7},{5,6},{6,5},{7,4},{8,11},{9,10},{10,... | collective-permute-start | bytes 294920 | tf_op jit(solution)/shard_map/ppermute | solution.py:16
  33.2 11.8 %collective-permute-start.12 = (f32[64,896]{1,0:T(8,128)S(1)}, f32[64,896]{1,0:T(8,128)S(1)}, u32[]{:S(2)}, u32[]{:S(2)}) collective-permute-start(f32[64,896]{1,0:T(8,128)S(1)} %pad_maximum_fusion), channel_id=1, source_target_pairs={{0,1},{1,0},{2,3},{3,2},{4,5},{5,4},{6,7},{7,6},{8,9},{9,8},{10,11... | collective-permute-start | bytes 688136 | tf_op jit(solution)/shard_map/ppermute | solution.py:16

commit v7 on v6

--- a/solution.py
+++ b/solution.py
@@ -55,55 +55,40 @@
     )
 
 
-def first_kernel(widths, count, place, act, dy, out, masked, x, y, tokens, middle_dy, sems):
-    side, middle, last = widths
-    core = place[0] % CORES
-    other = pl.multiple_of((1 - core) * sum(widths), 128)
-    mine = pl.multiple_of(core * sum(widths), 128)
-    moves = [
-        (other + side, middle_dy, 0, middle),
-        (other, x, 0, side),
-        (mine + side, x, side, middle),
-        (mine, y, 0, side),
-        (other + side + middle, y, side, last),
-        (mine + side + middle, y, side + last, last),
+def first_kernel(start, count, place, act, dy, out, masked, tokens, columns, sems):
+    width = columns.shape[1]
+    half = dy.shape[1] // CORES
+    column = pl.multiple_of((1 - place[0] % CORES) * half + start, 128)
+    copies = [
+        pltpu.make_async_copy(act, tokens, sems.at[0]),
+        pltpu.make_async_copy(dy.at[:, pl.ds(column, width)], columns, sems.at[1]),
     ]
-    copies = [pltpu.make_async_copy(act, tokens, sems.at[0])]
-    for column, target, start, width in moves:
-        source = dy.at[:, pl.ds(column, width)]
-        target = target.at[:, start : start + width]
-        copies.append(pltpu.make_async_copy(source, target, sems.at[len(copies)]))
     for copy in copies:
         copy.start()
     copies[0].wait()
     live = lax.broadcasted_iota(jnp.int32, (act.shape[0], 1), 0) < count[0, 0, 0]
     masked[...] = jnp.where(live, tokens[...], jnp.zeros_like(tokens))
     copies[1].wait()
-    out[...] = product(masked[...], middle_dy[...])
-    for copy in copies[2:]:
-        copy.wait()
-
-
-def first_term(counts, place, act, dy, widths):
+    out[...] = product(masked[...], columns[...])
+
+
+def first_term(counts, place, act, dy, start, width):
     rows, hidden = act.shape
-    side, middle, last = widths
     smem = pl.BlockSpec(memory_space=pltpu.SMEM)
     vmem = pl.BlockSpec(memory_space=pltpu.VMEM)
     hbm = pl.BlockSpec(memory_space=pltpu.HBM)
     return pl.pallas_call(
-        functools.partial(first_kernel, widths),
+        functools.partial(first_kernel, start),
         out_shape=(
-            jax.ShapeDtypeStruct((hidden, middle), jnp.float32),
+            jax.ShapeDtypeStruct((hidden, width), jnp.float32),
             jax.ShapeDtypeStruct((rows, hidden), act.dtype),
-            jax.ShapeDtypeStruct((rows, side + middle), dy.dtype),
-            jax.ShapeDtypeStruct((rows, side + 2 * last), dy.dtype),
         ),
         in_specs=[smem, smem, hbm, hbm],
-        out_specs=(vmem,) * 4,
+        out_specs=(vmem,) * 2,
         scratch_shapes=[
             pltpu.VMEM((rows, hidden), act.dtype),
-            pltpu.VMEM((rows, middle), dy.dtype),
-            pltpu.SemaphoreType.DMA((7,)),
+            pltpu.VMEM((rows, width), dy.dtype),
+            pltpu.SemaphoreType.DMA((2,)),
         ],
         compiler_params=pltpu.CompilerParams(vmem_limit_bytes=VMEM_BYTES),
     )(
@@ -114,24 +99,24 @@
     )
 
 
-def terms_kernel(masked, columns, *outs):
-    start = 0
-    for out in outs:
-        width = out.shape[1]
-        out[...] = product(masked[...], columns[:, start : start + width])
-        start += width
-
-
-def terms(masked, columns, *widths):
+def terms_kernel(spans, place, masked, dy, *outs):
+    half = dy.shape[1] // CORES
+    core = place[0] % CORES
+    for (own, start), out in zip(spans, outs):
+        column = pl.multiple_of((core if own else 1 - core) * half + start, 128)
+        out[...] = product(masked[...], dy[:, pl.ds(column, out.shape[1])])
+
+
+def terms(place, masked, dy, *spans):
     vmem = pl.BlockSpec(memory_space=pltpu.VMEM)
     hidden = masked.shape[1]
     return pl.pallas_call(
-        terms_kernel,
-        out_shape=tuple(jax.ShapeDtypeStruct((hidden, w), jnp.float32) for w in widths),
-        in_specs=[vmem, vmem],
-        out_specs=(vmem,) * len(widths),
+        functools.partial(terms_kernel, [span[:2] for span in spans]),
+        out_shape=tuple(jax.ShapeDtypeStruct((hidden, span[2]), jnp.float32) for span in spans),
+        in_specs=[pl.BlockSpec(memory_space=pltpu.SMEM), vmem, vmem],
+        out_specs=(vmem,) * len(spans),
         compiler_params=pltpu.CompilerParams(vmem_limit_bytes=VMEM_BYTES),
-    )(masked, columns)
+    )(place, masked, dy)
 
 
 def scaled_kernel(entries, side, place, totals, late, early, parcel, *refs):
@@ -204,14 +189,21 @@
     def by_row_part(x):
         return x.reshape(n_loop, n_y, own_rows // n_y, -1).transpose(1, 0, 2, 3)
 
-    late_other, masked, columns, more_columns = first_term(
-        counts, place, tokens, upstream, widths
-    )
+    side, middle, last = widths
+    late_other, masked = first_term(counts, place, tokens, upstream, side, middle)
     late_other = swap(late_other, "line", 1)
-    first_other, late = terms(masked, columns, *widths[:2])
+    first_other, late = terms(
+        place, masked, upstream, (False, 0, side), (True, side, middle)
+    )
     first_other = swap(first_other, "line", 1)
-    first_sum, second_both = terms(masked, more_columns, widths[0], 2 * widths[2])
-    second_other, second_sum = second_both[:, : widths[2]], second_both[:, widths[2] :]
+    first_sum, second_other, second_sum = terms(
+        place,
+        masked,
+        upstream,
+        (True, 0, side),
+        (False, side + middle, last),
+        (True, side + middle, last),
+    )
     second_other = swap(second_other, "line", 1)
     late = (late + late_other).reshape(n_loop, own_rows, widths[1])
     late_sends = parcels(late, over_z)
@@ -254,8 +246,9 @@
     total = after(total, hidden_grad)
     height = own_rows // n_y
     rows_late = [late[start : start + height] for start in range(0, own_rows, height)]
-    parcel = swap(jnp.concatenate([early, *rows_late], axis=1), "line", 1)
-    far = [swap(early, "line", d) for d in range(CORES, n_y * CORES)]
+    parcel = jnp.concatenate([early, *rows_late], axis=1)
+    far = [swap(after(early, parcel), "line", d) for d in range(CORES, n_y * CORES)]
+    parcel = swap(parcel, "line", 1)
     everyone = ("mod", "loop", "line")
     members = lax.axis_size(everyone)
     totals = lax.all_to_all(

time: 46.3 us -> 46.3 us (level)
  no operation moved by 1% of the time
where the time goes in v7:
time: 46.3 us; the launch traced here: 46.1 us
  starting transfers between devices  16.4 us (35%)
  blocking collectives  10.9 us (24%)
  waiting for transfers between devices  10.3 us (22%)
  Pallas kernels  4.3 us (9%)
  matrix products  2.09 us (5%)
  between operations  1.58 us (3%)
    ppermute x15, starting transfers between devices, swap(): return lax.ppermute(x, axis, [(i, i ^ distance) for i in range(size)])  16.4 us
    all_to_all x1, blocking collectives, on_device(): lax.all_to_all(jnp.broadcast_to(total[None], (members, 1, 128)), everyone...  10.9 us
    ppermute x15, waiting for transfers between devices, swap(): return lax.ppermute(x, axis, [(i, i ^ distance) for i in range(size)])  10.3 us
    dot_general x1, matrix products, on_device(): lax.dot_general(after(upstream, *sends.values()), weight, (((1,), (1,)),...  2.09 us
    pallas_call x1, Pallas kernels, first_term(): pl.pallas_call(functools.partial(first_kernel, start), out_shape=(jax.Sha...  1.73 us
    pallas_call x2, Pallas kernels, terms(): pl.pallas_call(functools.partial(terms_kernel, [span[:2] for span in span...  1.45 us
    pallas_call x1, Pallas kernels, scaled(): pl.pallas_call(functools.partial(scaled_kernel, entries, side), out_shape...  1.12 us
  transfers between devices with their start and end apart: 15, of which 3 were waited for; matrix products, arithmetic and copies ran while one was open for 6% of the time, Pallas kernels for 3%

profile of v7, /device:TPU:0, one launch (start us, length us, event | category | flops | bytes accessed | tf_op | source)
XLA Modules:
  0.0 46.1 jit_solution(15174790743057263060)
XLA Ops:
  0.6 0.0 copy-start
  0.6 0.0 copy-start.1
  1.5 1.7 %shard_map.59 = (f32[512,256]{1,0:T(8,128)S(1)}, bf16[768,512]{1,0:T(8,128)(2,1)S(1)}) custom-call(s32[1,1,1]{2,1,0:T(1,128)} %copy.6.count, s32[1]{0:T(128)} %bitcast.place, bf16[768,512]{1,0:T(8,128)(2,1)} %bitcast.68, bf16[768,1280]{1,0:T(8,128)(2,1)} %bitcast.57), custom_call_target="tpu_custom_call" | custom-call | tf_op jit(solution)/shard_map/pallas_call | solution.py:80
  3.2 0.5 %collective-permute-start.1 = (f32[512,256]{1,0:T(8,128)S(1)}, f32[512,256]{1,0:T(8,128)S(1)}, u32[]{:S(2)}, u32[]{:S(2)}) collective-permute-start(f32[512,256]{1,0:T(8,128)S(1)} %get-tuple-element.32), channel_id=1, source_target_pairs={{0,1},{1,0},{2,3},{3,2},{4,5},{5,4},{6,7},{7,6},{8,9},{9,8},{10,11... | collective-permute-start | bytes 1572872 | tf_op jit(solution)/shard_map/ppermute | solution.py:16
  3.7 0.0 copy-done.1
  3.7 0.6 %shard_map.61 = (f32[512,256]{1,0:T(8,128)S(1)}, f32[512,256]{1,0:T(8,128)S(1)}) custom-call(s32[1]{0:T(128)} %bitcast.place, bf16[768,512]{1,0:T(8,128)(2,1)S(1)} %get-tuple-element.28.masked, bf16[768,1280]{1,0:T(8,128)(2,1)S(1)} %bitcast.58), custom_call_target="tpu_custom_call" | custom-call | tf_op jit(solution)/shard_map/pallas_call | solution.py:113
  4.4 0.1 collective-permute-start
  4.5 0.8 %shard_map.60 = (f32[512,256]{1,0:T(8,128)S(1)}, f32[512,128]{1,0:T(8,128)S(1)}, f32[512,128]{1,0:T(8,128)S(1)}) custom-call(s32[1]{0:T(128)} %bitcast.place, bf16[768,512]{1,0:T(8,128)(2,1)S(1)} %get-tuple-element.28.masked, bf16[768,1280]{1,0:T(8,128)(2,1)S(1)} %bitcast.59), custom_call_target="tpu_custom_call" | custom-call | tf_op jit(solution)/shard_map/pallas_call | solution.py:113
  5.3 0.5 %collective-permute-start.3 = (f32[512,128]{1,0:T(8,128)S(1)}, f32[512,128]{1,0:T(8,128)S(1)}, u32[]{:S(2)}, u32[]{:S(2)}) collective-permute-start(f32[512,128]{1,0:T(8,128)S(1)} %get-tuple-element.38), channel_id=1, source_target_pairs={{0,1},{1,0},{2,3},{3,2},{4,5},{5,4},{6,7},{7,6},{8,9},{9,8},{10,11... | collective-permute-start | bytes 786440 | tf_op jit(solution)/shard_map/ppermute | solution.py:16
  5.8 0.0 collective-permute-done.1
  5.8 0.1 add.49
  6.0 3.7 %collective-permute-start.8 = (f32[128,256]{1,0:T(8,128)S(1)}, f32[128,256]{1,0:T(8,128)S(1)}, u32[]{:S(2)}, u32[]{:S(2)}) collective-permute-start(f32[128,256]{1,0:T(8,128)S(1)} %get-tuple-element.58), channel_id=1, source_target_pairs={{0,8},{4,12},{8,0},{12,4},{1,9},{5,13},{9,1},{13,5},{2,10},{6,14},... | collective-permute-start | bytes 393224 | tf_op jit(solution)/shard_map/ppermute | solution.py:16
  9.6 0.0 collective-permute-done
  9.6 0.1 add.50
  9.7 1.6 %collective-permute-start.2 = (f32[4,64,256]{2,1,0:T(8,128)S(1)}, f32[4,64,256]{2,1,0:T(8,128)S(1)}, u32[]{:S(2)}, u32[]{:S(2)}) collective-permute-start(f32[4,64,256]{2,1,0:T(8,128)S(1)} %dynamic-slice_bitcast_fusion), channel_id=1, source_target_pairs={{0,2},{1,3},{2,0},{3,1},{4,6},{5,7},{6,4},{7,5},{8,10},{9,11},{10,... | collective-permute-start | bytes 786440 | tf_op jit(solution)/shard_map/ppermute | solution.py:16
  11.3 1.4 %collective-permute-start.9 = (f32[128,256]{1,0:T(8,128)S(1)}, f32[128,256]{1,0:T(8,128)S(1)}, u32[]{:S(2)}, u32[]{:S(2)}) collective-permute-start(f32[128,256]{1,0:T(8,128)S(1)} %get-tuple-element.57), channel_id=1, source_target_pairs={{0,12},{4,8},{8,4},{12,0},{1,13},{5,9},{9,5},{13,1},{2,14},{6,10},... | collective-permute-start | bytes 393224 | tf_op jit(solution)/shard_map/ppermute | solution.py:16
  12.8 0.1 collective-permute-start.10
  12.9 0.0 collective-permute-done.3
  13.0 0.6 %collective-permute-start.4 = (f32[4,64,128]{2,1,0:T(8,128)S(1)}, f32[4,64,128]{2,1,0:T(8,128)S(1)}, u32[]{:S(2)}, u32[]{:S(2)}) collective-permute-start(f32[4,64,128]{2,1,0:T(8,128)S(1)} %dynamic-slice_bitcast_fusion.1), channel_id=1, source_target_pairs={{0,2},{1,3},{2,0},{3,1},{4,6},{5,7},{6,4},{7,5},{8,10},{9,11},{10,... | collective-permute-start | bytes 393224 | tf_op jit(solution)/shard_map/ppermute | solution.py:16
  13.5 0.0 copy-done
  13.5 2.1 %select_convert_fusion = bf16[768,512]{1,0:T(8,128)(2,1)} fusion(bf16[768,1280]{1,0:T(8,128)(2,1)S(1)} %bitcast.60, bf16[1,512,1280]{2,1,0:T(8,128)(2,1)S(1)} %copy-done, pred[768]{0:T(1024)(128)(4,1)S(1)} %iota_compare_fusion), kind=kOutput, calls=%fused_computation | convolution fusion | flops 1007419392 | bytes 4064000 | tf_op jit(solution)/shard_map/dot_general | solution.py:219
  15.6 5.4 %collective-permute-done.4 = f32[4,64,128]{2,1,0:T(8,128)S(1)} collective-permute-done((f32[4,64,128]{2,1,0:T(8,128)S(1)}, f32[4,64,128]{2,1,0:T(8,128)S(1)}, u32[]{:S(2)}, u32[]{:S(2)}) %collective-permute-start.4) | collective-permute-done | bytes 131104 | tf_op jit(solution)/shard_map/ppermute | solution.py:16
  21.0 0.0 collective-permute-done.2
  21.1 0.7 %collective-permute-start.5 = (f32[64,384]{1,0:T(8,128)S(1)}, f32[64,384]{1,0:T(8,128)S(1)}, u32[]{:S(2)}, u32[]{:S(2)}) collective-permute-start(f32[64,384]{1,0:T(8,128)S(1)} %get-tuple-element.59), channel_id=1, source_target_pairs={{0,8},{4,12},{8,0},{12,4},{1,9},{5,13},{9,1},{13,5},{2,10},{6,14},... | collective-permute-start | bytes 294920 | tf_op jit(solution)/shard_map/ppermute | solution.py:16
  21.8 3.3 %collective-permute-start.6 = (f32[64,384]{1,0:T(8,128)S(1)}, f32[64,384]{1,0:T(8,128)S(1)}, u32[]{:S(2)}, u32[]{:S(2)}) collective-permute-start(f32[64,384]{1,0:T(8,128)S(1)} %get-tuple-element.60), channel_id=1, source_target_pairs={{0,12},{4,8},{8,4},{12,0},{1,13},{5,9},{9,5},{13,1},{2,14},{6,10},... | collective-permute-start | bytes 294920 | tf_op jit(solution)/shard_map/ppermute | solution.py:16
  25.1 0.0 collective-permute-done.8
  25.1 0.0 collective-permute-start.7
  25.1 0.0 collective-permute-done.9
  25.1 0.0 collective-permute-done.10
  25.2 1.6 %collective-permute-start.11 = (f32[128,256]{1,0:T(8,128)S(1)}, f32[128,256]{1,0:T(8,128)S(1)}, u32[]{:S(2)}, u32[]{:S(2)}) collective-permute-start(f32[128,256]{1,0:T(8,128)S(1)} %fusion.2), channel_id=1, source_target_pairs={{0,2},{1,3},{2,0},{3,1},{4,6},{5,7},{6,4},{7,5},{8,10},{9,11},{10,... | collective-permute-start | bytes 393224 | tf_op jit(solution)/shard_map/ppermute | solution.py:16
  26.8 4.7 %collective-permute-done.5 = f32[64,384]{1,0:T(8,128)S(1)} collective-permute-done((f32[64,384]{1,0:T(8,128)S(1)}, f32[64,384]{1,0:T(8,128)S(1)}, u32[]{:S(2)}, u32[]{:S(2)}) %collective-permute-start.5) | collective-permute-done | bytes 98336 | tf_op jit(solution)/shard_map/ppermute | solution.py:16
  31.4 0.0 collective-permute-done.6
  31.4 0.2 collective-permute-done.7
  31.7 0.0 collective-permute-done.11
  31.8 1.6 %collective-permute-start.13 = (f32[64,384]{1,0:T(8,128)S(1)}, f32[64,384]{1,0:T(8,128)S(1)}, u32[]{:S(2)}, u32[]{:S(2)}) collective-permute-start(f32[64,384]{1,0:T(8,128)S(1)} %get-tuple-element.51.early), channel_id=1, source_target_pairs={{0,2},{1,3},{2,0},{3,1},{4,6},{5,7},{6,4},{7,5},{8,10},{9,11},{10,... | collective-permute-start | bytes 294920 | tf_op jit(solution)/shard_map/ppermute | solution.py:16
  33.4 0.0 collective-permute-start.14
  33.4 0.6 %collective-permute-start.12 = (f32[64,896]{1,0:T(8,128)S(1)}, f32[64,896]{1,0:T(8,128)S(1)}, u32[]{:S(2)}, u32[]{:S(2)}) collective-permute-start(f32[64,896]{1,0:T(8,128)S(1)} %pad_maximum_fusion), channel_id=1, source_target_pairs={{0,1},{1,0},{2,3},{3,2},{4,5},{5,4},{6,7},{7,6},{8,9},{9,8},{10,11... | collective-permute-start | bytes 688136 | tf_op jit(solution)/shard_map/ppermute | solution.py:16
  34.1 10.9 %all_to_all.5 = f32[32,1,128]{2,1,0:T(1,128)S(1)} all-to-all(f32[32,1,128]{2,1,0:T(1,128)S(1)} %broadcast_in_dim.33), channel_id=1, replica_groups=mesh['mod'=2,'loop'=4,'line'=4] {'mod','loop','line'}, dimensions={0} | all-to-all | bytes 32768 | tf_op jit(solution)/shard_map/all_to_all | solution.py:254
  45.0 0.0 collective-permute-done.13.refs_0_
  45.0 0.0 collective-permute-done.14.refs_1_
  45.0 0.0 collective-permute-done.12.parcel
  45.0 1.1 %shard_map.62 = f32[128,1280]{1,0:T(8,128)} custom-call(s32[1]{0:T(128)} %bitcast.place, f32[32,128]{1,0:T(8,128)S(1)} %bitcast.61, f32[128,256]{1,0:T(8,128)S(1)} %get-tuple-element.53.late, f32[64,384]{1,0:T(8,128)S(1)} %get-tuple-element.51.early, f32[64,896]{1,0:T(8,128)S(1)} %collective-permute-done.12.parcel, ...), custom_call_target="tpu_custom_call" | custom-call | tf_op jit(solution)/shard_map/pallas_call | solution.py:152
  (17 shorter events, 0.4 us)
Async XLA Ops:
  0.6 12.9 %copy-start = (bf16[1,512,1280]{2,1,0:T(8,128)(2,1)S(1)}, bf16[1,512,1280]{2,1,0:T(8,128)(2,1)}, u32[]{:S(2)}) copy-start(bf16[1,512,1280]{2,1,0:T(8,128)(2,1)} %param.6) | copy-start | bytes 3932164
  0.6 3.1 %copy-start.1 = (bf16[1,768,1280]{2,1,0:T(8,128)(2,1)S(1)}, bf16[1,768,1280]{2,1,0:T(8,128)(2,1)}, u32[]{:S(2)}) copy-start(bf16[1,768,1280]{2,1,0:T(8,128)(2,1)} %param.5) | copy-start | bytes 5898244
  3.2 2.6 %collective-permute-start.1 = (f32[512,256]{1,0:T(8,128)S(1)}, f32[512,256]{1,0:T(8,128)S(1)}, u32[]{:S(2)}, u32[]{:S(2)}) collective-permute-start(f32[512,256]{1,0:T(8,128)S(1)} %get-tuple-element.32), channel_id=1, source_target_pairs={{0,1},{1,0},{2,3},{3,2},{4,5},{5,4},{6,7},{7,6},{8,9},{9,8},{10,11... | collective-permute-start | bytes 1572872 | tf_op jit(solution)/shard_map/ppermute | solution.py:16
  4.4 5.3 %collective-permute-start = (f32[512,256]{1,0:T(8,128)S(1)}, f32[512,256]{1,0:T(8,128)S(1)}, u32[]{:S(2)}, u32[]{:S(2)}) collective-permute-start(f32[512,256]{1,0:T(8,128)S(1)} %get-tuple-element.30), channel_id=1, source_target_pairs={{0,1},{1,0},{2,3},{3,2},{4,5},{5,4},{6,7},{7,6},{8,9},{9,8},{10,11... | collective-permute-start | bytes 1572872 | tf_op jit(solution)/shard_map/ppermute | solution.py:16
  5.3 7.6 %collective-permute-start.3 = (f32[512,128]{1,0:T(8,128)S(1)}, f32[512,128]{1,0:T(8,128)S(1)}, u32[]{:S(2)}, u32[]{:S(2)}) collective-permute-start(f32[512,128]{1,0:T(8,128)S(1)} %get-tuple-element.38), channel_id=1, source_target_pairs={{0,1},{1,0},{2,3},{3,2},{4,5},{5,4},{6,7},{7,6},{8,9},{9,8},{10,11... | collective-permute-start | bytes 786440 | tf_op jit(solution)/shard_map/ppermute | solution.py:16
  6.0 19.2 %collective-permute-start.8 = (f32[128,256]{1,0:T(8,128)S(1)}, f32[128,256]{1,0:T(8,128)S(1)}, u32[]{:S(2)}, u32[]{:S(2)}) collective-permute-start(f32[128,256]{1,0:T(8,128)S(1)} %get-tuple-element.58), channel_id=1, source_target_pairs={{0,8},{4,12},{8,0},{12,4},{1,9},{5,13},{9,1},{13,5},{2,10},{6,14},... | collective-permute-start | bytes 393224 | tf_op jit(solution)/shard_map/ppermute | solution.py:16
  9.7 11.3 %collective-permute-start.2 = (f32[4,64,256]{2,1,0:T(8,128)S(1)}, f32[4,64,256]{2,1,0:T(8,128)S(1)}, u32[]{:S(2)}, u32[]{:S(2)}) collective-permute-start(f32[4,64,256]{2,1,0:T(8,128)S(1)} %dynamic-slice_bitcast_fusion), channel_id=1, source_target_pairs={{0,2},{1,3},{2,0},{3,1},{4,6},{5,7},{6,4},{7,5},{8,10},{9,11},{10,... | collective-permute-start | bytes 786440 | tf_op jit(solution)/shard_map/ppermute | solution.py:16
  11.3 13.8 %collective-permute-start.9 = (f32[128,256]{1,0:T(8,128)S(1)}, f32[128,256]{1,0:T(8,128)S(1)}, u32[]{:S(2)}, u32[]{:S(2)}) collective-permute-start(f32[128,256]{1,0:T(8,128)S(1)} %get-tuple-element.57), channel_id=1, source_target_pairs={{0,12},{4,8},{8,4},{12,0},{1,13},{5,9},{9,5},{13,1},{2,14},{6,10},... | collective-permute-start | bytes 393224 | tf_op jit(solution)/shard_map/ppermute | solution.py:16
  12.8 12.4 %collective-permute-start.10 = (f32[128,256]{1,0:T(8,128)S(1)}, f32[128,256]{1,0:T(8,128)S(1)}, u32[]{:S(2)}, u32[]{:S(2)}) collective-permute-start(f32[128,256]{1,0:T(8,128)S(1)} %get-tuple-element.56), channel_id=1, source_target_pairs={{0,4},{4,0},{8,12},{12,8},{1,5},{5,1},{9,13},{13,9},{2,6},{6,2},{1... | collective-permute-start | bytes 393224 | tf_op jit(solution)/shard_map/ppermute | solution.py:16
  13.0 8.1 %collective-permute-start.4 = (f32[4,64,128]{2,1,0:T(8,128)S(1)}, f32[4,64,128]{2,1,0:T(8,128)S(1)}, u32[]{:S(2)}, u32[]{:S(2)}) collective-permute-start(f32[4,64,128]{2,1,0:T(8,128)S(1)} %dynamic-slice_bitcast_fusion.1), channel_id=1, source_target_pairs={{0,2},{1,3},{2,0},{3,1},{4,6},{5,7},{6,4},{7,5},{8,10},{9,11},{10,... | collective-permute-start | bytes 393224 | tf_op jit(solution)/shard_map/ppermute | solution.py:16
  21.1 10.3 %collective-permute-start.5 = (f32[64,384]{1,0:T(8,128)S(1)}, f32[64,384]{1,0:T(8,128)S(1)}, u32[]{:S(2)}, u32[]{:S(2)}) collective-permute-start(f32[64,384]{1,0:T(8,128)S(1)} %get-tuple-element.59), channel_id=1, source_target_pairs={{0,8},{4,12},{8,0},{12,4},{1,9},{5,13},{9,1},{13,5},{2,10},{6,14},... | collective-permute-start | bytes 294920 | tf_op jit(solution)/shard_map/ppermute | solution.py:16
  21.8 9.7 %collective-permute-start.6 = (f32[64,384]{1,0:T(8,128)S(1)}, f32[64,384]{1,0:T(8,128)S(1)}, u32[]{:S(2)}, u32[]{:S(2)}) collective-permute-start(f32[64,384]{1,0:T(8,128)S(1)} %get-tuple-element.60), channel_id=1, source_target_pairs={{0,12},{4,8},{8,4},{12,0},{1,13},{5,9},{9,5},{13,1},{2,14},{6,10},... | collective-permute-start | bytes 294920 | tf_op jit(solution)/shard_map/ppermute | solution.py:16
  25.1 6.5 %collective-permute-start.7 = (f32[64,384]{1,0:T(8,128)S(1)}, f32[64,384]{1,0:T(8,128)S(1)}, u32[]{:S(2)}, u32[]{:S(2)}) collective-permute-start(f32[64,384]{1,0:T(8,128)S(1)} %get-tuple-element.61), channel_id=1, source_target_pairs={{0,4},{4,0},{8,12},{12,8},{1,5},{5,1},{9,13},{13,9},{2,6},{6,2},{1... | collective-permute-start | bytes 294920 | tf_op jit(solution)/shard_map/ppermute | solution.py:16
  25.2 6.5 %collective-permute-start.11 = (f32[128,256]{1,0:T(8,128)S(1)}, f32[128,256]{1,0:T(8,128)S(1)}, u32[]{:S(2)}, u32[]{:S(2)}) collective-permute-start(f32[128,256]{1,0:T(8,128)S(1)} %fusion.2), channel_id=1, source_target_pairs={{0,2},{1,3},{2,0},{3,1},{4,6},{5,7},{6,4},{7,5},{8,10},{9,11},{10,... | collective-permute-start | bytes 393224 | tf_op jit(solution)/shard_map/ppermute | solution.py:16
  31.8 13.1 %collective-permute-start.13 = (f32[64,384]{1,0:T(8,128)S(1)}, f32[64,384]{1,0:T(8,128)S(1)}, u32[]{:S(2)}, u32[]{:S(2)}) collective-permute-start(f32[64,384]{1,0:T(8,128)S(1)} %get-tuple-element.51.early), channel_id=1, source_target_pairs={{0,2},{1,3},{2,0},{3,1},{4,6},{5,7},{6,4},{7,5},{8,10},{9,11},{10,... | collective-permute-start | bytes 294920 | tf_op jit(solution)/shard_map/ppermute | solution.py:16
  33.4 11.6 %collective-permute-start.14 = (f32[64,384]{1,0:T(8,128)S(1)}, f32[64,384]{1,0:T(8,128)S(1)}, u32[]{:S(2)}, u32[]{:S(2)}) collective-permute-start(f32[64,384]{1,0:T(8,128)S(1)} %get-tuple-element.51.early), channel_id=1, source_target_pairs={{0,3},{1,2},{2,1},{3,0},{4,7},{5,6},{6,5},{7,4},{8,11},{9,10},{10,... | collective-permute-start | bytes 294920 | tf_op jit(solution)/shard_map/ppermute | solution.py:16
  33.4 11.6 %collective-permute-start.12 = (f32[64,896]{1,0:T(8,128)S(1)}, f32[64,896]{1,0:T(8,128)S(1)}, u32[]{:S(2)}, u32[]{:S(2)}) collective-permute-start(f32[64,896]{1,0:T(8,128)S(1)} %pad_maximum_fusion), channel_id=1, source_target_pairs={{0,1},{1,0},{2,3},{3,2},{4,5},{5,4},{6,7},{7,6},{8,9},{9,8},{10,11... | collective-permute-start | bytes 688136 | tf_op jit(solution)/shard_map/ppermute | solution.py:16

commit v8 on v7

--- a/solution.py
+++ b/solution.py
@@ -102,9 +102,19 @@
 def terms_kernel(spans, place, masked, dy, *outs):
     half = dy.shape[1] // CORES
     core = place[0] % CORES
+    columns = []
     for (own, start), out in zip(spans, outs):
         column = pl.multiple_of((core if own else 1 - core) * half + start, 128)
-        out[...] = product(masked[...], dy[:, pl.ds(column, out.shape[1])])
+        columns.append(dy[:, pl.ds(column, out.shape[1])])
+    narrow = [i for i, out in enumerate(outs) if out.shape[1] <= 128]
+    if len(narrow) == 2:
+        both = product(masked[...], jnp.concatenate([columns[i] for i in narrow], axis=1))
+        width = outs[narrow[0]].shape[1]
+        outs[narrow[0]][...] = both[:, :width]
+        outs[narrow[1]][...] = both[:, width:]
+    for i, out in enumerate(outs):
+        if len(narrow) != 2 or i not in narrow:
+            out[...] = product(masked[...], columns[i])
 
 
 def terms(place, masked, dy, *spans):

time: 46.3 us -> 46.2 us (level)
  no operation moved by 1% of the time
where the time goes in v8:
time: 46.2 us; the launch traced here: 46 us
  starting transfers between devices  16.4 us (35%)
  blocking collectives  11.1 us (24%)
  waiting for transfers between devices  10.2 us (22%)
  Pallas kernels  4.1 us (9%)
  matrix products  2.09 us (5%)
  between operations  1.58 us (3%)
    ppermute x15, starting transfers between devices, swap(): return lax.ppermute(x, axis, [(i, i ^ distance) for i in range(size)])  16.4 us
    all_to_all x1, blocking collectives, on_device(): lax.all_to_all(jnp.broadcast_to(total[None], (members, 1, 128)), everyone...  11.1 us
    ppermute x15, waiting for transfers between devices, swap(): return lax.ppermute(x, axis, [(i, i ^ distance) for i in range(size)])  10.2 us
    dot_general x1, matrix products, on_device(): lax.dot_general(after(upstream, *sends.values()), weight, (((1,), (1,)),...  2.09 us
    pallas_call x1, Pallas kernels, first_term(): pl.pallas_call(functools.partial(first_kernel, start), out_shape=(jax.Sha...  1.73 us
    pallas_call x2, Pallas kernels, terms(): pl.pallas_call(functools.partial(terms_kernel, [span[:2] for span in span...  1.25 us
    pallas_call x1, Pallas kernels, scaled(): pl.pallas_call(functools.partial(scaled_kernel, entries, side), out_shape...  1.12 us
  transfers between devices with their start and end apart: 15, of which 3 were waited for; matrix products, arithmetic and copies ran while one was open for 6% of the time, Pallas kernels for 3%

profile of v8, /device:TPU:0, one launch (start us, length us, event | category | flops | bytes accessed | tf_op | source)
XLA Modules:
  0.0 46.0 jit_solution(15978177072529701544)
XLA Ops:
  0.6 0.0 copy-start
  0.6 0.0 copy-start.1
  1.5 1.7 %shard_map.59 = (f32[512,256]{1,0:T(8,128)S(1)}, bf16[768,512]{1,0:T(8,128)(2,1)S(1)}) custom-call(s32[1,1,1]{2,1,0:T(1,128)} %copy.6.count, s32[1]{0:T(128)} %bitcast.place, bf16[768,512]{1,0:T(8,128)(2,1)} %bitcast.68, bf16[768,1280]{1,0:T(8,128)(2,1)} %bitcast.57), custom_call_target="tpu_custom_call" | custom-call | tf_op jit(solution)/shard_map/pallas_call | solution.py:80
  3.2 0.5 %collective-permute-start.1 = (f32[512,256]{1,0:T(8,128)S(1)}, f32[512,256]{1,0:T(8,128)S(1)}, u32[]{:S(2)}, u32[]{:S(2)}) collective-permute-start(f32[512,256]{1,0:T(8,128)S(1)} %get-tuple-element.32), channel_id=1, source_target_pairs={{0,1},{1,0},{2,3},{3,2},{4,5},{5,4},{6,7},{7,6},{8,9},{9,8},{10,11... | collective-permute-start | bytes 1572872 | tf_op jit(solution)/shard_map/ppermute | solution.py:16
  3.7 0.0 copy-done.1
  3.7 0.6 %shard_map.61 = (f32[512,256]{1,0:T(8,128)S(1)}, f32[512,256]{1,0:T(8,128)S(1)}) custom-call(s32[1]{0:T(128)} %bitcast.place, bf16[768,512]{1,0:T(8,128)(2,1)S(1)} %get-tuple-element.28.masked, bf16[768,1280]{1,0:T(8,128)(2,1)S(1)} %bitcast.58), custom_call_target="tpu_custom_call" | custom-call | tf_op jit(solution)/shard_map/pallas_call | solution.py:123
  4.4 0.1 collective-permute-start
  4.5 0.6 %shard_map.60 = (f32[512,256]{1,0:T(8,128)S(1)}, f32[512,128]{1,0:T(8,128)S(1)}, f32[512,128]{1,0:T(8,128)S(1)}) custom-call(s32[1]{0:T(128)} %bitcast.place, bf16[768,512]{1,0:T(8,128)(2,1)S(1)} %get-tuple-element.28.masked, bf16[768,1280]{1,0:T(8,128)(2,1)S(1)} %bitcast.59), custom_call_target="tpu_custom_call" | custom-call | tf_op jit(solution)/shard_map/pallas_call | solution.py:123
  5.1 0.5 %collective-permute-start.3 = (f32[512,128]{1,0:T(8,128)S(1)}, f32[512,128]{1,0:T(8,128)S(1)}, u32[]{:S(2)}, u32[]{:S(2)}) collective-permute-start(f32[512,128]{1,0:T(8,128)S(1)} %get-tuple-element.38), channel_id=1, source_target_pairs={{0,1},{1,0},{2,3},{3,2},{4,5},{5,4},{6,7},{7,6},{8,9},{9,8},{10,11... | collective-permute-start | bytes 786440 | tf_op jit(solution)/shard_map/ppermute | solution.py:16
  5.6 0.0 collective-permute-done.1
  5.6 0.1 add.49
  5.7 3.7 %collective-permute-start.8 = (f32[128,256]{1,0:T(8,128)S(1)}, f32[128,256]{1,0:T(8,128)S(1)}, u32[]{:S(2)}, u32[]{:S(2)}) collective-permute-start(f32[128,256]{1,0:T(8,128)S(1)} %get-tuple-element.58), channel_id=1, source_target_pairs={{0,8},{4,12},{8,0},{12,4},{1,9},{5,13},{9,1},{13,5},{2,10},{6,14},... | collective-permute-start | bytes 393224 | tf_op jit(solution)/shard_map/ppermute | solution.py:16
  9.4 0.0 collective-permute-done
  9.4 0.1 add.50
  9.5 1.6 %collective-permute-start.2 = (f32[4,64,256]{2,1,0:T(8,128)S(1)}, f32[4,64,256]{2,1,0:T(8,128)S(1)}, u32[]{:S(2)}, u32[]{:S(2)}) collective-permute-start(f32[4,64,256]{2,1,0:T(8,128)S(1)} %dynamic-slice_bitcast_fusion), channel_id=1, source_target_pairs={{0,2},{1,3},{2,0},{3,1},{4,6},{5,7},{6,4},{7,5},{8,10},{9,11},{10,... | collective-permute-start | bytes 786440 | tf_op jit(solution)/shard_map/ppermute | solution.py:16
  11.1 1.6 %collective-permute-start.9 = (f32[128,256]{1,0:T(8,128)S(1)}, f32[128,256]{1,0:T(8,128)S(1)}, u32[]{:S(2)}, u32[]{:S(2)}) collective-permute-start(f32[128,256]{1,0:T(8,128)S(1)} %get-tuple-element.57), channel_id=1, source_target_pairs={{0,12},{4,8},{8,4},{12,0},{1,13},{5,9},{9,5},{13,1},{2,14},{6,10},... | collective-permute-start | bytes 393224 | tf_op jit(solution)/shard_map/ppermute | solution.py:16
  12.8 0.0 collective-permute-start.10
  12.8 0.0 collective-permute-done.3
  12.8 0.6 %collective-permute-start.4 = (f32[4,64,128]{2,1,0:T(8,128)S(1)}, f32[4,64,128]{2,1,0:T(8,128)S(1)}, u32[]{:S(2)}, u32[]{:S(2)}) collective-permute-start(f32[4,64,128]{2,1,0:T(8,128)S(1)} %dynamic-slice_bitcast_fusion.1), channel_id=1, source_target_pairs={{0,2},{1,3},{2,0},{3,1},{4,6},{5,7},{6,4},{7,5},{8,10},{9,11},{10,... | collective-permute-start | bytes 393224 | tf_op jit(solution)/shard_map/ppermute | solution.py:16
  13.4 0.0 copy-done
  13.4 2.1 %select_convert_fusion = bf16[768,512]{1,0:T(8,128)(2,1)} fusion(bf16[768,1280]{1,0:T(8,128)(2,1)S(1)} %bitcast.60, bf16[1,512,1280]{2,1,0:T(8,128)(2,1)S(1)} %copy-done, pred[768]{0:T(1024)(128)(4,1)S(1)} %iota_compare_fusion), kind=kOutput, calls=%fused_computation | convolution fusion | flops 1007419392 | bytes 4064000 | tf_op jit(solution)/shard_map/dot_general | solution.py:229
  15.5 5.3 %collective-permute-done.4 = f32[4,64,128]{2,1,0:T(8,128)S(1)} collective-permute-done((f32[4,64,128]{2,1,0:T(8,128)S(1)}, f32[4,64,128]{2,1,0:T(8,128)S(1)}, u32[]{:S(2)}, u32[]{:S(2)}) %collective-permute-start.4) | collective-permute-done | bytes 131104 | tf_op jit(solution)/shard_map/ppermute | solution.py:16
  20.8 0.0 collective-permute-done.2
  20.9 0.9 %collective-permute-start.5 = (f32[64,384]{1,0:T(8,128)S(1)}, f32[64,384]{1,0:T(8,128)S(1)}, u32[]{:S(2)}, u32[]{:S(2)}) collective-permute-start(f32[64,384]{1,0:T(8,128)S(1)} %get-tuple-element.59), channel_id=1, source_target_pairs={{0,8},{4,12},{8,0},{12,4},{1,9},{5,13},{9,1},{13,5},{2,10},{6,14},... | collective-permute-start | bytes 294920 | tf_op jit(solution)/shard_map/ppermute | solution.py:16
  21.8 3.1 %collective-permute-start.6 = (f32[64,384]{1,0:T(8,128)S(1)}, f32[64,384]{1,0:T(8,128)S(1)}, u32[]{:S(2)}, u32[]{:S(2)}) collective-permute-start(f32[64,384]{1,0:T(8,128)S(1)} %get-tuple-element.60), channel_id=1, source_target_pairs={{0,12},{4,8},{8,4},{12,0},{1,13},{5,9},{9,5},{13,1},{2,14},{6,10},... | collective-permute-start | bytes 294920 | tf_op jit(solution)/shard_map/ppermute | solution.py:16
  24.9 0.0 collective-permute-done.8
  24.9 0.0 collective-permute-start.7
  24.9 0.0 collective-permute-done.9
  24.9 0.0 collective-permute-done.10
  25.0 1.6 %collective-permute-start.11 = (f32[128,256]{1,0:T(8,128)S(1)}, f32[128,256]{1,0:T(8,128)S(1)}, u32[]{:S(2)}, u32[]{:S(2)}) collective-permute-start(f32[128,256]{1,0:T(8,128)S(1)} %fusion.2), channel_id=1, source_target_pairs={{0,2},{1,3},{2,0},{3,1},{4,6},{5,7},{6,4},{7,5},{8,10},{9,11},{10,... | collective-permute-start | bytes 393224 | tf_op jit(solution)/shard_map/ppermute | solution.py:16
  26.6 4.7 %collective-permute-done.5 = f32[64,384]{1,0:T(8,128)S(1)} collective-permute-done((f32[64,384]{1,0:T(8,128)S(1)}, f32[64,384]{1,0:T(8,128)S(1)}, u32[]{:S(2)}, u32[]{:S(2)}) %collective-permute-start.5) | collective-permute-done | bytes 98336 | tf_op jit(solution)/shard_map/ppermute | solution.py:16
  31.2 0.0 collective-permute-done.6
  31.3 0.2 collective-permute-done.7
  31.5 0.0 collective-permute-done.11
  31.6 1.6 %collective-permute-start.13 = (f32[64,384]{1,0:T(8,128)S(1)}, f32[64,384]{1,0:T(8,128)S(1)}, u32[]{:S(2)}, u32[]{:S(2)}) collective-permute-start(f32[64,384]{1,0:T(8,128)S(1)} %get-tuple-element.51.early), channel_id=1, source_target_pairs={{0,2},{1,3},{2,0},{3,1},{4,6},{5,7},{6,4},{7,5},{8,10},{9,11},{10,... | collective-permute-start | bytes 294920 | tf_op jit(solution)/shard_map/ppermute | solution.py:16
  33.2 0.0 collective-permute-start.14
  33.2 0.6 %collective-permute-start.12 = (f32[64,896]{1,0:T(8,128)S(1)}, f32[64,896]{1,0:T(8,128)S(1)}, u32[]{:S(2)}, u32[]{:S(2)}) collective-permute-start(f32[64,896]{1,0:T(8,128)S(1)} %pad_maximum_fusion), channel_id=1, source_target_pairs={{0,1},{1,0},{2,3},{3,2},{4,5},{5,4},{6,7},{7,6},{8,9},{9,8},{10,11... | collective-permute-start | bytes 688136 | tf_op jit(solution)/shard_map/ppermute | solution.py:16
  33.9 11.1 %all_to_all.5 = f32[32,1,128]{2,1,0:T(1,128)S(1)} all-to-all(f32[32,1,128]{2,1,0:T(1,128)S(1)} %broadcast_in_dim.33), channel_id=1, replica_groups=mesh['mod'=2,'loop'=4,'line'=4] {'mod','loop','line'}, dimensions={0} | all-to-all | bytes 32768 | tf_op jit(solution)/shard_map/all_to_all | solution.py:264
  44.9 0.0 collective-permute-done.13.refs_0_
  44.9 0.0 collective-permute-done.14.refs_1_
  44.9 0.0 collective-permute-done.12.parcel
  44.9 1.1 %shard_map.62 = f32[128,1280]{1,0:T(8,128)} custom-call(s32[1]{0:T(128)} %bitcast.place, f32[32,128]{1,0:T(8,128)S(1)} %bitcast.61, f32[128,256]{1,0:T(8,128)S(1)} %get-tuple-element.53.late, f32[64,384]{1,0:T(8,128)S(1)} %get-tuple-element.51.early, f32[64,896]{1,0:T(8,128)S(1)} %collective-permute-done.12.parcel, ...), custom_call_target="tpu_custom_call" | custom-call | tf_op jit(solution)/shard_map/pallas_call | solution.py:162
  (17 shorter events, 0.4 us)
Async XLA Ops:
  0.6 12.8 %copy-start = (bf16[1,512,1280]{2,1,0:T(8,128)(2,1)S(1)}, bf16[1,512,1280]{2,1,0:T(8,128)(2,1)}, u32[]{:S(2)}) copy-start(bf16[1,512,1280]{2,1,0:T(8,128)(2,1)} %param.6) | copy-start | bytes 3932164
  0.6 3.1 %copy-start.1 = (bf16[1,768,1280]{2,1,0:T(8,128)(2,1)S(1)}, bf16[1,768,1280]{2,1,0:T(8,128)(2,1)}, u32[]{:S(2)}) copy-start(bf16[1,768,1280]{2,1,0:T(8,128)(2,1)} %param.5) | copy-start | bytes 5898244
  3.2 2.4 %collective-permute-start.1 = (f32[512,256]{1,0:T(8,128)S(1)}, f32[512,256]{1,0:T(8,128)S(1)}, u32[]{:S(2)}, u32[]{:S(2)}) collective-permute-start(f32[512,256]{1,0:T(8,128)S(1)} %get-tuple-element.32), channel_id=1, source_target_pairs={{0,1},{1,0},{2,3},{3,2},{4,5},{5,4},{6,7},{7,6},{8,9},{9,8},{10,11... | collective-permute-start | bytes 1572872 | tf_op jit(solution)/shard_map/ppermute | solution.py:16
  4.4 5.1 %collective-permute-start = (f32[512,256]{1,0:T(8,128)S(1)}, f32[512,256]{1,0:T(8,128)S(1)}, u32[]{:S(2)}, u32[]{:S(2)}) collective-permute-start(f32[512,256]{1,0:T(8,128)S(1)} %get-tuple-element.30), channel_id=1, source_target_pairs={{0,1},{1,0},{2,3},{3,2},{4,5},{5,4},{6,7},{7,6},{8,9},{9,8},{10,11... | collective-permute-start | bytes 1572872 | tf_op jit(solution)/shard_map/ppermute | solution.py:16
  5.1 7.7 %collective-permute-start.3 = (f32[512,128]{1,0:T(8,128)S(1)}, f32[512,128]{1,0:T(8,128)S(1)}, u32[]{:S(2)}, u32[]{:S(2)}) collective-permute-start(f32[512,128]{1,0:T(8,128)S(1)} %get-tuple-element.38), channel_id=1, source_target_pairs={{0,1},{1,0},{2,3},{3,2},{4,5},{5,4},{6,7},{7,6},{8,9},{9,8},{10,11... | collective-permute-start | bytes 786440 | tf_op jit(solution)/shard_map/ppermute | solution.py:16
  5.7 19.2 %collective-permute-start.8 = (f32[128,256]{1,0:T(8,128)S(1)}, f32[128,256]{1,0:T(8,128)S(1)}, u32[]{:S(2)}, u32[]{:S(2)}) collective-permute-start(f32[128,256]{1,0:T(8,128)S(1)} %get-tuple-element.58), channel_id=1, source_target_pairs={{0,8},{4,12},{8,0},{12,4},{1,9},{5,13},{9,1},{13,5},{2,10},{6,14},... | collective-permute-start | bytes 393224 | tf_op jit(solution)/shard_map/ppermute | solution.py:16
  9.5 11.3 %collective-permute-start.2 = (f32[4,64,256]{2,1,0:T(8,128)S(1)}, f32[4,64,256]{2,1,0:T(8,128)S(1)}, u32[]{:S(2)}, u32[]{:S(2)}) collective-permute-start(f32[4,64,256]{2,1,0:T(8,128)S(1)} %dynamic-slice_bitcast_fusion), channel_id=1, source_target_pairs={{0,2},{1,3},{2,0},{3,1},{4,6},{5,7},{6,4},{7,5},{8,10},{9,11},{10,... | collective-permute-start | bytes 786440 | tf_op jit(solution)/shard_map/ppermute | solution.py:16
  11.1 13.8 %collective-permute-start.9 = (f32[128,256]{1,0:T(8,128)S(1)}, f32[128,256]{1,0:T(8,128)S(1)}, u32[]{:S(2)}, u32[]{:S(2)}) collective-permute-start(f32[128,256]{1,0:T(8,128)S(1)} %get-tuple-element.57), channel_id=1, source_target_pairs={{0,12},{4,8},{8,4},{12,0},{1,13},{5,9},{9,5},{13,1},{2,14},{6,10},... | collective-permute-start | bytes 393224 | tf_op jit(solution)/shard_map/ppermute | solution.py:16
  12.8 12.2 %collective-permute-start.10 = (f32[128,256]{1,0:T(8,128)S(1)}, f32[128,256]{1,0:T(8,128)S(1)}, u32[]{:S(2)}, u32[]{:S(2)}) collective-permute-start(f32[128,256]{1,0:T(8,128)S(1)} %get-tuple-element.56), channel_id=1, source_target_pairs={{0,4},{4,0},{8,12},{12,8},{1,5},{5,1},{9,13},{13,9},{2,6},{6,2},{1... | collective-permute-start | bytes 393224 | tf_op jit(solution)/shard_map/ppermute | solution.py:16
  12.8 8.0 %collective-permute-start.4 = (f32[4,64,128]{2,1,0:T(8,128)S(1)}, f32[4,64,128]{2,1,0:T(8,128)S(1)}, u32[]{:S(2)}, u32[]{:S(2)}) collective-permute-start(f32[4,64,128]{2,1,0:T(8,128)S(1)} %dynamic-slice_bitcast_fusion.1), channel_id=1, source_target_pairs={{0,2},{1,3},{2,0},{3,1},{4,6},{5,7},{6,4},{7,5},{8,10},{9,11},{10,... | collective-permute-start | bytes 393224 | tf_op jit(solution)/shard_map/ppermute | solution.py:16
  20.9 10.3 %collective-permute-start.5 = (f32[64,384]{1,0:T(8,128)S(1)}, f32[64,384]{1,0:T(8,128)S(1)}, u32[]{:S(2)}, u32[]{:S(2)}) collective-permute-start(f32[64,384]{1,0:T(8,128)S(1)} %get-tuple-element.59), channel_id=1, source_target_pairs={{0,8},{4,12},{8,0},{12,4},{1,9},{5,13},{9,1},{13,5},{2,10},{6,14},... | collective-permute-start | bytes 294920 | tf_op jit(solution)/shard_map/ppermute | solution.py:16
  21.8 9.5 %collective-permute-start.6 = (f32[64,384]{1,0:T(8,128)S(1)}, f32[64,384]{1,0:T(8,128)S(1)}, u32[]{:S(2)}, u32[]{:S(2)}) collective-permute-start(f32[64,384]{1,0:T(8,128)S(1)} %get-tuple-element.60), channel_id=1, source_target_pairs={{0,12},{4,8},{8,4},{12,0},{1,13},{5,9},{9,5},{13,1},{2,14},{6,10},... | collective-permute-start | bytes 294920 | tf_op jit(solution)/shard_map/ppermute | solution.py:16
  24.9 6.5 %collective-permute-start.7 = (f32[64,384]{1,0:T(8,128)S(1)}, f32[64,384]{1,0:T(8,128)S(1)}, u32[]{:S(2)}, u32[]{:S(2)}) collective-permute-start(f32[64,384]{1,0:T(8,128)S(1)} %get-tuple-element.61), channel_id=1, source_target_pairs={{0,4},{4,0},{8,12},{12,8},{1,5},{5,1},{9,13},{13,9},{2,6},{6,2},{1... | collective-permute-start | bytes 294920 | tf_op jit(solution)/shard_map/ppermute | solution.py:16
  25.0 6.5 %collective-permute-start.11 = (f32[128,256]{1,0:T(8,128)S(1)}, f32[128,256]{1,0:T(8,128)S(1)}, u32[]{:S(2)}, u32[]{:S(2)}) collective-permute-start(f32[128,256]{1,0:T(8,128)S(1)} %fusion.2), channel_id=1, source_target_pairs={{0,2},{1,3},{2,0},{3,1},{4,6},{5,7},{6,4},{7,5},{8,10},{9,11},{10,... | collective-permute-start | bytes 393224 | tf_op jit(solution)/shard_map/ppermute | solution.py:16
  31.6 13.3 %collective-permute-start.13 = (f32[64,384]{1,0:T(8,128)S(1)}, f32[64,384]{1,0:T(8,128)S(1)}, u32[]{:S(2)}, u32[]{:S(2)}) collective-permute-start(f32[64,384]{1,0:T(8,128)S(1)} %get-tuple-element.51.early), channel_id=1, source_target_pairs={{0,2},{1,3},{2,0},{3,1},{4,6},{5,7},{6,4},{7,5},{8,10},{9,11},{10,... | collective-permute-start | bytes 294920 | tf_op jit(solution)/shard_map/ppermute | solution.py:16
  33.2 11.7 %collective-permute-start.14 = (f32[64,384]{1,0:T(8,128)S(1)}, f32[64,384]{1,0:T(8,128)S(1)}, u32[]{:S(2)}, u32[]{:S(2)}) collective-permute-start(f32[64,384]{1,0:T(8,128)S(1)} %get-tuple-element.51.early), channel_id=1, source_target_pairs={{0,3},{1,2},{2,1},{3,0},{4,7},{5,6},{6,5},{7,4},{8,11},{9,10},{10,... | collective-permute-start | bytes 294920 | tf_op jit(solution)/shard_map/ppermute | solution.py:16
  33.2 11.7 %collective-permute-start.12 = (f32[64,896]{1,0:T(8,128)S(1)}, f32[64,896]{1,0:T(8,128)S(1)}, u32[]{:S(2)}, u32[]{:S(2)}) collective-permute-start(f32[64,896]{1,0:T(8,128)S(1)} %pad_maximum_fusion), channel_id=1, source_target_pairs={{0,1},{1,0},{2,3},{3,2},{4,5},{5,4},{6,7},{7,6},{8,9},{9,8},{10,11... | collective-permute-start | bytes 688136 | tf_op jit(solution)/shard_map/ppermute | solution.py:16

commit v9 on v8

--- a/solution.py
+++ b/solution.py
@@ -191,7 +191,7 @@
     own_rows = hidden // n_loop
     half = block // CORES
     tile = half // 5 // 128 * 128
-    widths = (2 * tile, 2 * tile, half - 4 * tile)
+    widths = (tile, 2 * tile, half - 3 * tile)
 
     live = lax.broadcasted_iota(jnp.int32, (rows, 1), 0) < counts[0, 0]
     entries = lax.axis_size("mod") * hidden * block
@@ -202,15 +202,14 @@
     side, middle, last = widths
     late_other, masked = first_term(counts, place, tokens, upstream, side, middle)
     late_other = swap(late_other, "line", 1)
-    first_other, late = terms(
-        place, masked, upstream, (False, 0, side), (True, side, middle)
+    first_other, first_sum, late = terms(
+        place, masked, upstream, (False, 0, side), (True, 0, side), (True, side, middle)
     )
     first_other = swap(first_other, "line", 1)
-    first_sum, second_other, second_sum = terms(
+    second_other, second_sum = terms(
         place,
         masked,
         upstream,
-        (True, 0, side),
         (False, side + middle, last),
         (True, side + middle, last),
     )

time: 46.2 us -> 46.1 us (level)
  blocking collectives: 11.1 us -> 10.6 us
where the time goes in v9:
time: 46.1 us; the launch traced here: 45.9 us
  starting transfers between devices  16.5 us (36%)
  blocking collectives  10.6 us (23%)
  waiting for transfers between devices  10.4 us (23%)
  Pallas kernels  4.11 us (9%)
  matrix products  2.09 us (5%)
  between operations  1.57 us (3%)
    ppermute x15, starting transfers between devices, swap(): return lax.ppermute(x, axis, [(i, i ^ distance) for i in range(size)])  16.5 us
    all_to_all x1, blocking collectives, on_device(): lax.all_to_all(jnp.broadcast_to(total[None], (members, 1, 128)), everyone...  10.6 us
    ppermute x15, waiting for transfers between devices, swap(): return lax.ppermute(x, axis, [(i, i ^ distance) for i in range(size)])  10.4 us
    dot_general x1, matrix products, on_device(): lax.dot_general(after(upstream, *sends.values()), weight, (((1,), (1,)),...  2.09 us
    pallas_call x1, Pallas kernels, first_term(): pl.pallas_call(functools.partial(first_kernel, start), out_shape=(jax.Sha...  1.73 us
    pallas_call x2, Pallas kernels, terms(): pl.pallas_call(functools.partial(terms_kernel, [span[:2] for span in span...  1.26 us
    pallas_call x1, Pallas kernels, scaled(): pl.pallas_call(functools.partial(scaled_kernel, entries, side), out_shape...  1.12 us
  transfers between devices with their start and end apart: 15, of which 3 were waited for; matrix products, arithmetic and copies ran while one was open for 6% of the time, Pallas kernels for 3%

profile of v9, /device:TPU:0, one launch (start us, length us, event | category | flops | bytes accessed | tf_op | source)
XLA Modules:
  0.0 45.9 jit_solution(11623571346054094697)
XLA Ops:
  0.6 0.0 copy-start
  0.6 0.0 copy-start.1
  1.5 1.7 %shard_map.59 = (f32[512,256]{1,0:T(8,128)S(1)}, bf16[768,512]{1,0:T(8,128)(2,1)S(1)}) custom-call(s32[1,1,1]{2,1,0:T(1,128)} %copy.6.count, s32[1]{0:T(128)} %bitcast.place, bf16[768,512]{1,0:T(8,128)(2,1)} %bitcast.68, bf16[768,1280]{1,0:T(8,128)(2,1)} %bitcast.57), custom_call_target="tpu_custom_call" | custom-call | tf_op jit(solution)/shard_map/pallas_call | solution.py:80
  3.2 0.5 %collective-permute-start.1 = (f32[512,256]{1,0:T(8,128)S(1)}, f32[512,256]{1,0:T(8,128)S(1)}, u32[]{:S(2)}, u32[]{:S(2)}) collective-permute-start(f32[512,256]{1,0:T(8,128)S(1)} %get-tuple-element.32), channel_id=1, source_target_pairs={{0,1},{1,0},{2,3},{3,2},{4,5},{5,4},{6,7},{7,6},{8,9},{9,8},{10,11... | collective-permute-start | bytes 1572872 | tf_op jit(solution)/shard_map/ppermute | solution.py:16
  3.7 0.0 copy-done.1
  3.7 0.6 %shard_map.61 = (f32[512,256]{1,0:T(8,128)S(1)}, f32[512,256]{1,0:T(8,128)S(1)}) custom-call(s32[1]{0:T(128)} %bitcast.place, bf16[768,512]{1,0:T(8,128)(2,1)S(1)} %get-tuple-element.28.masked, bf16[768,1280]{1,0:T(8,128)(2,1)S(1)} %bitcast.58), custom_call_target="tpu_custom_call" | custom-call | tf_op jit(solution)/shard_map/pallas_call | solution.py:123
  4.4 0.1 collective-permute-start.3
  4.5 0.6 %shard_map.60 = (f32[512,128]{1,0:T(8,128)S(1)}, f32[512,128]{1,0:T(8,128)S(1)}, f32[512,256]{1,0:T(8,128)S(1)}) custom-call(s32[1]{0:T(128)} %bitcast.place, bf16[768,512]{1,0:T(8,128)(2,1)S(1)} %get-tuple-element.28.masked, bf16[768,1280]{1,0:T(8,128)(2,1)S(1)} %bitcast.59), custom_call_target="tpu_custom_call" | custom-call | tf_op jit(solution)/shard_map/pallas_call | solution.py:123
  5.1 0.5 %collective-permute-start = (f32[512,128]{1,0:T(8,128)S(1)}, f32[512,128]{1,0:T(8,128)S(1)}, u32[]{:S(2)}, u32[]{:S(2)}) collective-permute-start(f32[512,128]{1,0:T(8,128)S(1)} %get-tuple-element.30), channel_id=1, source_target_pairs={{0,1},{1,0},{2,3},{3,2},{4,5},{5,4},{6,7},{7,6},{8,9},{9,8},{10,11... | collective-permute-start | bytes 786440 | tf_op jit(solution)/shard_map/ppermute | solution.py:16
  5.6 0.0 collective-permute-done.1
  5.6 0.1 add.49
  5.8 3.7 %collective-permute-start.8 = (f32[128,256]{1,0:T(8,128)S(1)}, f32[128,256]{1,0:T(8,128)S(1)}, u32[]{:S(2)}, u32[]{:S(2)}) collective-permute-start(f32[128,256]{1,0:T(8,128)S(1)} %get-tuple-element.58), channel_id=1, source_target_pairs={{0,8},{4,12},{8,0},{12,4},{1,9},{5,13},{9,1},{13,5},{2,10},{6,14},... | collective-permute-start | bytes 393224 | tf_op jit(solution)/shard_map/ppermute | solution.py:16
  9.4 0.0 collective-permute-done
  9.5 1.6 %collective-permute-start.2 = (f32[4,64,128]{2,1,0:T(8,128)S(1)}, f32[4,64,128]{2,1,0:T(8,128)S(1)}, u32[]{:S(2)}, u32[]{:S(2)}) collective-permute-start(f32[4,64,128]{2,1,0:T(8,128)S(1)} %dynamic-slice_bitcast_fusion.3), channel_id=1, source_target_pairs={{0,2},{1,3},{2,0},{3,1},{4,6},{5,7},{6,4},{7,5},{8,10},{9,11},{10,... | collective-permute-start | bytes 393224 | tf_op jit(solution)/shard_map/ppermute | solution.py:16
  11.1 2.3 %collective-permute-start.9 = (f32[128,256]{1,0:T(8,128)S(1)}, f32[128,256]{1,0:T(8,128)S(1)}, u32[]{:S(2)}, u32[]{:S(2)}) collective-permute-start(f32[128,256]{1,0:T(8,128)S(1)} %get-tuple-element.57), channel_id=1, source_target_pairs={{0,12},{4,8},{8,4},{12,0},{1,13},{5,9},{9,5},{13,1},{2,14},{6,10},... | collective-permute-start | bytes 393224 | tf_op jit(solution)/shard_map/ppermute | solution.py:16
  13.4 0.0 collective-permute-start.10
  13.4 0.0 collective-permute-done.3
  13.4 0.1 add.51
  13.5 0.6 %collective-permute-start.4 = (f32[4,64,256]{2,1,0:T(8,128)S(1)}, f32[4,64,256]{2,1,0:T(8,128)S(1)}, u32[]{:S(2)}, u32[]{:S(2)}) collective-permute-start(f32[4,64,256]{2,1,0:T(8,128)S(1)} %dynamic-slice_bitcast_fusion), channel_id=1, source_target_pairs={{0,2},{1,3},{2,0},{3,1},{4,6},{5,7},{6,4},{7,5},{8,10},{9,11},{10,... | collective-permute-start | bytes 786440 | tf_op jit(solution)/shard_map/ppermute | solution.py:16
  14.1 0.0 copy-done
  14.1 2.1 %select_convert_fusion = bf16[768,512]{1,0:T(8,128)(2,1)} fusion(bf16[768,1280]{1,0:T(8,128)(2,1)S(1)} %bitcast.60, bf16[1,512,1280]{2,1,0:T(8,128)(2,1)S(1)} %copy-done, pred[768]{0:T(1024)(128)(4,1)S(1)} %iota_compare_fusion), kind=kOutput, calls=%fused_computation | convolution fusion | flops 1007419392 | bytes 4064000 | tf_op jit(solution)/shard_map/dot_general | solution.py:228
  16.2 0.0 collective-permute-done.2
  16.2 5.2 %collective-permute-done.4 = f32[4,64,256]{2,1,0:T(8,128)S(1)} collective-permute-done((f32[4,64,256]{2,1,0:T(8,128)S(1)}, f32[4,64,256]{2,1,0:T(8,128)S(1)}, u32[]{:S(2)}, u32[]{:S(2)}) %collective-permute-start.4) | collective-permute-done | bytes 262176 | tf_op jit(solution)/shard_map/ppermute | solution.py:16
  21.4 1.9 %collective-permute-start.5 = (f32[64,384]{1,0:T(8,128)S(1)}, f32[64,384]{1,0:T(8,128)S(1)}, u32[]{:S(2)}, u32[]{:S(2)}) collective-permute-start(f32[64,384]{1,0:T(8,128)S(1)} %get-tuple-element.59), channel_id=1, source_target_pairs={{0,8},{4,12},{8,0},{12,4},{1,9},{5,13},{9,1},{13,5},{2,10},{6,14},... | collective-permute-start | bytes 294920 | tf_op jit(solution)/shard_map/ppermute | solution.py:16
  23.4 2.3 %collective-permute-start.6 = (f32[64,384]{1,0:T(8,128)S(1)}, f32[64,384]{1,0:T(8,128)S(1)}, u32[]{:S(2)}, u32[]{:S(2)}) collective-permute-start(f32[64,384]{1,0:T(8,128)S(1)} %get-tuple-element.60), channel_id=1, source_target_pairs={{0,12},{4,8},{8,4},{12,0},{1,13},{5,9},{9,5},{13,1},{2,14},{6,10},... | collective-permute-start | bytes 294920 | tf_op jit(solution)/shard_map/ppermute | solution.py:16
  25.6 0.0 collective-permute-done.8
  25.6 0.0 collective-permute-start.7
  25.6 0.0 collective-permute-done.9
  25.6 0.0 collective-permute-done.10
  25.7 0.8 %collective-permute-start.11 = (f32[128,256]{1,0:T(8,128)S(1)}, f32[128,256]{1,0:T(8,128)S(1)}, u32[]{:S(2)}, u32[]{:S(2)}) collective-permute-start(f32[128,256]{1,0:T(8,128)S(1)} %fusion.2), channel_id=1, source_target_pairs={{0,2},{1,3},{2,0},{3,1},{4,6},{5,7},{6,4},{7,5},{8,10},{9,11},{10,... | collective-permute-start | bytes 393224 | tf_op jit(solution)/shard_map/ppermute | solution.py:16
  26.5 4.5 %collective-permute-done.5 = f32[64,384]{1,0:T(8,128)S(1)} collective-permute-done((f32[64,384]{1,0:T(8,128)S(1)}, f32[64,384]{1,0:T(8,128)S(1)}, u32[]{:S(2)}, u32[]{:S(2)}) %collective-permute-start.5) | collective-permute-done | bytes 98336 | tf_op jit(solution)/shard_map/ppermute | solution.py:16
  31.1 0.0 collective-permute-done.6
  31.1 0.7 %collective-permute-done.7 = f32[64,384]{1,0:T(8,128)S(1)} collective-permute-done((f32[64,384]{1,0:T(8,128)S(1)}, f32[64,384]{1,0:T(8,128)S(1)}, u32[]{:S(2)}, u32[]{:S(2)}) %collective-permute-start.7) | collective-permute-done | bytes 98336 | tf_op jit(solution)/shard_map/ppermute | solution.py:16
  31.8 0.0 collective-permute-done.11
  31.9 0.9 %collective-permute-start.13 = (f32[64,384]{1,0:T(8,128)S(1)}, f32[64,384]{1,0:T(8,128)S(1)}, u32[]{:S(2)}, u32[]{:S(2)}) collective-permute-start(f32[64,384]{1,0:T(8,128)S(1)} %get-tuple-element.51.early), channel_id=1, source_target_pairs={{0,2},{1,3},{2,0},{3,1},{4,6},{5,7},{6,4},{7,5},{8,10},{9,11},{10,... | collective-permute-start | bytes 294920 | tf_op jit(solution)/shard_map/ppermute | solution.py:16
  32.7 0.0 collective-permute-start.14
  32.7 1.3 %collective-permute-start.12 = (f32[64,896]{1,0:T(8,128)S(1)}, f32[64,896]{1,0:T(8,128)S(1)}, u32[]{:S(2)}, u32[]{:S(2)}) collective-permute-start(f32[64,896]{1,0:T(8,128)S(1)} %pad_maximum_fusion), channel_id=1, source_target_pairs={{0,1},{1,0},{2,3},{3,2},{4,5},{5,4},{6,7},{7,6},{8,9},{9,8},{10,11... | collective-permute-start | bytes 688136 | tf_op jit(solution)/shard_map/ppermute | solution.py:16
  34.1 10.6 %all_to_all.5 = f32[32,1,128]{2,1,0:T(1,128)S(1)} all-to-all(f32[32,1,128]{2,1,0:T(1,128)S(1)} %broadcast_in_dim.33), channel_id=1, replica_groups=mesh['mod'=2,'loop'=4,'line'=4] {'mod','loop','line'}, dimensions={0} | all-to-all | bytes 32768 | tf_op jit(solution)/shard_map/all_to_all | solution.py:263
  44.8 0.0 collective-permute-done.13.refs_0_
  44.8 0.0 collective-permute-done.14.refs_1_
  44.8 0.0 collective-permute-done.12.parcel
  44.8 1.1 %shard_map.62 = f32[128,1280]{1,0:T(8,128)} custom-call(s32[1]{0:T(128)} %bitcast.place, f32[32,128]{1,0:T(8,128)S(1)} %bitcast.61, f32[128,256]{1,0:T(8,128)S(1)} %get-tuple-element.53.late, f32[64,384]{1,0:T(8,128)S(1)} %get-tuple-element.51.early, f32[64,896]{1,0:T(8,128)S(1)} %collective-permute-done.12.parcel, ...), custom_call_target="tpu_custom_call" | custom-call | tf_op jit(solution)/shard_map/pallas_call | solution.py:162
  (17 shorter events, 0.4 us)
Async XLA Ops:
  0.6 13.5 %copy-start = (bf16[1,512,1280]{2,1,0:T(8,128)(2,1)S(1)}, bf16[1,512,1280]{2,1,0:T(8,128)(2,1)}, u32[]{:S(2)}) copy-start(bf16[1,512,1280]{2,1,0:T(8,128)(2,1)} %param.6) | copy-start | bytes 3932164
  0.6 3.1 %copy-start.1 = (bf16[1,768,1280]{2,1,0:T(8,128)(2,1)S(1)}, bf16[1,768,1280]{2,1,0:T(8,128)(2,1)}, u32[]{:S(2)}) copy-start(bf16[1,768,1280]{2,1,0:T(8,128)(2,1)} %param.5) | copy-start | bytes 5898244
  3.2 2.4 %collective-permute-start.1 = (f32[512,256]{1,0:T(8,128)S(1)}, f32[512,256]{1,0:T(8,128)S(1)}, u32[]{:S(2)}, u32[]{:S(2)}) collective-permute-start(f32[512,256]{1,0:T(8,128)S(1)} %get-tuple-element.32), channel_id=1, source_target_pairs={{0,1},{1,0},{2,3},{3,2},{4,5},{5,4},{6,7},{7,6},{8,9},{9,8},{10,11... | collective-permute-start | bytes 1572872 | tf_op jit(solution)/shard_map/ppermute | solution.py:16
  4.4 9.1 %collective-permute-start.3 = (f32[512,256]{1,0:T(8,128)S(1)}, f32[512,256]{1,0:T(8,128)S(1)}, u32[]{:S(2)}, u32[]{:S(2)}) collective-permute-start(f32[512,256]{1,0:T(8,128)S(1)} %get-tuple-element.38), channel_id=1, source_target_pairs={{0,1},{1,0},{2,3},{3,2},{4,5},{5,4},{6,7},{7,6},{8,9},{9,8},{10,11... | collective-permute-start | bytes 1572872 | tf_op jit(solution)/shard_map/ppermute | solution.py:16
  5.1 4.3 %collective-permute-start = (f32[512,128]{1,0:T(8,128)S(1)}, f32[512,128]{1,0:T(8,128)S(1)}, u32[]{:S(2)}, u32[]{:S(2)}) collective-permute-start(f32[512,128]{1,0:T(8,128)S(1)} %get-tuple-element.30), channel_id=1, source_target_pairs={{0,1},{1,0},{2,3},{3,2},{4,5},{5,4},{6,7},{7,6},{8,9},{9,8},{10,11... | collective-permute-start | bytes 786440 | tf_op jit(solution)/shard_map/ppermute | solution.py:16
  5.8 19.9 %collective-permute-start.8 = (f32[128,256]{1,0:T(8,128)S(1)}, f32[128,256]{1,0:T(8,128)S(1)}, u32[]{:S(2)}, u32[]{:S(2)}) collective-permute-start(f32[128,256]{1,0:T(8,128)S(1)} %get-tuple-element.58), channel_id=1, source_target_pairs={{0,8},{4,12},{8,0},{12,4},{1,9},{5,13},{9,1},{13,5},{2,10},{6,14},... | collective-permute-start | bytes 393224 | tf_op jit(solution)/shard_map/ppermute | solution.py:16
  9.5 6.7 %collective-permute-start.2 = (f32[4,64,128]{2,1,0:T(8,128)S(1)}, f32[4,64,128]{2,1,0:T(8,128)S(1)}, u32[]{:S(2)}, u32[]{:S(2)}) collective-permute-start(f32[4,64,128]{2,1,0:T(8,128)S(1)} %dynamic-slice_bitcast_fusion.3), channel_id=1, source_target_pairs={{0,2},{1,3},{2,0},{3,1},{4,6},{5,7},{6,4},{7,5},{8,10},{9,11},{10,... | collective-permute-start | bytes 393224 | tf_op jit(solution)/shard_map/ppermute | solution.py:16
  11.1 14.5 %collective-permute-start.9 = (f32[128,256]{1,0:T(8,128)S(1)}, f32[128,256]{1,0:T(8,128)S(1)}, u32[]{:S(2)}, u32[]{:S(2)}) collective-permute-start(f32[128,256]{1,0:T(8,128)S(1)} %get-tuple-element.57), channel_id=1, source_target_pairs={{0,12},{4,8},{8,4},{12,0},{1,13},{5,9},{9,5},{13,1},{2,14},{6,10},... | collective-permute-start | bytes 393224 | tf_op jit(solution)/shard_map/ppermute | solution.py:16
  13.4 12.2 %collective-permute-start.10 = (f32[128,256]{1,0:T(8,128)S(1)}, f32[128,256]{1,0:T(8,128)S(1)}, u32[]{:S(2)}, u32[]{:S(2)}) collective-permute-start(f32[128,256]{1,0:T(8,128)S(1)} %get-tuple-element.56), channel_id=1, source_target_pairs={{0,4},{4,0},{8,12},{12,8},{1,5},{5,1},{9,13},{13,9},{2,6},{6,2},{1... | collective-permute-start | bytes 393224 | tf_op jit(solution)/shard_map/ppermute | solution.py:16
  13.5 7.9 %collective-permute-start.4 = (f32[4,64,256]{2,1,0:T(8,128)S(1)}, f32[4,64,256]{2,1,0:T(8,128)S(1)}, u32[]{:S(2)}, u32[]{:S(2)}) collective-permute-start(f32[4,64,256]{2,1,0:T(8,128)S(1)} %dynamic-slice_bitcast_fusion), channel_id=1, source_target_pairs={{0,2},{1,3},{2,0},{3,1},{4,6},{5,7},{6,4},{7,5},{8,10},{9,11},{10,... | collective-permute-start | bytes 786440 | tf_op jit(solution)/shard_map/ppermute | solution.py:16
  21.4 9.6 %collective-permute-start.5 = (f32[64,384]{1,0:T(8,128)S(1)}, f32[64,384]{1,0:T(8,128)S(1)}, u32[]{:S(2)}, u32[]{:S(2)}) collective-permute-start(f32[64,384]{1,0:T(8,128)S(1)} %get-tuple-element.59), channel_id=1, source_target_pairs={{0,8},{4,12},{8,0},{12,4},{1,9},{5,13},{9,1},{13,5},{2,10},{6,14},... | collective-permute-start | bytes 294920 | tf_op jit(solution)/shard_map/ppermute | solution.py:16
  23.4 7.7 %collective-permute-start.6 = (f32[64,384]{1,0:T(8,128)S(1)}, f32[64,384]{1,0:T(8,128)S(1)}, u32[]{:S(2)}, u32[]{:S(2)}) collective-permute-start(f32[64,384]{1,0:T(8,128)S(1)} %get-tuple-element.60), channel_id=1, source_target_pairs={{0,12},{4,8},{8,4},{12,0},{1,13},{5,9},{9,5},{13,1},{2,14},{6,10},... | collective-permute-start | bytes 294920 | tf_op jit(solution)/shard_map/ppermute | solution.py:16
  25.6 6.1 %collective-permute-start.7 = (f32[64,384]{1,0:T(8,128)S(1)}, f32[64,384]{1,0:T(8,128)S(1)}, u32[]{:S(2)}, u32[]{:S(2)}) collective-permute-start(f32[64,384]{1,0:T(8,128)S(1)} %get-tuple-element.61), channel_id=1, source_target_pairs={{0,4},{4,0},{8,12},{12,8},{1,5},{5,1},{9,13},{13,9},{2,6},{6,2},{1... | collective-permute-start | bytes 294920 | tf_op jit(solution)/shard_map/ppermute | solution.py:16
  25.7 6.1 %collective-permute-start.11 = (f32[128,256]{1,0:T(8,128)S(1)}, f32[128,256]{1,0:T(8,128)S(1)}, u32[]{:S(2)}, u32[]{:S(2)}) collective-permute-start(f32[128,256]{1,0:T(8,128)S(1)} %fusion.2), channel_id=1, source_target_pairs={{0,2},{1,3},{2,0},{3,1},{4,6},{5,7},{6,4},{7,5},{8,10},{9,11},{10,... | collective-permute-start | bytes 393224 | tf_op jit(solution)/shard_map/ppermute | solution.py:16
  31.9 12.9 %collective-permute-start.13 = (f32[64,384]{1,0:T(8,128)S(1)}, f32[64,384]{1,0:T(8,128)S(1)}, u32[]{:S(2)}, u32[]{:S(2)}) collective-permute-start(f32[64,384]{1,0:T(8,128)S(1)} %get-tuple-element.51.early), channel_id=1, source_target_pairs={{0,2},{1,3},{2,0},{3,1},{4,6},{5,7},{6,4},{7,5},{8,10},{9,11},{10,... | collective-permute-start | bytes 294920 | tf_op jit(solution)/shard_map/ppermute | solution.py:16
  32.7 12.0 %collective-permute-start.14 = (f32[64,384]{1,0:T(8,128)S(1)}, f32[64,384]{1,0:T(8,128)S(1)}, u32[]{:S(2)}, u32[]{:S(2)}) collective-permute-start(f32[64,384]{1,0:T(8,128)S(1)} %get-tuple-element.51.early), channel_id=1, source_target_pairs={{0,3},{1,2},{2,1},{3,0},{4,7},{5,6},{6,5},{7,4},{8,11},{9,10},{10,... | collective-permute-start | bytes 294920 | tf_op jit(solution)/shard_map/ppermute | solution.py:16
  32.7 12.0 %collective-permute-start.12 = (f32[64,896]{1,0:T(8,128)S(1)}, f32[64,896]{1,0:T(8,128)S(1)}, u32[]{:S(2)}, u32[]{:S(2)}) collective-permute-start(f32[64,896]{1,0:T(8,128)S(1)} %pad_maximum_fusion), channel_id=1, source_target_pairs={{0,1},{1,0},{2,3},{3,2},{4,5},{5,4},{6,7},{7,6},{8,9},{9,8},{10,11... | collective-permute-start | bytes 688136 | tf_op jit(solution)/shard_map/ppermute | solution.py:16
